TPU v7x, 512 devices: a whole 4x8x8 slice. The times are simulated.
512 devices in a mesh: slab: 16 (over y, core), col: 32 (over x, z).
Axes of the slice: x: 4, y: 8, z: 8, core: 2. Of those that a mesh axis runs over, the one named last changes fastest.
Arguments:
- load: float32 [3, 256, 512, 128], P(None, 'slab', 'col'), may hold values from -6 to 6
- density: int32 [256, 512, 128], P('slab', 'col'), may hold values from 0 to 7
- moduli: float32 [8], replicated, may hold values from 0.1 to 10
- fixed: int32 [256, 512, 128], P('slab', 'col'), may hold values 0 or 1
Outputs:
- solution_field: float32 [3, 256, 512, 128], P(None, 'slab', 'col')
- residual: float32 [3, 256, 512, 128], P(None, 'slab', 'col')
All inputs are finite; a program needn't handle non-finite values. No bound on the sum of `fixed` on one device may be relied on, other than what follows from the above.
Results may differ from a plain program's by a relative error of at most 0.0001.
Values sent between devices are 32-bit elements; how exact they have to be, the bound alone decides.
No kernel may reach another device: no remote copies, remote signals or barrier semaphores. Data moves between devices by JAX's collectives and lax.ppermute only.
A program may use at most 128 MiB of HBM per device.

v0:
```python
import jax
import jax.numpy as jnp
from jax import lax
from jax.sharding import PartitionSpec as P

LEVELS = 3
PRE = 2
POST = 2
COARSE_SWEEPS = 8
CLASSES = 8


OMEGA = 0.6
COUPLE = 0.05


def padded_2(block, sides, width):
    for axis, dim in sides:
        count = lax.axis_size(axis)
        forward = [(i, i + 1) for i in range(count - 1)]
        backward = [(target, source) for source, target in forward]
        low = lax.ppermute(
            lax.slice_in_dim(block, block.shape[dim] - width, None, axis=dim), axis, forward
        )
        high = lax.ppermute(lax.slice_in_dim(block, 0, width, axis=dim), axis, backward)
        block = jnp.concatenate([low, block, high], axis=dim)
    return block


def shrink(arr):
    lead = arr.shape[:-3]
    za, yb, xc = arr.shape[-3:]
    blocks = arr.reshape(tuple(lead) + (za // 2, 2, yb // 2, 2, xc // 2, 2))
    return blocks.mean(axis=(-5, -3, -1))


def grow(arr):
    return jnp.repeat(jnp.repeat(jnp.repeat(arr, 2, axis=-3), 2, axis=-2), 2, axis=-1)


def beside_all(padded):
    return [
        padded[..., 2:, 1:-1, 1:-1],
        padded[..., :-2, 1:-1, 1:-1],
        padded[..., 1:-1, 2:, 1:-1],
        padded[..., 1:-1, :-2, 1:-1],
        padded[..., 1:-1, 1:-1, 2:],
        padded[..., 1:-1, 1:-1, :-2],
    ]


def diagonal_of(stiff_pad, scale):
    centre = stiff_pad[1:-1, 1:-1, 1:-1]
    total = jnp.zeros_like(centre)
    for near in beside_all(stiff_pad):
        total = total + 0.5 * (centre + near)
    return scale * total + 2.0 * COUPLE * centre


def apply_op(field_pad, stiff_pad, scale):
    centre = stiff_pad[1:-1, 1:-1, 1:-1]
    field = field_pad[:, 1:-1, 1:-1, 1:-1]
    total = jnp.zeros_like(field)
    for near_k, near_u in zip(beside_all(stiff_pad), beside_all(field_pad)):
        total = total + 0.5 * (centre + near_k) * (field - near_u)
    return scale * total + COUPLE * centre * (field + jnp.sum(field, axis=0, keepdims=True))


def pad_xdim(padded):
    return jnp.pad(padded, ((0, 0), (0, 0), (0, 0), (1, 1)))


def field_extended(field):
    return pad_xdim(padded_2(field, (("slab", 1), ("col", 2)), 1))


def coarse_extended(field):
    return pad_xdim(padded_2(field, (("slab", 1), ("col", 2)), 1))


def sweeps(field, rhs, stiff_pad, diag, scale, weight, count, extend):
    if field is None:
        field = OMEGA * weight * rhs / diag
        count = count - 1
    for turn in range(count):
        field = field + OMEGA * weight * (rhs - apply_op(extend(field), stiff_pad, scale)) / diag
    return field


def on_device(load, density, moduli, fixed):
    stiff = jnp.zeros(density.shape, jnp.float32)
    for klass in range(CLASSES):
        stiff = stiff + jnp.where(density == klass, moduli[klass], jnp.float32(0.0))
    mask = 1.0 - fixed.astype(jnp.float32)
    pads = []
    current = stiff
    for level in range(LEVELS + 1):
        rimmed = padded_2(current, (("slab", 0), ("col", 1)), 1)
        pads.append(jnp.pad(rimmed, ((0, 0), (0, 0), (1, 1))))
        if level < LEVELS:
            current = shrink(current)
    diags = [diagonal_of(pads[level], 0.25**level) for level in range(LEVELS + 1)]
    saved = []
    rhs = load
    for level in range(LEVELS):
        weight = mask if level == 0 else 1.0
        scale = 0.25**level
        field = sweeps(None, rhs, pads[level], diags[level], scale, weight, PRE, field_extended)
        resid = weight * (rhs - apply_op(field_extended(field), pads[level], scale))
        saved.append((field, rhs))
        rhs = shrink(resid)
    coarse_scale = 0.25**LEVELS
    field = sweeps(
        None, rhs, pads[LEVELS], diags[LEVELS], coarse_scale, 1.0, COARSE_SWEEPS, coarse_extended
    )
    for level in range(LEVELS - 1, -1, -1):
        weight = mask if level == 0 else 1.0
        fine, rhs = saved[level]
        field = fine + weight * grow(field)
        field = sweeps(
            field, rhs, pads[level], diags[level], 0.25**level, weight, POST, field_extended
        )
    residual = mask * (load - apply_op(field_extended(field), pads[0], 1.0))
    return (field, residual)


def solution(mesh):
    placed = (P(None, "slab", "col", None), P("slab", "col", None), P(), P("slab", "col", None))
    return jax.shard_map(
        on_device,
        mesh=mesh,
        in_specs=placed,
        out_specs=(P(None, "slab", "col", None), P(None, "slab", "col", None)),
        check_vma=False,
    )
```

profile of v0, /device:TPU:38, one launch (start us, length us, event | category | flops | bytes accessed | tf_op | source)
XLA Modules:
  0.0 501.9 jit_solution(4641607528996507221)
XLA Ops:
  2.3 6.1 %convert_subtract_fusion = (f32[16,16,128]{2,1,0:T(8,128)S(1)}, f32[16,16,128]{2,1,0:T(8,128)S(1)}, f32[16,16,128]{2,1,0:T(8,128)S(1)}, f32[16,16,128]{2,1,0:T(8,128)S(1)}) fusion(s32[16,16,128]{2,1,0:T(8,128)} %param.7, f32[]{:T(128)} %bitcast.7, s32[16,16,128]{2,1,0:T(8,128)} %param.5, f32[]{:T(128)} %bitcast.6, f32[]{:T(128)} %bitcast.5, f32[]{:T(128)} %bitcast.4, ...), kind=kLoop, calls=%fused_computation.219 | loop fusion | flops 884736 | bytes 786464 | tf_op jit(solution)/shard_map/sub | solution.py:94
  12.7 9.8 %reshape.112 = f32[8,2,8,2,64,2]{5,4,3,2,1,0:T(8,128)} reshape(f32[16,16,128]{2,1,0:T(8,128)S(1)} %get-tuple-element.192) | data formatting | bytes 262144 | tf_op jit(solution)/shard_map/reshape | solution.py:33
  22.5 4.0 reduce_sum.237
  26.6 4.4 collective-permute-start.12
  34.2 4.9 collective-permute-start.24
  39.3 11.2 %collective-permute-start.2 = (f32[18,1,128]{2,1,0:T(1,128)S(1)}, f32[18,1,128]{2,1,0:T(1,128)S(1)}, u32[]{:S(2)}, u32[]{:S(2)}) collective-permute-start(f32[18,1,128]{2,1,0:T(1,128)S(1)} %get-tuple-element.95), channel_id=1, source_target_pairs={{1,0},{2,1},{3,2},{4,3},{5,4},{6,5},{7,6},{8,7},{9,8},{10,9},{11,1... | collective-permute-start | bytes 27656 | tf_op jit(solution)/shard_map/ppermute | solution.py:25
  54.4 3.8 collective-permute-done.3
  63.1 4.7 collective-permute-start.14
  67.9 4.4 collective-permute-start.6
  76.2 3.9 collective-permute-done.7
  85.9 3.8 collective-permute-done.9
  95.7 5.3 %collective-permute-done.11 = f32[3,18,1,128]{3,2,1,0:T(1,128)S(1)} collective-permute-done((f32[3,18,1,128]{3,2,1,0:T(1,128)S(1)}, f32[3,18,1,128]{3,2,1,0:T(1,128)S(1)}, u32[]{:S(2)}, u32[]{:S(2)}) %collective-permute-start.11) | collective-permute-done | bytes 27680 | tf_op jit(solution)/shard_map/ppermute | solution.py:22
  102.3 26.5 %reshape.111 = f32[3,8,2,8,2,64,2]{6,5,4,3,2,1,0:T(8,128)} reshape(f32[3,16,16,128]{3,2,1,0:T(8,128)S(1)} %fusion.64) | data formatting | bytes 786432 | tf_op jit(solution)/shard_map/reshape | solution.py:33
  128.9 9.4 %reduce_sum.236 = f32[3,8,8,64]{3,2,1,0:T(8,128)S(1)} reduce(f32[3,8,2,8,2,64,2]{6,5,4,3,2,1,0:T(8,128)} %reshape.111, f32[]{:T(128)} %constant.24.clone.1), dimensions={2,4,6}, to_apply=%region_2.3 | reduce | flops 86016 | bytes 442372 | tf_op jit(solution)/shard_map/reduce_sum | solution.py:34
  143.3 4.4 collective-permute-start.36
  151.6 3.9 collective-permute-start.19
  155.5 4.0 collective-permute-start.26
  161.9 4.3 collective-permute-start.20
  168.3 4.2 collective-permute-done.21
  172.5 5.8 %collective-permute-start.22 = (f32[3,10,1,64]{3,2,1,0:T(1,128)S(1)}, f32[3,10,1,64]{3,2,1,0:T(1,128)S(1)}, u32[]{:S(2)}, u32[]{:S(2)}) collective-permute-start(f32[3,10,1,64]{3,2,1,0:T(1,128)S(1)} %get-tuple-element.107), channel_id=1, source_target_pairs={{1,0},{2,1},{3,2},{4,3},{5,4},{6,5},{7,6},{8,7},{9,8},{10,9},{11,1... | collective-permute-start | bytes 23048 | tf_op jit(solution)/shard_map/ppermute | solution.py:25
  181.1 4.9 collective-permute-done.23
  187.1 4.1 reshape.113
  202.9 3.9 collective-permute-start.31
  206.8 4.0 collective-permute-start.38
  222.0 6.0 %collective-permute-start.34 = (f32[3,6,1,32]{3,2,1,0:T(1,128)S(1)}, f32[3,6,1,32]{3,2,1,0:T(1,128)S(1)}, u32[]{:S(2)}, u32[]{:S(2)}) collective-permute-start(f32[3,6,1,32]{3,2,1,0:T(1,128)S(1)} %get-tuple-element.127), channel_id=1, source_target_pairs={{1,0},{2,1},{3,2},{4,3},{5,4},{6,5},{7,6},{8,7},{9,8},{10,9},{11,1... | collective-permute-start | bytes 6920 | tf_op jit(solution)/shard_map/ppermute | solution.py:25
  230.9 4.9 collective-permute-done.35
  241.6 3.7 collective-permute-done.41
  247.2 3.9 collective-permute-start.43
  251.2 3.7 collective-permute-done.43
  259.4 3.7 collective-permute-done.45
  265.1 3.9 collective-permute-start.47
  269.0 3.7 collective-permute-done.47
  277.3 3.7 collective-permute-done.49
  283.0 3.9 collective-permute-start.51
  295.2 3.7 collective-permute-done.53
  300.8 3.9 collective-permute-start.55
  313.1 3.7 collective-permute-done.57
  318.7 3.9 collective-permute-start.59
  322.7 3.7 collective-permute-done.59
  330.9 3.7 collective-permute-done.61
  336.6 3.9 collective-permute-start.63
  348.8 3.7 collective-permute-done.65
  354.5 3.9 collective-permute-start.67
  367.1 3.7 collective-permute-done.69
  372.8 3.9 collective-permute-start.71
  376.7 3.7 collective-permute-done.71
  385.1 3.7 collective-permute-done.73
  390.8 3.9 collective-permute-start.75
  394.8 3.7 collective-permute-done.75
  404.0 3.8 collective-permute-done.77
  409.8 3.9 collective-permute-start.79
  413.7 3.8 collective-permute-done.79
  422.3 3.8 collective-permute-done.81
  428.1 3.9 collective-permute-start.83
  432.0 3.8 collective-permute-done.83
  447.4 3.9 collective-permute-done.85
  453.3 4.1 collective-permute-start.87
  457.5 3.7 collective-permute-done.87
  466.8 3.9 collective-permute-done.89
  472.7 3.9 collective-permute-start.91
  476.7 3.9 collective-permute-done.91
  486.3 3.9 collective-permute-done.93
  492.2 3.9 collective-permute-start.95
  496.1 3.9 collective-permute-done.95
  (378 shorter events, 196.4 us)
Async XLA Ops:
  8.4 30.8 %collective-permute-start = (f32[1,16,128]{2,1,0:T(8,128)S(1)}, f32[1,16,128]{2,1,0:T(8,128)S(1)}, u32[]{:S(2)}, u32[]{:S(2)}) collective-permute-start(f32[1,16,128]{2,1,0:T(8,128)S(1)} %get-tuple-element.101), channel_id=1, source_target_pairs={{32,0},{64,32},{96,64},{128,96},{160,128},{192,160},{224,192},{256... | collective-permute-start | bytes 24584 | tf_op jit(solution)/shard_map/ppermute | solution.py:25
  10.3 28.9 %collective-permute-start.1 = (f32[1,16,128]{2,1,0:T(8,128)S(1)}, f32[1,16,128]{2,1,0:T(8,128)S(1)}, u32[]{:S(2)}, u32[]{:S(2)}) collective-permute-start(f32[1,16,128]{2,1,0:T(8,128)S(1)} %get-tuple-element.100), channel_id=1, source_target_pairs={{0,32},{32,64},{64,96},{96,128},{128,160},{160,192},{192,224},{224... | collective-permute-start | bytes 24584 | tf_op jit(solution)/shard_map/ppermute | solution.py:22
  26.6 34.1 %collective-permute-start.12 = (f32[1,8,64]{2,1,0:T(8,128)S(1)}, f32[1,8,64]{2,1,0:T(8,128)S(1)}, u32[]{:S(2)}, u32[]{:S(2)}) collective-permute-start(f32[1,8,64]{2,1,0:T(8,128)S(1)} %get-tuple-element.134), channel_id=1, source_target_pairs={{32,0},{64,32},{96,64},{128,96},{160,128},{192,160},{224,192},{256... | collective-permute-start | bytes 6152 | tf_op jit(solution)/shard_map/ppermute | solution.py:25
  31.0 32.1 %collective-permute-start.13 = (f32[1,8,64]{2,1,0:T(8,128)S(1)}, f32[1,8,64]{2,1,0:T(8,128)S(1)}, u32[]{:S(2)}, u32[]{:S(2)}) collective-permute-start(f32[1,8,64]{2,1,0:T(8,128)S(1)} %get-tuple-element.133), channel_id=1, source_target_pairs={{0,32},{32,64},{64,96},{96,128},{128,160},{160,192},{192,224},{224... | collective-permute-start | bytes 6152 | tf_op jit(solution)/shard_map/ppermute | solution.py:22
  34.2 117.4 %collective-permute-start.24 = (f32[1,4,32]{2,1,0:T(4,128)S(1)}, f32[1,4,32]{2,1,0:T(4,128)S(1)}, u32[]{:S(2)}, u32[]{:S(2)}) collective-permute-start(f32[1,4,32]{2,1,0:T(4,128)S(1)} %get-tuple-element.163), channel_id=1, source_target_pairs={{32,0},{64,32},{96,64},{128,96},{160,128},{192,160},{224,192},{256... | collective-permute-start | bytes 1544 | tf_op jit(solution)/shard_map/ppermute | solution.py:25
  39.3 13.2 %collective-permute-start.2 = (f32[18,1,128]{2,1,0:T(1,128)S(1)}, f32[18,1,128]{2,1,0:T(1,128)S(1)}, u32[]{:S(2)}, u32[]{:S(2)}) collective-permute-start(f32[18,1,128]{2,1,0:T(1,128)S(1)} %get-tuple-element.95), channel_id=1, source_target_pairs={{1,0},{2,1},{3,2},{4,3},{5,4},{6,5},{7,6},{8,7},{9,8},{10,9},{11,1... | collective-permute-start | bytes 27656 | tf_op jit(solution)/shard_map/ppermute | solution.py:25
  50.5 7.7 %collective-permute-start.3 = (f32[18,1,128]{2,1,0:T(1,128)S(1)}, f32[18,1,128]{2,1,0:T(1,128)S(1)}, u32[]{:S(2)}, u32[]{:S(2)}) collective-permute-start(f32[18,1,128]{2,1,0:T(1,128)S(1)} %get-tuple-element.94), channel_id=1, source_target_pairs={{0,1},{1,2},{2,3},{3,4},{4,5},{5,6},{6,7},{7,8},{8,9},{9,10},{10,1... | collective-permute-start | bytes 27656 | tf_op jit(solution)/shard_map/ppermute | solution.py:22
  52.5 103.1 %collective-permute-start.25 = (f32[1,4,32]{2,1,0:T(4,128)S(1)}, f32[1,4,32]{2,1,0:T(4,128)S(1)}, u32[]{:S(2)}, u32[]{:S(2)}) collective-permute-start(f32[1,4,32]{2,1,0:T(4,128)S(1)} %get-tuple-element.162), channel_id=1, source_target_pairs={{0,32},{32,64},{64,96},{96,128},{128,160},{160,192},{192,224},{224... | collective-permute-start | bytes 1544 | tf_op jit(solution)/shard_map/ppermute | solution.py:22
  58.7 9.1 %collective-permute-start.4 = (f32[3,1,16,128]{3,2,1,0:T(8,128)S(1)}, f32[3,1,16,128]{3,2,1,0:T(8,128)S(1)}, u32[]{:S(2)}, u32[]{:S(2)}) collective-permute-start(f32[3,1,16,128]{3,2,1,0:T(8,128)S(1)} %get-tuple-element.91), channel_id=1, source_target_pairs={{32,0},{64,32},{96,64},{128,96},{160,128},{192,160},{224,192},{256... | collective-permute-start | bytes 73736 | tf_op jit(solution)/shard_map/ppermute | solution.py:25
  60.7 7.2 %collective-permute-start.5 = (f32[3,1,16,128]{3,2,1,0:T(8,128)S(1)}, f32[3,1,16,128]{3,2,1,0:T(8,128)S(1)}, u32[]{:S(2)}, u32[]{:S(2)}) collective-permute-start(f32[3,1,16,128]{3,2,1,0:T(8,128)S(1)} %get-tuple-element.90), channel_id=1, source_target_pairs={{0,32},{32,64},{64,96},{96,128},{128,160},{160,192},{192,224},{224... | collective-permute-start | bytes 73736 | tf_op jit(solution)/shard_map/ppermute | solution.py:22
  63.1 20.2 %collective-permute-start.14 = (f32[10,1,64]{2,1,0:T(1,128)S(1)}, f32[10,1,64]{2,1,0:T(1,128)S(1)}, u32[]{:S(2)}, u32[]{:S(2)}) collective-permute-start(f32[10,1,64]{2,1,0:T(1,128)S(1)} %get-tuple-element.121), channel_id=1, source_target_pairs={{1,0},{2,1},{3,2},{4,3},{5,4},{6,5},{7,6},{8,7},{9,8},{10,9},{11,1... | collective-permute-start | bytes 7688 | tf_op jit(solution)/shard_map/ppermute | solution.py:25
  67.9 6.4 %collective-permute-start.6 = (f32[3,18,1,128]{3,2,1,0:T(1,128)S(1)}, f32[3,18,1,128]{3,2,1,0:T(1,128)S(1)}, u32[]{:S(2)}, u32[]{:S(2)}) collective-permute-start(f32[3,18,1,128]{3,2,1,0:T(1,128)S(1)} %get-tuple-element.81), channel_id=1, source_target_pairs={{1,0},{2,1},{3,2},{4,3},{5,4},{6,5},{7,6},{8,7},{9,8},{10,9},{11,1... | collective-permute-start | bytes 82952 | tf_op jit(solution)/shard_map/ppermute | solution.py:25
  72.3 7.9 %collective-permute-start.7 = (f32[3,18,1,128]{3,2,1,0:T(1,128)S(1)}, f32[3,18,1,128]{3,2,1,0:T(1,128)S(1)}, u32[]{:S(2)}, u32[]{:S(2)}) collective-permute-start(f32[3,18,1,128]{3,2,1,0:T(1,128)S(1)} %get-tuple-element.80), channel_id=1, source_target_pairs={{0,1},{1,2},{2,3},{3,4},{4,5},{5,6},{6,7},{7,8},{8,9},{9,10},{10,1... | collective-permute-start | bytes 82952 | tf_op jit(solution)/shard_map/ppermute | solution.py:22
  74.3 11.4 %collective-permute-start.15 = (f32[10,1,64]{2,1,0:T(1,128)S(1)}, f32[10,1,64]{2,1,0:T(1,128)S(1)}, u32[]{:S(2)}, u32[]{:S(2)}) collective-permute-start(f32[10,1,64]{2,1,0:T(1,128)S(1)} %get-tuple-element.120), channel_id=1, source_target_pairs={{0,1},{1,2},{2,3},{3,4},{4,5},{5,6},{6,7},{7,8},{8,9},{9,10},{10,1... | collective-permute-start | bytes 7688 | tf_op jit(solution)/shard_map/ppermute | solution.py:22
  83.3 6.4 %collective-permute-start.9 = (f32[3,1,16,128]{3,2,1,0:T(8,128)S(1)}, f32[3,1,16,128]{3,2,1,0:T(8,128)S(1)}, u32[]{:S(2)}, u32[]{:S(2)}) collective-permute-start(f32[3,1,16,128]{3,2,1,0:T(8,128)S(1)} %get-tuple-element.88), channel_id=1, source_target_pairs={{0,32},{32,64},{64,96},{96,128},{128,160},{160,192},{192,224},{224... | collective-permute-start | bytes 73736 | tf_op jit(solution)/shard_map/ppermute | solution.py:22
  93.2 7.9 %collective-permute-start.11 = (f32[3,18,1,128]{3,2,1,0:T(1,128)S(1)}, f32[3,18,1,128]{3,2,1,0:T(1,128)S(1)}, u32[]{:S(2)}, u32[]{:S(2)}) collective-permute-start(f32[3,18,1,128]{3,2,1,0:T(1,128)S(1)} %get-tuple-element.78), channel_id=1, source_target_pairs={{0,1},{1,2},{2,3},{3,4},{4,5},{5,6},{6,7},{7,8},{8,9},{9,10},{10,1... | collective-permute-start | bytes 82952 | tf_op jit(solution)/shard_map/ppermute | solution.py:22
  138.3 9.3 %collective-permute-start.16 = (f32[3,1,8,64]{3,2,1,0:T(8,128)S(1)}, f32[3,1,8,64]{3,2,1,0:T(8,128)S(1)}, u32[]{:S(2)}, u32[]{:S(2)}) collective-permute-start(f32[3,1,8,64]{3,2,1,0:T(8,128)S(1)} %get-tuple-element.119), channel_id=1, source_target_pairs={{32,0},{64,32},{96,64},{128,96},{160,128},{192,160},{224,192},{256... | collective-permute-start | bytes 18440 | tf_op jit(solution)/shard_map/ppermute | solution.py:25
  140.3 9.3 %collective-permute-start.17 = (f32[3,1,8,64]{3,2,1,0:T(8,128)S(1)}, f32[3,1,8,64]{3,2,1,0:T(8,128)S(1)}, u32[]{:S(2)}, u32[]{:S(2)}) collective-permute-start(f32[3,1,8,64]{3,2,1,0:T(8,128)S(1)} %get-tuple-element.118), channel_id=1, source_target_pairs={{0,32},{32,64},{64,96},{96,128},{128,160},{160,192},{192,224},{224... | collective-permute-start | bytes 18440 | tf_op jit(solution)/shard_map/ppermute | solution.py:22
  143.3 53.9 %collective-permute-start.36 = (f32[1,2,16]{2,1,0:T(2,128)}, f32[1,2,16]{2,1,0:T(2,128)}, u32[]{:S(2)}, u32[]{:S(2)}) collective-permute-start(f32[1,2,16]{2,1,0:T(2,128)} %get-tuple-element.182), channel_id=1, source_target_pairs={{32,0},{64,32},{96,64},{128,96},{160,128},{192,160},{224,192},{256... | collective-permute-start | bytes 392 | tf_op jit(solution)/shard_map/ppermute | solution.py:25
  147.7 49.5 %collective-permute-start.37 = (f32[1,2,16]{2,1,0:T(2,128)}, f32[1,2,16]{2,1,0:T(2,128)}, u32[]{:S(2)}, u32[]{:S(2)}) collective-permute-start(f32[1,2,16]{2,1,0:T(2,128)} %get-tuple-element.181), channel_id=1, source_target_pairs={{0,32},{32,64},{64,96},{96,128},{128,160},{160,192},{192,224},{224... | collective-permute-start | bytes 392 | tf_op jit(solution)/shard_map/ppermute | solution.py:22
  149.6 9.9 %collective-permute-start.18 = (f32[3,10,1,64]{3,2,1,0:T(1,128)S(1)}, f32[3,10,1,64]{3,2,1,0:T(1,128)S(1)}, u32[]{:S(2)}, u32[]{:S(2)}) collective-permute-start(f32[3,10,1,64]{3,2,1,0:T(1,128)S(1)} %get-tuple-element.109), channel_id=1, source_target_pairs={{1,0},{2,1},{3,2},{4,3},{5,4},{6,5},{7,6},{8,7},{9,8},{10,9},{11,1... | collective-permute-start | bytes 23048 | tf_op jit(solution)/shard_map/ppermute | solution.py:25
  151.6 9.9 %collective-permute-start.19 = (f32[3,10,1,64]{3,2,1,0:T(1,128)S(1)}, f32[3,10,1,64]{3,2,1,0:T(1,128)S(1)}, u32[]{:S(2)}, u32[]{:S(2)}) collective-permute-start(f32[3,10,1,64]{3,2,1,0:T(1,128)S(1)} %get-tuple-element.108), channel_id=1, source_target_pairs={{0,1},{1,2},{2,3},{3,4},{4,5},{5,6},{6,7},{7,8},{8,9},{9,10},{10,1... | collective-permute-start | bytes 23048 | tf_op jit(solution)/shard_map/ppermute | solution.py:22
  155.5 10.7 %collective-permute-start.26 = (f32[6,1,32]{2,1,0:T(1,128)S(1)}, f32[6,1,32]{2,1,0:T(1,128)S(1)}, u32[]{:S(2)}, u32[]{:S(2)}) collective-permute-start(f32[6,1,32]{2,1,0:T(1,128)S(1)} %get-tuple-element.158), channel_id=1, source_target_pairs={{1,0},{2,1},{3,2},{4,3},{5,4},{6,5},{7,6},{8,7},{9,8},{10,9},{11,1... | collective-permute-start | bytes 2312 | tf_op jit(solution)/shard_map/ppermute | solution.py:25
  159.6 8.6 %collective-permute-start.27 = (f32[6,1,32]{2,1,0:T(1,128)S(1)}, f32[6,1,32]{2,1,0:T(1,128)S(1)}, u32[]{:S(2)}, u32[]{:S(2)}) collective-permute-start(f32[6,1,32]{2,1,0:T(1,128)S(1)} %get-tuple-element.157), channel_id=1, source_target_pairs={{0,1},{1,2},{2,3},{3,4},{4,5},{5,6},{6,7},{7,8},{8,9},{9,10},{10,1... | collective-permute-start | bytes 2312 | tf_op jit(solution)/shard_map/ppermute | solution.py:22
  161.9 6.3 %collective-permute-start.20 = (f32[3,1,8,64]{3,2,1,0:T(8,128)S(1)}, f32[3,1,8,64]{3,2,1,0:T(8,128)S(1)}, u32[]{:S(2)}, u32[]{:S(2)}) collective-permute-start(f32[3,1,8,64]{3,2,1,0:T(8,128)S(1)} %get-tuple-element.117), channel_id=1, source_target_pairs={{32,0},{64,32},{96,64},{128,96},{160,128},{192,160},{224,192},{256... | collective-permute-start | bytes 18440 | tf_op jit(solution)/shard_map/ppermute | solution.py:25
  166.2 6.2 %collective-permute-start.21 = (f32[3,1,8,64]{3,2,1,0:T(8,128)S(1)}, f32[3,1,8,64]{3,2,1,0:T(8,128)S(1)}, u32[]{:S(2)}, u32[]{:S(2)}) collective-permute-start(f32[3,1,8,64]{3,2,1,0:T(8,128)S(1)} %get-tuple-element.116), channel_id=1, source_target_pairs={{0,32},{32,64},{64,96},{96,128},{128,160},{160,192},{192,224},{224... | collective-permute-start | bytes 18440 | tf_op jit(solution)/shard_map/ppermute | solution.py:22
  172.5 8.6 %collective-permute-start.22 = (f32[3,10,1,64]{3,2,1,0:T(1,128)S(1)}, f32[3,10,1,64]{3,2,1,0:T(1,128)S(1)}, u32[]{:S(2)}, u32[]{:S(2)}) collective-permute-start(f32[3,10,1,64]{3,2,1,0:T(1,128)S(1)} %get-tuple-element.107), channel_id=1, source_target_pairs={{1,0},{2,1},{3,2},{4,3},{5,4},{6,5},{7,6},{8,7},{9,8},{10,9},{11,1... | collective-permute-start | bytes 23048 | tf_op jit(solution)/shard_map/ppermute | solution.py:25
  178.3 7.7 %collective-permute-start.23 = (f32[3,10,1,64]{3,2,1,0:T(1,128)S(1)}, f32[3,10,1,64]{3,2,1,0:T(1,128)S(1)}, u32[]{:S(2)}, u32[]{:S(2)}) collective-permute-start(f32[3,10,1,64]{3,2,1,0:T(1,128)S(1)} %get-tuple-element.106), channel_id=1, source_target_pairs={{0,1},{1,2},{2,3},{3,4},{4,5},{5,6},{6,7},{7,8},{8,9},{9,10},{10,1... | collective-permute-start | bytes 23048 | tf_op jit(solution)/shard_map/ppermute | solution.py:22
  194.8 6.2 %collective-permute-start.29 = (f32[3,1,4,32]{3,2,1,0:T(4,128)S(1)}, f32[3,1,4,32]{3,2,1,0:T(4,128)S(1)}, u32[]{:S(2)}, u32[]{:S(2)}) collective-permute-start(f32[3,1,4,32]{3,2,1,0:T(4,128)S(1)} %get-tuple-element.141), channel_id=1, source_target_pairs={{0,32},{32,64},{64,96},{96,128},{128,160},{160,192},{192,224},{224... | collective-permute-start | bytes 4616 | tf_op jit(solution)/shard_map/ppermute | solution.py:22
  201.0 11.8 %collective-permute-start.30 = (f32[3,6,1,32]{3,2,1,0:T(1,128)S(1)}, f32[3,6,1,32]{3,2,1,0:T(1,128)S(1)}, u32[]{:S(2)}, u32[]{:S(2)}) collective-permute-start(f32[3,6,1,32]{3,2,1,0:T(1,128)S(1)} %get-tuple-element.129), channel_id=1, source_target_pairs={{1,0},{2,1},{3,2},{4,3},{5,4},{6,5},{7,6},{8,7},{9,8},{10,9},{11,1... | collective-permute-start | bytes 6920 | tf_op jit(solution)/shard_map/ppermute | solution.py:25
  202.9 9.9 %collective-permute-start.31 = (f32[3,6,1,32]{3,2,1,0:T(1,128)S(1)}, f32[3,6,1,32]{3,2,1,0:T(1,128)S(1)}, u32[]{:S(2)}, u32[]{:S(2)}) collective-permute-start(f32[3,6,1,32]{3,2,1,0:T(1,128)S(1)} %get-tuple-element.128), channel_id=1, source_target_pairs={{0,1},{1,2},{2,3},{3,4},{4,5},{5,6},{6,7},{7,8},{8,9},{9,10},{10,1... | collective-permute-start | bytes 6920 | tf_op jit(solution)/shard_map/ppermute | solution.py:22
  206.8 11.4 %collective-permute-start.38 = (f32[4,1,16]{2,1,0:T(1,128)S(1)}, f32[4,1,16]{2,1,0:T(1,128)S(1)}, u32[]{:S(2)}, u32[]{:S(2)}) collective-permute-start(f32[4,1,16]{2,1,0:T(1,128)S(1)} %get-tuple-element.179), channel_id=1, source_target_pairs={{1,0},{2,1},{3,2},{4,3},{5,4},{6,5},{7,6},{8,7},{9,8},{10,9},{11,1... | collective-permute-start | bytes 776 | tf_op jit(solution)/shard_map/ppermute | solution.py:25
  210.9 7.6 %collective-permute-start.39 = (f32[4,1,16]{2,1,0:T(1,128)S(1)}, f32[4,1,16]{2,1,0:T(1,128)S(1)}, u32[]{:S(2)}, u32[]{:S(2)}) collective-permute-start(f32[4,1,16]{2,1,0:T(1,128)S(1)} %get-tuple-element.178), channel_id=1, source_target_pairs={{0,1},{1,2},{2,3},{3,4},{4,5},{5,6},{6,7},{7,8},{8,9},{9,10},{10,1... | collective-permute-start | bytes 776 | tf_op jit(solution)/shard_map/ppermute | solution.py:22
  215.9 6.2 %collective-permute-start.33 = (f32[3,1,4,32]{3,2,1,0:T(4,128)S(1)}, f32[3,1,4,32]{3,2,1,0:T(4,128)S(1)}, u32[]{:S(2)}, u32[]{:S(2)}) collective-permute-start(f32[3,1,4,32]{3,2,1,0:T(4,128)S(1)} %get-tuple-element.139), channel_id=1, source_target_pairs={{0,32},{32,64},{64,96},{96,128},{128,160},{160,192},{192,224},{224... | collective-permute-start | bytes 4616 | tf_op jit(solution)/shard_map/ppermute | solution.py:22
  222.0 8.8 %collective-permute-start.34 = (f32[3,6,1,32]{3,2,1,0:T(1,128)S(1)}, f32[3,6,1,32]{3,2,1,0:T(1,128)S(1)}, u32[]{:S(2)}, u32[]{:S(2)}) collective-permute-start(f32[3,6,1,32]{3,2,1,0:T(1,128)S(1)} %get-tuple-element.127), channel_id=1, source_target_pairs={{1,0},{2,1},{3,2},{4,3},{5,4},{6,5},{7,6},{8,7},{9,8},{10,9},{11,1... | collective-permute-start | bytes 6920 | tf_op jit(solution)/shard_map/ppermute | solution.py:25
  228.1 7.7 %collective-permute-start.35 = (f32[3,6,1,32]{3,2,1,0:T(1,128)S(1)}, f32[3,6,1,32]{3,2,1,0:T(1,128)S(1)}, u32[]{:S(2)}, u32[]{:S(2)}) collective-permute-start(f32[3,6,1,32]{3,2,1,0:T(1,128)S(1)} %get-tuple-element.126), channel_id=1, source_target_pairs={{0,1},{1,2},{2,3},{3,4},{4,5},{5,6},{6,7},{7,8},{8,9},{9,10},{10,1... | collective-permute-start | bytes 6920 | tf_op jit(solution)/shard_map/ppermute | solution.py:22
  239.2 6.1 %collective-permute-start.41 = (f32[3,1,2,16]{3,2,1,0:T(2,128)S(1)}, f32[3,1,2,16]{3,2,1,0:T(2,128)S(1)}, u32[]{:S(2)}, u32[]{:S(2)}) collective-permute-start(f32[3,1,2,16]{3,2,1,0:T(2,128)S(1)} %get-tuple-element.176), channel_id=1, source_target_pairs={{0,32},{32,64},{64,96},{96,128},{128,160},{160,192},{192,224},{224... | collective-permute-start | bytes 1160 | tf_op jit(solution)/shard_map/ppermute | solution.py:22
  247.2 7.6 %collective-permute-start.43 = (f32[3,4,1,16]{3,2,1,0:T(1,128)S(1)}, f32[3,4,1,16]{3,2,1,0:T(1,128)S(1)}, u32[]{:S(2)}, u32[]{:S(2)}) collective-permute-start(f32[3,4,1,16]{3,2,1,0:T(1,128)S(1)} %get-tuple-element.155), channel_id=1, source_target_pairs={{0,1},{1,2},{2,3},{3,4},{4,5},{5,6},{6,7},{7,8},{8,9},{9,10},{10,1... | collective-permute-start | bytes 2312 | tf_op jit(solution)/shard_map/ppermute | solution.py:22
  257.0 6.1 %collective-permute-start.45 = (f32[3,1,2,16]{3,2,1,0:T(2,128)S(1)}, f32[3,1,2,16]{3,2,1,0:T(2,128)S(1)}, u32[]{:S(2)}, u32[]{:S(2)}) collective-permute-start(f32[3,1,2,16]{3,2,1,0:T(2,128)S(1)} %get-tuple-element.174), channel_id=1, source_target_pairs={{0,32},{32,64},{64,96},{96,128},{128,160},{160,192},{192,224},{224... | collective-permute-start | bytes 1160 | tf_op jit(solution)/shard_map/ppermute | solution.py:22
  265.1 7.6 %collective-permute-start.47 = (f32[3,4,1,16]{3,2,1,0:T(1,128)S(1)}, f32[3,4,1,16]{3,2,1,0:T(1,128)S(1)}, u32[]{:S(2)}, u32[]{:S(2)}) collective-permute-start(f32[3,4,1,16]{3,2,1,0:T(1,128)S(1)} %get-tuple-element.153), channel_id=1, source_target_pairs={{0,1},{1,2},{2,3},{3,4},{4,5},{5,6},{6,7},{7,8},{8,9},{9,10},{10,1... | collective-permute-start | bytes 2312 | tf_op jit(solution)/shard_map/ppermute | solution.py:22
  274.9 6.1 %collective-permute-start.49 = (f32[3,1,2,16]{3,2,1,0:T(2,128)S(1)}, f32[3,1,2,16]{3,2,1,0:T(2,128)S(1)}, u32[]{:S(2)}, u32[]{:S(2)}) collective-permute-start(f32[3,1,2,16]{3,2,1,0:T(2,128)S(1)} %get-tuple-element.172), channel_id=1, source_target_pairs={{0,32},{32,64},{64,96},{96,128},{128,160},{160,192},{192,224},{224... | collective-permute-start | bytes 1160 | tf_op jit(solution)/shard_map/ppermute | solution.py:22
  283.0 7.6 %collective-permute-start.51 = (f32[3,4,1,16]{3,2,1,0:T(1,128)S(1)}, f32[3,4,1,16]{3,2,1,0:T(1,128)S(1)}, u32[]{:S(2)}, u32[]{:S(2)}) collective-permute-start(f32[3,4,1,16]{3,2,1,0:T(1,128)S(1)} %get-tuple-element.151), channel_id=1, source_target_pairs={{0,1},{1,2},{2,3},{3,4},{4,5},{5,6},{6,7},{7,8},{8,9},{9,10},{10,1... | collective-permute-start | bytes 2312 | tf_op jit(solution)/shard_map/ppermute | solution.py:22
  292.8 6.1 %collective-permute-start.53 = (f32[3,1,2,16]{3,2,1,0:T(2,128)S(1)}, f32[3,1,2,16]{3,2,1,0:T(2,128)S(1)}, u32[]{:S(2)}, u32[]{:S(2)}) collective-permute-start(f32[3,1,2,16]{3,2,1,0:T(2,128)S(1)} %get-tuple-element.170), channel_id=1, source_target_pairs={{0,32},{32,64},{64,96},{96,128},{128,160},{160,192},{192,224},{224... | collective-permute-start | bytes 1160 | tf_op jit(solution)/shard_map/ppermute | solution.py:22
  300.8 7.6 %collective-permute-start.55 = (f32[3,4,1,16]{3,2,1,0:T(1,128)S(1)}, f32[3,4,1,16]{3,2,1,0:T(1,128)S(1)}, u32[]{:S(2)}, u32[]{:S(2)}) collective-permute-start(f32[3,4,1,16]{3,2,1,0:T(1,128)S(1)} %get-tuple-element.149), channel_id=1, source_target_pairs={{0,1},{1,2},{2,3},{3,4},{4,5},{5,6},{6,7},{7,8},{8,9},{9,10},{10,1... | collective-permute-start | bytes 2312 | tf_op jit(solution)/shard_map/ppermute | solution.py:22
  310.6 6.1 %collective-permute-start.57 = (f32[3,1,2,16]{3,2,1,0:T(2,128)S(1)}, f32[3,1,2,16]{3,2,1,0:T(2,128)S(1)}, u32[]{:S(2)}, u32[]{:S(2)}) collective-permute-start(f32[3,1,2,16]{3,2,1,0:T(2,128)S(1)} %get-tuple-element.168), channel_id=1, source_target_pairs={{0,32},{32,64},{64,96},{96,128},{128,160},{160,192},{192,224},{224... | collective-permute-start | bytes 1160 | tf_op jit(solution)/shard_map/ppermute | solution.py:22
  318.7 7.6 %collective-permute-start.59 = (f32[3,4,1,16]{3,2,1,0:T(1,128)S(1)}, f32[3,4,1,16]{3,2,1,0:T(1,128)S(1)}, u32[]{:S(2)}, u32[]{:S(2)}) collective-permute-start(f32[3,4,1,16]{3,2,1,0:T(1,128)S(1)} %get-tuple-element.147), channel_id=1, source_target_pairs={{0,1},{1,2},{2,3},{3,4},{4,5},{5,6},{6,7},{7,8},{8,9},{9,10},{10,1... | collective-permute-start | bytes 2312 | tf_op jit(solution)/shard_map/ppermute | solution.py:22
  328.5 6.1 %collective-permute-start.61 = (f32[3,1,2,16]{3,2,1,0:T(2,128)S(1)}, f32[3,1,2,16]{3,2,1,0:T(2,128)S(1)}, u32[]{:S(2)}, u32[]{:S(2)}) collective-permute-start(f32[3,1,2,16]{3,2,1,0:T(2,128)S(1)} %get-tuple-element.166), channel_id=1, source_target_pairs={{0,32},{32,64},{64,96},{96,128},{128,160},{160,192},{192,224},{224... | collective-permute-start | bytes 1160 | tf_op jit(solution)/shard_map/ppermute | solution.py:22
  336.6 7.6 %collective-permute-start.63 = (f32[3,4,1,16]{3,2,1,0:T(1,128)S(1)}, f32[3,4,1,16]{3,2,1,0:T(1,128)S(1)}, u32[]{:S(2)}, u32[]{:S(2)}) collective-permute-start(f32[3,4,1,16]{3,2,1,0:T(1,128)S(1)} %get-tuple-element.145), channel_id=1, source_target_pairs={{0,1},{1,2},{2,3},{3,4},{4,5},{5,6},{6,7},{7,8},{8,9},{9,10},{10,1... | collective-permute-start | bytes 2312 | tf_op jit(solution)/shard_map/ppermute | solution.py:22
  346.4 6.1 %collective-permute-start.65 = (f32[3,1,2,16]{3,2,1,0:T(2,128)S(1)}, f32[3,1,2,16]{3,2,1,0:T(2,128)S(1)}, u32[]{:S(2)}, u32[]{:S(2)}) collective-permute-start(f32[3,1,2,16]{3,2,1,0:T(2,128)S(1)} %get-tuple-element.164), channel_id=1, source_target_pairs={{0,32},{32,64},{64,96},{96,128},{128,160},{160,192},{192,224},{224... | collective-permute-start | bytes 1160 | tf_op jit(solution)/shard_map/ppermute | solution.py:22
  354.5 7.6 %collective-permute-start.67 = (f32[3,4,1,16]{3,2,1,0:T(1,128)S(1)}, f32[3,4,1,16]{3,2,1,0:T(1,128)S(1)}, u32[]{:S(2)}, u32[]{:S(2)}) collective-permute-start(f32[3,4,1,16]{3,2,1,0:T(1,128)S(1)} %get-tuple-element.143), channel_id=1, source_target_pairs={{0,1},{1,2},{2,3},{3,4},{4,5},{5,6},{6,7},{7,8},{8,9},{9,10},{10,1... | collective-permute-start | bytes 2312 | tf_op jit(solution)/shard_map/ppermute | solution.py:22
  364.7 6.2 %collective-permute-start.69 = (f32[3,1,4,32]{3,2,1,0:T(4,128)S(1)}, f32[3,1,4,32]{3,2,1,0:T(4,128)S(1)}, u32[]{:S(2)}, u32[]{:S(2)}) collective-permute-start(f32[3,1,4,32]{3,2,1,0:T(4,128)S(1)} %get-tuple-element.137), channel_id=1, source_target_pairs={{0,32},{32,64},{64,96},{96,128},{128,160},{160,192},{192,224},{224... | collective-permute-start | bytes 4616 | tf_op jit(solution)/shard_map/ppermute | solution.py:22
  372.8 7.7 %collective-permute-start.71 = (f32[3,6,1,32]{3,2,1,0:T(1,128)S(1)}, f32[3,6,1,32]{3,2,1,0:T(1,128)S(1)}, u32[]{:S(2)}, u32[]{:S(2)}) collective-permute-start(f32[3,6,1,32]{3,2,1,0:T(1,128)S(1)} %get-tuple-element.124), channel_id=1, source_target_pairs={{0,1},{1,2},{2,3},{3,4},{4,5},{5,6},{6,7},{7,8},{8,9},{9,10},{10,1... | collective-permute-start | bytes 6920 | tf_op jit(solution)/shard_map/ppermute | solution.py:22
  382.7 6.2 %collective-permute-start.73 = (f32[3,1,4,32]{3,2,1,0:T(4,128)S(1)}, f32[3,1,4,32]{3,2,1,0:T(4,128)S(1)}, u32[]{:S(2)}, u32[]{:S(2)}) collective-permute-start(f32[3,1,4,32]{3,2,1,0:T(4,128)S(1)} %get-tuple-element.135), channel_id=1, source_target_pairs={{0,32},{32,64},{64,96},{96,128},{128,160},{160,192},{192,224},{224... | collective-permute-start | bytes 4616 | tf_op jit(solution)/shard_map/ppermute | solution.py:22
  390.8 7.7 %collective-permute-start.75 = (f32[3,6,1,32]{3,2,1,0:T(1,128)S(1)}, f32[3,6,1,32]{3,2,1,0:T(1,128)S(1)}, u32[]{:S(2)}, u32[]{:S(2)}) collective-permute-start(f32[3,6,1,32]{3,2,1,0:T(1,128)S(1)} %get-tuple-element.122), channel_id=1, source_target_pairs={{0,1},{1,2},{2,3},{3,4},{4,5},{5,6},{6,7},{7,8},{8,9},{9,10},{10,1... | collective-permute-start | bytes 6920 | tf_op jit(solution)/shard_map/ppermute | solution.py:22
  401.6 6.2 %collective-permute-start.77 = (f32[3,1,8,64]{3,2,1,0:T(8,128)S(1)}, f32[3,1,8,64]{3,2,1,0:T(8,128)S(1)}, u32[]{:S(2)}, u32[]{:S(2)}) collective-permute-start(f32[3,1,8,64]{3,2,1,0:T(8,128)S(1)} %get-tuple-element.114), channel_id=1, source_target_pairs={{0,32},{32,64},{64,96},{96,128},{128,160},{160,192},{192,224},{224... | collective-permute-start | bytes 18440 | tf_op jit(solution)/shard_map/ppermute | solution.py:22
  409.8 7.7 %collective-permute-start.79 = (f32[3,10,1,64]{3,2,1,0:T(1,128)S(1)}, f32[3,10,1,64]{3,2,1,0:T(1,128)S(1)}, u32[]{:S(2)}, u32[]{:S(2)}) collective-permute-start(f32[3,10,1,64]{3,2,1,0:T(1,128)S(1)} %get-tuple-element.104), channel_id=1, source_target_pairs={{0,1},{1,2},{2,3},{3,4},{4,5},{5,6},{6,7},{7,8},{8,9},{9,10},{10,1... | collective-permute-start | bytes 23048 | tf_op jit(solution)/shard_map/ppermute | solution.py:22
  419.9 6.2 %collective-permute-start.81 = (f32[3,1,8,64]{3,2,1,0:T(8,128)S(1)}, f32[3,1,8,64]{3,2,1,0:T(8,128)S(1)}, u32[]{:S(2)}, u32[]{:S(2)}) collective-permute-start(f32[3,1,8,64]{3,2,1,0:T(8,128)S(1)} %get-tuple-element.112), channel_id=1, source_target_pairs={{0,32},{32,64},{64,96},{96,128},{128,160},{160,192},{192,224},{224... | collective-permute-start | bytes 18440 | tf_op jit(solution)/shard_map/ppermute | solution.py:22
  428.1 7.7 %collective-permute-start.83 = (f32[3,10,1,64]{3,2,1,0:T(1,128)S(1)}, f32[3,10,1,64]{3,2,1,0:T(1,128)S(1)}, u32[]{:S(2)}, u32[]{:S(2)}) collective-permute-start(f32[3,10,1,64]{3,2,1,0:T(1,128)S(1)} %get-tuple-element.102), channel_id=1, source_target_pairs={{0,1},{1,2},{2,3},{3,4},{4,5},{5,6},{6,7},{7,8},{8,9},{9,10},{10,1... | collective-permute-start | bytes 23048 | tf_op jit(solution)/shard_map/ppermute | solution.py:22
  445.0 6.4 %collective-permute-start.85 = (f32[3,1,16,128]{3,2,1,0:T(8,128)S(1)}, f32[3,1,16,128]{3,2,1,0:T(8,128)S(1)}, u32[]{:S(2)}, u32[]{:S(2)}) collective-permute-start(f32[3,1,16,128]{3,2,1,0:T(8,128)S(1)} %get-tuple-element.86), channel_id=1, source_target_pairs={{0,32},{32,64},{64,96},{96,128},{128,160},{160,192},{192,224},{224... | collective-permute-start | bytes 73736 | tf_op jit(solution)/shard_map/ppermute | solution.py:22
  453.3 7.9 %collective-permute-start.87 = (f32[3,18,1,128]{3,2,1,0:T(1,128)S(1)}, f32[3,18,1,128]{3,2,1,0:T(1,128)S(1)}, u32[]{:S(2)}, u32[]{:S(2)}) collective-permute-start(f32[3,18,1,128]{3,2,1,0:T(1,128)S(1)} %get-tuple-element.76), channel_id=1, source_target_pairs={{0,1},{1,2},{2,3},{3,4},{4,5},{5,6},{6,7},{7,8},{8,9},{9,10},{10,1... | collective-permute-start | bytes 82952 | tf_op jit(solution)/shard_map/ppermute | solution.py:22
  464.4 6.4 %collective-permute-start.89 = (f32[3,1,16,128]{3,2,1,0:T(8,128)S(1)}, f32[3,1,16,128]{3,2,1,0:T(8,128)S(1)}, u32[]{:S(2)}, u32[]{:S(2)}) collective-permute-start(f32[3,1,16,128]{3,2,1,0:T(8,128)S(1)} %get-tuple-element.84), channel_id=1, source_target_pairs={{0,32},{32,64},{64,96},{96,128},{128,160},{160,192},{192,224},{224... | collective-permute-start | bytes 73736 | tf_op jit(solution)/shard_map/ppermute | solution.py:22
  472.7 7.9 %collective-permute-start.91 = (f32[3,18,1,128]{3,2,1,0:T(1,128)S(1)}, f32[3,18,1,128]{3,2,1,0:T(1,128)S(1)}, u32[]{:S(2)}, u32[]{:S(2)}) collective-permute-start(f32[3,18,1,128]{3,2,1,0:T(1,128)S(1)} %get-tuple-element.74), channel_id=1, source_target_pairs={{0,1},{1,2},{2,3},{3,4},{4,5},{5,6},{6,7},{7,8},{8,9},{9,10},{10,1... | collective-permute-start | bytes 82952 | tf_op jit(solution)/shard_map/ppermute | solution.py:22
  483.9 6.4 %collective-permute-start.93 = (f32[3,1,16,128]{3,2,1,0:T(8,128)S(1)}, f32[3,1,16,128]{3,2,1,0:T(8,128)S(1)}, u32[]{:S(2)}, u32[]{:S(2)}) collective-permute-start(f32[3,1,16,128]{3,2,1,0:T(8,128)S(1)} %get-tuple-element.82), channel_id=1, source_target_pairs={{0,32},{32,64},{64,96},{96,128},{128,160},{160,192},{192,224},{224... | collective-permute-start | bytes 73736 | tf_op jit(solution)/shard_map/ppermute | solution.py:22
  492.2 7.9 %collective-permute-start.95 = (f32[3,18,1,128]{3,2,1,0:T(1,128)S(1)}, f32[3,18,1,128]{3,2,1,0:T(1,128)S(1)}, u32[]{:S(2)}, u32[]{:S(2)}) collective-permute-start(f32[3,18,1,128]{3,2,1,0:T(1,128)S(1)} %get-tuple-element.72), channel_id=1, source_target_pairs={{0,1},{1,2},{2,3},{3,4},{4,5},{5,6},{6,7},{7,8},{8,9},{9,10},{10,1... | collective-permute-start | bytes 82952 | tf_op jit(solution)/shard_map/ppermute | solution.py:22
  (84 other events, 2969.3 us)
where the time goes:
time: 505 us; the launch traced here: 502 us
  starting transfers between devices  266 us (53%)
  waiting for transfers between devices  142 us (28%)
  local copies, waits for them, and re-layouts  51 us (10%)
  other arithmetic  39.8 us (8%)
    ppermute x48, waiting for transfers between devices, padded_2(): lax.ppermute(lax.slice_in_dim(block, block.shape[dim] - width, None, axis...  142 us
    ppermute x48, starting transfers between devices, padded_2(): lax.ppermute(lax.slice_in_dim(block, block.shape[dim] - width, None, axis...  135 us
    ppermute x48, starting transfers between devices, padded_2(): lax.ppermute(lax.slice_in_dim(block, 0, width, axis=dim), axis, backward)  131 us
    reshape x4, local copies, waits for them, and re-layouts, shrink(): blocks = arr.reshape(tuple(lead) + (za // 2, 2, yb // 2, 2, xc // 2, 2))  40.6 us
    reduce_sum x6, other arithmetic, shrink(): return blocks.mean(axis=(-5, -3, -1))  14.7 us
  transfers between devices with their start and end apart: 96, of which 38 were waited for; matrix products, arithmetic and copies ran while one was open for 13% of the time, Pallas kernels for 0%

commit v1 on v0

v1 whole, which is shorter than its diff:
```python
import functools

import jax
import jax.numpy as jnp
from jax import lax
from jax.experimental import pallas as pl
from jax.experimental.pallas import tpu as pltpu
from jax.sharding import PartitionSpec as P

CLASSES = 8
OMEGA = 0.6
COUPLE = 0.05
SLAB = 16
COL = 32
F32 = jnp.float32


def lanes_of(rows):
    return lax.broadcasted_iota(jnp.int32, (rows, 128), 1)


def lane_next(v, step):
    return pltpu.roll(v, 128 - step, 1)


def lane_prev(v, step):
    return pltpu.roll(v, step, 1)


def row_next(v):
    return pltpu.roll(v, v.shape[0] - 1, 0)


def row_prev(v):
    return pltpu.roll(v, 1, 0)


def spread(v, lane, width):
    step = 1
    while step < width:
        v = v + jnp.where((lane & step) != 0, lane_prev(v, step), lane_next(v, step))
        step *= 2
    return v


def coefficients(k, k_lo, k_hi, scale, step, mask, total=None):
    lane = lanes_of(k.shape[0])
    half = 0.5 * scale
    k_next = lane_next(k, step)
    cx = jnp.where(lane < 128 - step, half * (k + k_next), 0.0)
    ky = row_next(k)
    cy = half * (k + ky)
    cz = half * (k + k_hi)
    if total is None:
        sides = jnp.where(lane < 128 - step, k_next, 0.0) + jnp.where(lane >= step, lane_prev(k, step), 0.0)
        total = half * (6.0 * k + sides + ky + row_prev(k) + k_lo + k_hi)
    diag = total + 2.0 * COUPLE * k
    top = OMEGA if mask is None else OMEGA * mask
    weight = jnp.where(k > 0.0, top / diag, 0.0)
    return cx, cy, cz, total + COUPLE * k, weight


def remainder(b, u, u_lo, u_hi, k, cx, cy, cz, cz_lo, e, step):
    cx_lo = lane_prev(cx, step)
    cy_lo = row_prev(cy)
    shared = COUPLE * k * (u[0] + u[1] + u[2])
    out = []
    for c in range(3):
        v = u[c]
        around = cx * lane_next(v, step) + cx_lo * lane_prev(v, step)
        around = around + cy * row_next(v) + cy_lo * row_prev(v)
        around = around + cz * u_hi[c] + cz_lo * u_lo[c]
        out.append((b[c] - shared) + (around - e * v))
    return out


def fill_coefficients(k_ref, co, planes, scale, step, mask_ref=None, total_ref=None):
    cx_ref, cy_ref, cz_ref, e_ref, w_ref = co

    def body(p, carry):
        mask = None if mask_ref is None else mask_ref[p]
        total = None if total_ref is None else total_ref[p]
        cx, cy, cz, e, w = coefficients(k_ref[p], k_ref[p - 1], k_ref[p + 1], scale, step, mask, total)
        cx_ref[p] = cx
        cy_ref[p] = cy
        cz_ref[p] = cz
        e_ref[p] = e
        w_ref[p] = w
        return carry

    lax.fori_loop(planes[0], planes[1], body, 0)


def left_over(p, b_ref, u_ref, k_ref, co, step, rows=slice(None)):
    cx_ref, cy_ref, cz_ref, e_ref, _ = co
    b = [b_ref[c, p] for c in range(3)]
    u = [u_ref[c, p] for c in range(3)]
    lo = [u_ref[c, p - 1] for c in range(3)]
    hi = [u_ref[c, p + 1] for c in range(3)]
    return u, remainder(b, u, lo, hi, k_ref[p], cx_ref[p], cy_ref[p], cz_ref[p], cz_ref[p - 1], e_ref[p], step)


def sweep(planes, b_ref, u_ref, new_ref, k_ref, co, step):
    def body(p, carry):
        u, rest = left_over(p, b_ref, u_ref, k_ref, co, step)
        w = co[4][p]
        for c in range(3):
            new_ref[c, p] = u[c] + w * rest[c]
        return carry

    lax.fori_loop(planes[0], planes[1], body, 0)


def first_sweep(planes, b_ref, new_ref, w_ref):
    def body(p, carry):
        w = w_ref[p]
        for c in range(3):
            new_ref[c, p] = w * b_ref[c, p]
        return carry

    lax.fori_loop(planes[0], planes[1], body, 0)


def block_mean(a, b, tmp, step):
    lane = lanes_of(a.shape[0])
    s = a + b
    s = s + jnp.where((lane & step) != 0, lane_prev(s, step), lane_next(s, step))
    n = a.shape[0]
    tmp[0:n] = s
    return 0.125 * (tmp[pl.ds(0, n // 2, stride=2)] + tmp[pl.ds(1, n // 2, stride=2)])


def double_rows(v, tmp):
    n = v.shape[0]
    tmp[pl.ds(0, n, stride=2)] = v
    tmp[pl.ds(1, n, stride=2)] = v


def prep_kernel(moduli, load, density, fixed, k_out, m_out, low, high):
    for z in range(16):
        d = density[z]
        k = jnp.zeros((16, 128), F32)
        for klass in range(CLASSES):
            k = jnp.where(d == klass, moduli[klass], k)
        m = 1.0 - fixed[z].astype(F32)
        k_out[z] = k
        m_out[z] = m
        for c in range(3):
            low[z, 4 * c : 4 * c + 4] = load[c, z, 0:4]
            high[z, 4 * c : 4 * c + 4] = load[c, z, 12:16]
        low[z, 12:16] = m[0:4]
        high[z, 12:16] = m[12:16]
        low[z, 16:24] = k[0:8]
        high[z, 16:24] = k[8:16]


def planes_kernel(load, k, m, from_low, from_high, low, high):
    for out, start in ((low, 0), (high, 12)):
        for q in range(4):
            z = start + q
            for a in range(4):
                base = 24 * (4 * a + q)
                own = load[a, z] if a < 3 else m[z]
                out[base : base + 4] = from_low[z, 4 * a : 4 * a + 4]
                out[base + 4 : base + 20] = own
                out[base + 20 : base + 24] = from_high[z, 4 * a : 4 * a + 4]
        for q in range(5):
            z = q if start == 0 else 11 + q
            base = 384 + 32 * q
            out[base : base + 8] = from_low[z, 16:24]
            out[base + 8 : base + 24] = k[z]
            out[base + 24 : base + 32] = from_high[z, 16:24]


def fine_kernel(load, k_own, m_own, y_low, y_high, z_low, z_high,
                b, u, k, m, message,
                cx, cy, cz, e, w, first, k1, tmp):
    co = (cx, cy, cz, e, w)
    for z in range(16):
        p = z + 5
        for c in range(3):
            b[c, p, 4:8] = y_low[z, 4 * c : 4 * c + 4]
            b[c, p, 8:24] = load[c, z]
            b[c, p, 24:28] = y_high[z, 4 * c : 4 * c + 4]
        m[p, 4:8] = y_low[z, 12:16]
        m[p, 8:24] = m_own[z]
        m[p, 24:28] = y_high[z, 12:16]
        k[p, 0:8] = y_low[z, 16:24]
        k[p, 8:24] = k_own[z]
        k[p, 24:32] = y_high[z, 16:24]
    for src, start, k_start in ((z_low, 1, 0), (z_high, 21, 21)):
        for q in range(4):
            for a in range(4):
                part = src[24 * (4 * a + q) : 24 * (4 * a + q) + 24]
                if a < 3:
                    b[a, start + q, 4:28] = part
                else:
                    m[start + q, 4:28] = part
        for q in range(5):
            k[k_start + q] = src[384 + 32 * q : 416 + 32 * q]
    fill_coefficients(k, co, (1, 25), 1.0, 1, m)
    first_sweep((1, 25), b, first, w)
    sweep((2, 24), b, first, u, k, co, 1)

    for z1 in range(-1, 9):
        p = 2 * z1 + 5
        k1[z1 + 1] = block_mean(k[p], k[p + 1], tmp, 1)
    lane = lanes_of(16)
    odd = (lane & 1) != 0
    for z1 in range(8):
        p = 2 * z1 + 5
        rests = [left_over(q, b, u, k, co, 1)[1] for q in (p, p + 1)]
        parts = [
            block_mean(m[p] * rests[0][c], m[p + 1] * rests[1][c], tmp, 1) for c in range(3)
        ]
        centre = k1[z1 + 1]
        sides = jnp.where(lane < 126, lane_next(centre, 2), 0.0) + jnp.where(lane >= 2, lane_prev(centre, 2), 0.0)
        total = 0.125 * (6.0 * centre + sides + row_next(centre) + row_prev(centre) + k1[z1] + k1[z1 + 2])
        message[0, z1] = jnp.where(odd, parts[1], parts[0])[4:12]
        message[1, z1] = jnp.where(odd, centre, parts[2])[4:12]
        message[2, z1] = total[4:12]


def middle_kernel(place, z_low, z_mid, z_high,
                  b1, u1, k1, t1, b2, k2, packed,
                  cx, cy, cz, e, w, first, rest2, cx2, cy2, cz2, e2, w2, u2a, u2b, tmp):
    co = (cx, cy, cz, e, w)
    lane = lanes_of(24)
    odd = (lane & 1) != 0
    for src, start in ((z_low, 0), (z_mid, 8), (z_high, 16)):
        for q in range(8):
            p = start + q
            v = src[0, q]
            b1[0, p] = jnp.where(odd, lane_prev(v, 1), v)
            b1[1, p] = jnp.where(odd, v, lane_next(v, 1))
            v = src[1, q]
            b1[2, p] = jnp.where(odd, lane_prev(v, 1), v)
            k1[p] = jnp.where(odd, v, lane_next(v, 1))
            t1[p] = src[2, q]

    k_top = 23

    def fill(p, carry):
        k_hi = k1[jnp.minimum(p + 1, k_top)]
        cxv, cyv, czv, ev, wv = coefficients(k1[p], k1[p], k_hi, 0.25, 2, None, t1[p])
        cx[p] = cxv
        cy[p] = cyv
        cz[p] = czv
        e[p] = ev
        w[p] = wv
        return carry

    lax.fori_loop(0, 24, fill, 0)
    first_sweep((0, 24), b1, first, w)
    sweep((1, 23), b1, first, u1, k1, co, 2)
    for q2 in range(12):
        k2[q2, 4:16] = block_mean(k1[2 * q2], k1[2 * q2 + 1], tmp, 2)
        k2[q2, 0:4] = jnp.zeros((4, 128), F32)
    for q2 in range(1, 11):
        rests = [left_over(p, b1, u1, k1, co, 2)[1] for p in (2 * q2, 2 * q2 + 1)]
        for c in range(3):
            b2[c, q2, 4:16] = block_mean(rests[0][c], rests[1][c], tmp, 2)
            b2[c, q2, 0:4] = jnp.zeros((4, 128), F32)
    co2 = (cx2, cy2, cz2, e2, w2)
    fill_coefficients(k2, co2, (1, 11), 0.0625, 4)
    first_sweep((1, 11), b2, u2a, w2)
    sweep((2, 10), b2, u2a, u2b, k2, co2, 4)
    j = place[0] // 2
    lane = lanes_of(8)
    group = lane & 7
    pack = jnp.zeros((8, 128), F32)
    for zz in range(2):
        rests = [left_over(p, b2, u2b, k2, co2, 4)[1] for p in (4 + 2 * zz, 5 + 2 * zz)]
        parts = [block_mean(rests[0][c], rests[1][c], tmp, 4) for c in range(3)]
        parts.append(block_mean(k2[4 + 2 * zz], k2[5 + 2 * zz], tmp, 4))
        for a in range(4):
            pack = jnp.where(group == ((j + 2 * a + zz) & 7), parts[a], pack)
    packed[0:2] = pack[4:6]
    quad = lane & 3
    for c in range(3):
        v = u2b[c, 7, 8:16]
        for zz in (2, 1, 0):
            v = jnp.where(quad == zz, u2b[c, 4 + zz, 8:16], v)
        packed[2 + 4 * c : 6 + 4 * c] = v[0:4]
    packed[14:16] = jnp.zeros((2, 128), F32)


def window_kernel(place, received, out, tmp):
    c = place[1]
    for q in range(12):
        peer = c - 6 + q
        inside = jnp.logical_and(peer >= 0, peer < COL).astype(F32)
        tmp[2 * q : 2 * q + 2] = inside * received[jnp.clip(peer, 0, COL - 1), 0:2]
    for q in range(3):
        peer = c - 1 + q
        inside = jnp.logical_and(peer >= 0, peer < COL).astype(F32)
        for comp in range(3):
            part = received[jnp.clip(peer, 0, COL - 1), 2 + 4 * comp : 6 + 4 * comp]
            base = 24 + 12 * comp + 4 * q
            tmp[base : base + 4] = inside * part
    tmp[60:64] = jnp.zeros((4, 128), F32)
    whole = tmp[...]
    for d in range(SLAB):
        out[d] = whole


def upper_kernel(place, received, b2, k2, b1, u1, k1, t1, b0, u0, k0, m0,
                 field, residual,
                 b3, k3, co3, u3a, u3b, co2, u2a, u2b, co1, u1a, u1b, co0, u0a, u0b, tmp):
    d = place[0]
    lane = lanes_of(24)
    group = lane & 7
    for a in range(2):
        for r in range(8):
            mix = jnp.zeros((24, 128), F32)
            for j in range(8):
                mix = jnp.where(group == ((j + r) & 7), received[2 * j + a, 0:24], mix)
            if r:
                mix = jnp.where(group < 8 - r, lane_next(mix, r), lane_prev(mix, 8 - r))
            arr, plane = r // 2, 2 * a + r % 2
            if arr < 3:
                b3[arr, plane] = mix
            else:
                k3[plane] = mix

    def above(v_of, i):
        return v_of(i + 1) if i < 3 else jnp.where(group < 7, lane_next(v_of(0), 1), 0.0)

    def below(v_of, i):
        return v_of(i - 1) if i > 0 else jnp.where(group > 0, lane_prev(v_of(3), 1), 0.0)

    cx3, cy3, cz3, e3, w3 = (co3.at[n] for n in range(5))
    for i in range(4):
        cx, cy, cz, e, w = coefficients(
            k3[i], below(lambda q: k3[q], i), above(lambda q: k3[q], i), 1.0 / 64.0, 8, None
        )
        cx3[i] = cx
        cy3[i] = cy
        cz3[i] = cz
        e3[i] = e
        w3[i] = w
        for c in range(3):
            u3a[c, i] = w * b3[c, i]

    def coarse(src, dst):
        for i in range(4):
            u = [src[c, i] for c in range(3)]
            lo = [below(lambda q: src[c, q], i) for c in range(3)]
            hi = [above(lambda q: src[c, q], i) for c in range(3)]
            b = [b3[c, i] for c in range(3)]
            cz_lo = below(lambda q: cz3[q], i)
            rest = remainder(b, u, lo, hi, k3[i], cx3[i], cy3[i], cz3[i], cz_lo, e3[i], 8)
            for c in range(3):
                dst[c, i] = u[c] + w3[i] * rest[c]

    def two(t, carry):
        coarse(u3a, u3b)
        coarse(u3b, u3a)
        return carry

    lax.fori_loop(0, 3, two, 0)
    coarse(u3a, u3b)

    c2 = tuple(co2.at[n] for n in range(5))
    fill_coefficients(k2, c2, (1, 11), 0.0625, 4)
    c2[2][0] = (0.5 * 0.0625) * (k2[0] + k2[1])
    lane8 = lanes_of(8)
    lane12 = lanes_of(12)
    for q2 in range(12):
        zz = q2 % 4
        peer = d - 1 + q2 // 4
        inside = jnp.logical_and(peer >= 0, peer < SLAB)
        peer = jnp.clip(peer, 0, SLAB - 1)
        pick = jnp.logical_and((lane12 & 3) == zz, inside)
        for c in range(3):
            v = jnp.where(pick, received[peer, 24 + 12 * c : 36 + 12 * c], 0.0)
            u2a[c, q2, 4:16] = spread(v, lane12, 4)
            u2a[c, q2, 0:4] = jnp.zeros((4, 128), F32)
    for t in range(6):
        z = 2 * d - 2 + t
        i = (z + 32) & 3
        j = z >> 2
        for c in range(3):
            v = jnp.where((lane8 & 7) == j, u3b[c, i, 8:16], 0.0)
            double_rows(spread(v, lane8, 8), tmp)
            for q2 in (2 * t, 2 * t + 1):
                u2a[c, q2] = u2a[c, q2] + tmp[0:16]
    sweep((1, 11), b2, u2a, u2b, k2, c2, 4)
    sweep((2, 10), b2, u2b, u2a, k2, c2, 4)

    c1 = tuple(co1.at[n] for n in range(5))

    def fill(p, carry):
        for ref, v in zip(c1, coefficients(k1[p], k1[p], k1[p + 1], 0.25, 2, None, t1[p])):
            ref[p] = v
        return carry

    lax.fori_loop(4, 20, fill, 0)
    for q2 in range(2, 10):
        for c in range(3):
            double_rows(u2a[c, q2], tmp)
            more = tmp[8:32]
            for p in (2 * q2, 2 * q2 + 1):
                u1a[c, p] = u1[c, p] + more
    sweep((5, 19), b1, u1a, u1b, k1, c1, 2)
    sweep((6, 18), b1, u1b, u1a, k1, c1, 2)

    c0 = tuple(co0.at[n] for n in range(5))
    fill_coefficients(k0, c0, (2, 24), 1.0, 1, m0)
    for p1 in range(6, 18):
        for c in range(3):
            double_rows(u1a[c, p1], tmp)
            more = tmp[8:40]
            for p in (2 * p1 - 11, 2 * p1 - 10):
                if 2 <= p < 24:
                    u0a[c, p] = u0[c, p] + m0[p] * more
    sweep((3, 23), b0, u0a, u0b, k0, c0, 1)
    sweep((4, 22), b0, u0b, u0a, k0, c0, 1)

    def last(z, carry):
        p = z + 5
        u, rest = left_over(p, b0, u0a, k0, c0, 1)
        for c in range(3):
            field[c, z] = u[c][8:24]
            residual[c, z] = (m0[p] * rest[c])[8:24]
        return carry

    lax.fori_loop(0, 16, last, 0)


def struct(*shape):
    return jax.ShapeDtypeStruct(shape, F32)


def call(kernel, name, outs, scratch, *args, smem=0):
    vmem = pl.BlockSpec(memory_space=pltpu.VMEM)
    return pl.pallas_call(
        kernel,
        name=name,
        out_shape=outs,
        in_specs=[pl.BlockSpec(memory_space=pltpu.SMEM)] * smem + [vmem] * (len(args) - smem),
        out_specs=jax.tree.map(lambda _: vmem, outs),
        scratch_shapes=[pltpu.VMEM(s, F32) for s in scratch],
        compiler_params=pltpu.CompilerParams(vmem_limit_bytes=40 * 1024 * 1024),
    )(*args)


def shift(block, axis, count, by):
    pairs = [(i, i + by) for i in range(count) if 0 <= i + by < count]
    return lax.ppermute(block, axis, pairs)


def on_device(load, density, moduli, fixed):
    place = jnp.stack([lax.axis_index("slab"), lax.axis_index("col")]).astype(jnp.int32)
    k, m, low, high = call(
        prep_kernel, "prep",
        (struct(16, 16, 128), struct(16, 16, 128), struct(16, 24, 128), struct(16, 24, 128)),
        [], moduli, load, density, fixed, smem=1,
    )
    y_low = shift(high, "col", COL, 1)
    y_high = shift(low, "col", COL, -1)
    low, high = call(
        planes_kernel, "planes", (struct(544, 128), struct(544, 128)), [], load, k, m, y_low, y_high
    )
    z_low = shift(high, "slab", SLAB, 1)
    z_high = shift(low, "slab", SLAB, -1)
    full0, full0v = (26, 32, 128), (3, 26, 32, 128)
    b0, u0, k0, m0, message = call(
        fine_kernel, "fine",
        (struct(*full0v), struct(*full0v), struct(*full0), struct(*full0), struct(3, 8, 8, 128)),
        [full0] * 5 + [full0v, (10, 16, 128), (32, 128)],
        load, k, m, y_low, y_high, z_low, z_high,
    )
    y_low = shift(message, "col", COL, 1)
    y_high = shift(message, "col", COL, -1)
    wide = jnp.concatenate([y_low, message, y_high], axis=2)
    z_low = shift(wide, "slab", SLAB, 1)
    z_high = shift(wide, "slab", SLAB, -1)
    full1, full1v = (24, 24, 128), (3, 24, 24, 128)
    full2, full2v = (12, 16, 128), (3, 12, 16, 128)
    b1, u1, k1, t1, b2, k2, packed = call(
        middle_kernel, "middle",
        (struct(*full1v), struct(*full1v), struct(*full1), struct(*full1), struct(*full2v), struct(*full2),
         struct(16, 128)),
        [full1] * 5 + [full1v, full1v] + [full2] * 5 + [full2v, full2v, (32, 128)],
        place, z_low, wide, z_high, smem=1,
    )
    received = lax.all_to_all(jnp.broadcast_to(packed, (COL, 16, 128)), "col", 0, 0)
    window = call(window_kernel, "window", struct(SLAB, 64, 128), [(64, 128)], place, received, smem=1)
    received = lax.all_to_all(window, "slab", 0, 0)
    full3, full3v = (4, 24, 128), (3, 4, 24, 128)
    return call(
        upper_kernel, "upper",
        (struct(3, 16, 16, 128), struct(3, 16, 16, 128)),
        [full3v, full3, (5,) + full3, full3v, full3v, (5,) + full2, full2v, full2v,
         (5,) + full1, full1v, full1v, (5,) + full0, full0v, full0v, (48, 128)],
        place, received, b2, k2, b1, u1, k1, t1, b0, u0, k0, m0, smem=1,
    )


def solution(mesh):
    placed = (P(None, "slab", "col", None), P("slab", "col", None), P(), P("slab", "col", None))
    return jax.shard_map(
        on_device,
        mesh=mesh,
        in_specs=placed,
        out_specs=(P(None, "slab", "col", None), P(None, "slab", "col", None)),
        check_vma=False,
    )
```

time: 505 us -> 139 us (0.28)
  the two profiles are of different devices: /device:TPU:38 before, /device:TPU:1 now
where the time goes in v1:
time: 139 us; the launch traced here: 138 us
  blocking collectives  50.7 us (36%)
  Pallas kernels  36.2 us (26%)
  starting transfers between devices  24.8 us (18%)
  waiting for transfers between devices  21.1 us (15%)
  local copies, waits for them, and re-layouts  4.5 us (3%)
    pallas_call x6, Pallas kernels, call(): pl.pallas_call(kernel, name=name, out_shape=outs, in_specs=[pl.BlockSpec(...  36.2 us
    all_to_all x1, blocking collectives, on_device(): received = lax.all_to_all(window, 'slab', 0, 0)  30.1 us
    ppermute x8, starting transfers between devices, shift(): return lax.ppermute(block, axis, pairs)  24.8 us
    ppermute x8, waiting for transfers between devices, shift(): return lax.ppermute(block, axis, pairs)  21.1 us
    all_to_all x1, blocking collectives, on_device(): lax.all_to_all(jnp.broadcast_to(packed, (COL, 16, 128)), 'col', 0, 0)  20.6 us
    unnamed x16, local copies, waits for them, and re-layouts  4.47 us
  transfers between devices with their start and end apart: 8, of which 8 were waited for; matrix products, arithmetic and copies ran while one was open for 0% of the time, Pallas kernels for 0%

profile of v1, /device:TPU:1, one launch (start us, length us, event | category | flops | bytes accessed | tf_op | source)
XLA Modules:
  0.0 138.2 jit_solution(15674151491840231591)
XLA Ops:
  0.6 0.0 copy-start
  0.6 1.0 copy-done
  1.6 0.0 copy-start.4
  1.6 0.9 copy-done.4
  2.5 0.0 copy-start.5
  2.5 0.9 copy-done.5
  3.4 0.0 copy-start.6
  3.4 0.7 copy-done.6
  4.1 0.6 prep.1
  4.7 4.8 %collective-permute-start = (f32[16,24,128]{2,1,0:T(8,128)S(1)}, f32[16,24,128]{2,1,0:T(8,128)S(1)}, u32[]{:S(2)}, u32[]{:S(2)}) collective-permute-start(f32[16,24,128]{2,1,0:T(8,128)S(1)} %get-tuple-element.22), channel_id=1, source_target_pairs={{0,1},{1,2},{2,3},{3,4},{4,5},{5,6},{6,7},{7,8},{8,9},{9,10},{10,1... | collective-permute-start | bytes 589832 | tf_op jit(solution)/shard_map/ppermute | solution.py:450
  9.6 1.3 collective-permute-start.1
  10.9 1.3 collective-permute-done.from_low.y_low
  12.2 4.5 %collective-permute-done.1.from_high.y_high = f32[16,24,128]{2,1,0:T(8,128)S(1)} collective-permute-done((f32[16,24,128]{2,1,0:T(8,128)S(1)}, f32[16,24,128]{2,1,0:T(8,128)S(1)}, u32[]{:S(2)}, u32[]{:S(2)}) %collective-permute-start.1) | collective-permute-done | bytes 196640 | tf_op jit(solution)/shard_map/ppermute | solution.py:450
  16.6 0.0 copy-start.1
  16.6 1.0 copy-done.1
  17.7 5.9 %collective-permute-start.2 = (f32[544,128]{1,0:T(8,128)S(1)}, f32[544,128]{1,0:T(8,128)S(1)}, u32[]{:S(2)}, u32[]{:S(2)}) collective-permute-start(f32[544,128]{1,0:T(8,128)S(1)} %get-tuple-element.24), channel_id=1, source_target_pairs={{0,32},{32,64},{64,96},{96,128},{128,160},{160,192},{192,224},{224... | collective-permute-start | bytes 835592 | tf_op jit(solution)/shard_map/ppermute | solution.py:450
  23.6 1.9 %collective-permute-start.3 = (f32[544,128]{1,0:T(8,128)S(1)}, f32[544,128]{1,0:T(8,128)S(1)}, u32[]{:S(2)}, u32[]{:S(2)}) collective-permute-start(f32[544,128]{1,0:T(8,128)S(1)} %get-tuple-element.25), channel_id=1, source_target_pairs={{32,0},{64,32},{96,64},{128,96},{160,128},{192,160},{224,192},{256... | collective-permute-start | bytes 835592 | tf_op jit(solution)/shard_map/ppermute | solution.py:450
  25.5 1.5 %collective-permute-done.2.z_low = f32[544,128]{1,0:T(8,128)S(1)} collective-permute-done((f32[544,128]{1,0:T(8,128)S(1)}, f32[544,128]{1,0:T(8,128)S(1)}, u32[]{:S(2)}, u32[]{:S(2)}) %collective-permute-start.2) | collective-permute-done | bytes 278560 | tf_op jit(solution)/shard_map/ppermute | solution.py:450
  27.0 4.4 %collective-permute-done.3.z_high = f32[544,128]{1,0:T(8,128)S(1)} collective-permute-done((f32[544,128]{1,0:T(8,128)S(1)}, f32[544,128]{1,0:T(8,128)S(1)}, u32[]{:S(2)}, u32[]{:S(2)}) %collective-permute-start.3) | collective-permute-done | bytes 278560 | tf_op jit(solution)/shard_map/ppermute | solution.py:450
  31.4 6.4 %fine.1 = (f32[3,26,32,128]{3,2,1,0:T(8,128)S(1)}, f32[3,26,32,128]{3,2,1,0:T(8,128)S(1)}, f32[26,32,128]{2,1,0:T(8,128)S(1)}, f32[26,32,128]{2,1,0:T(8,128)S(1)}, f32[3,8,8,128]{3,2,1,0:T(8,128)S(1)}) custom-call(f32[3,16,16,128]{3,2,1,0:T(8,128)S(1)} %copy-done.1, f32[16,16,128]{2,1,0:T(8,128)S(1)} %get-tuple-element.20.k.k_own, ...), custom_call_target="tpu_custom_call" | custom-call | tf_op jit(solution)/shard_map/fine/pallas_call | solution.py:437
  37.9 0.0 copy-start.2
  37.9 4.0 %collective-permute-start.4 = (f32[3,8,8,128]{3,2,1,0:T(8,128)S(1)}, f32[3,8,8,128]{3,2,1,0:T(8,128)S(1)}, u32[]{:S(2)}, u32[]{:S(2)}) collective-permute-start(f32[3,8,8,128]{3,2,1,0:T(8,128)S(1)} %get-tuple-element.26), channel_id=1, source_target_pairs={{0,1},{1,2},{2,3},{3,4},{4,5},{5,6},{6,7},{7,8},{8,9},{9,10},{10,1... | collective-permute-start | bytes 294920 | tf_op jit(solution)/shard_map/ppermute | solution.py:450
  41.9 1.3 collective-permute-start.5
  43.2 0.3 collective-permute-done.4
  43.5 5.6 %collective-permute-done.5 = f32[3,8,8,128]{3,2,1,0:T(8,128)S(1)} collective-permute-done((f32[3,8,8,128]{3,2,1,0:T(8,128)S(1)}, f32[3,8,8,128]{3,2,1,0:T(8,128)S(1)}, u32[]{:S(2)}, u32[]{:S(2)}) %collective-permute-start.5) | collective-permute-done | bytes 98336 | tf_op jit(solution)/shard_map/ppermute | solution.py:450
  49.1 0.0 copy-done.2
  49.1 1.9 %collective-permute-start.7 = (f32[3,8,24,128]{3,2,1,0:T(8,128)S(1)}, f32[3,8,24,128]{3,2,1,0:T(8,128)}, u32[]{:S(2)}, u32[]{:S(2)}) collective-permute-start(f32[3,8,24,128]{3,2,1,0:T(8,128)S(1)} %constant_dynamic-update-slice_fusion.z_mid), channel_id=1, source_target_pairs={{32,0},{64,32},{96,64},{128,96},{160,128},{192,160},{224,192},{256... | collective-permute-start | bytes 884744 | tf_op jit(solution)/shard_map/ppermute | solution.py:450
  51.1 3.6 %collective-permute-start.6 = (f32[3,8,24,128]{3,2,1,0:T(8,128)S(1)}, f32[3,8,24,128]{3,2,1,0:T(8,128)}, u32[]{:S(2)}, u32[]{:S(2)}) collective-permute-start(f32[3,8,24,128]{3,2,1,0:T(8,128)S(1)} %constant_dynamic-update-slice_fusion.z_mid), channel_id=1, source_target_pairs={{0,32},{32,64},{64,96},{96,128},{128,160},{160,192},{192,224},{224... | collective-permute-start | bytes 884744 | tf_op jit(solution)/shard_map/ppermute | solution.py:450
  54.7 0.1 pad_add_fusion.place
  54.8 2.5 %collective-permute-done.7.z_high = f32[3,8,24,128]{3,2,1,0:T(8,128)} collective-permute-done((f32[3,8,24,128]{3,2,1,0:T(8,128)S(1)}, f32[3,8,24,128]{3,2,1,0:T(8,128)}, u32[]{:S(2)}, u32[]{:S(2)}) %collective-permute-start.7) | collective-permute-done | bytes 294944 | tf_op jit(solution)/shard_map/ppermute | solution.py:450
  57.3 1.1 collective-permute-done.6.z_low
  58.4 9.1 %middle.1 = (f32[3,24,24,128]{3,2,1,0:T(8,128)S(1)}, f32[3,24,24,128]{3,2,1,0:T(8,128)S(1)}, f32[24,24,128]{2,1,0:T(8,128)S(1)}, f32[24,24,128]{2,1,0:T(8,128)S(...) custom-call(s32[2]{0:T(128)S(1)} %pad_add_fusion.place, ...), custom_call_target="tpu_custom_call" | custom-call | tf_op jit(solution)/shard_map/middle/pallas_call | solution.py:437
  67.4 0.0 copy-start.3
  67.5 20.6 %all_to_all.10.received = f32[32,16,128]{2,1,0:T(8,128)S(1)} all-to-all(f32[32,16,128]{2,1,0:T(8,128)S(1)} %broadcast_in_dim.3), channel_id=1, replica_groups=mesh['slab'=16,'col'=32] {'col'}, dimensions={0} | all-to-all | bytes 524288 | tf_op jit(solution)/shard_map/all_to_all | solution.py:488
  88.1 0.6 window.1
  88.7 30.1 %all_to_all.11.received = f32[16,64,128]{2,1,0:T(8,128)S(1)} all-to-all(f32[16,64,128]{2,1,0:T(8,128)S(1)} %window.1), channel_id=1, replica_groups=mesh['slab'=16,'col'=32] {'slab'}, dimensions={0} | all-to-all | bytes 1048576 | tf_op jit(solution)/shard_map/all_to_all | solution.py:490
  118.8 0.0 copy-done.3
  118.8 19.4 %upper.1 = (f32[3,16,16,128]{3,2,1,0:T(8,128)}, f32[3,16,16,128]{3,2,1,0:T(8,128)}) custom-call(s32[2]{0:T(128)S(1)} %pad_add_fusion.place, f32[16,64,128]{2,1,0:T(8,128)S(1)} %all_to_all.11.received, f32[3,12,16,128]{3,2,1,0:T(8,128)S(1)} %get-tuple-element.28.b2, f32[12,16,128]{2,1,0:T(8,128)S(1)} %get-tuple-element.29.k2, ...), custom_call_target="tpu_custom_call" | custom-call | tf_op jit(solution)/shard_map/upper/pallas_call | solution.py:437
  (5 shorter events, 0.1 us)
Async XLA Ops:
  0.6 1.0 copy-start
  1.6 0.9 copy-start.4
  2.5 0.9 copy-start.5
  3.4 0.7 copy-start.6
  4.7 7.4 %collective-permute-start = (f32[16,24,128]{2,1,0:T(8,128)S(1)}, f32[16,24,128]{2,1,0:T(8,128)S(1)}, u32[]{:S(2)}, u32[]{:S(2)}) collective-permute-start(f32[16,24,128]{2,1,0:T(8,128)S(1)} %get-tuple-element.22), channel_id=1, source_target_pairs={{0,1},{1,2},{2,3},{3,4},{4,5},{5,6},{6,7},{7,8},{8,9},{9,10},{10,1... | collective-permute-start | bytes 589832 | tf_op jit(solution)/shard_map/ppermute | solution.py:450
  9.6 7.0 %collective-permute-start.1 = (f32[16,24,128]{2,1,0:T(8,128)S(1)}, f32[16,24,128]{2,1,0:T(8,128)S(1)}, u32[]{:S(2)}, u32[]{:S(2)}) collective-permute-start(f32[16,24,128]{2,1,0:T(8,128)S(1)} %get-tuple-element.23), channel_id=1, source_target_pairs={{1,0},{2,1},{3,2},{4,3},{5,4},{6,5},{7,6},{8,7},{9,8},{10,9},{11,1... | collective-permute-start | bytes 589832 | tf_op jit(solution)/shard_map/ppermute | solution.py:450
  16.6 1.0 copy-start.1
  17.7 9.4 %collective-permute-start.2 = (f32[544,128]{1,0:T(8,128)S(1)}, f32[544,128]{1,0:T(8,128)S(1)}, u32[]{:S(2)}, u32[]{:S(2)}) collective-permute-start(f32[544,128]{1,0:T(8,128)S(1)} %get-tuple-element.24), channel_id=1, source_target_pairs={{0,32},{32,64},{64,96},{96,128},{128,160},{160,192},{192,224},{224... | collective-permute-start | bytes 835592 | tf_op jit(solution)/shard_map/ppermute | solution.py:450
  23.6 7.9 %collective-permute-start.3 = (f32[544,128]{1,0:T(8,128)S(1)}, f32[544,128]{1,0:T(8,128)S(1)}, u32[]{:S(2)}, u32[]{:S(2)}) collective-permute-start(f32[544,128]{1,0:T(8,128)S(1)} %get-tuple-element.25), channel_id=1, source_target_pairs={{32,0},{64,32},{96,64},{128,96},{160,128},{192,160},{224,192},{256... | collective-permute-start | bytes 835592 | tf_op jit(solution)/shard_map/ppermute | solution.py:450
  37.9 11.2 %copy-start.2 = (f32[26,32,128]{2,1,0:T(8,128)}, f32[26,32,128]{2,1,0:T(8,128)S(1)}, u32[]{:S(2)}) copy-start(f32[26,32,128]{2,1,0:T(8,128)S(1)} %get-tuple-element.37.m0) | copy-start | bytes 1277956
  37.9 5.6 %collective-permute-start.4 = (f32[3,8,8,128]{3,2,1,0:T(8,128)S(1)}, f32[3,8,8,128]{3,2,1,0:T(8,128)S(1)}, u32[]{:S(2)}, u32[]{:S(2)}) collective-permute-start(f32[3,8,8,128]{3,2,1,0:T(8,128)S(1)} %get-tuple-element.26), channel_id=1, source_target_pairs={{0,1},{1,2},{2,3},{3,4},{4,5},{5,6},{6,7},{7,8},{8,9},{9,10},{10,1... | collective-permute-start | bytes 294920 | tf_op jit(solution)/shard_map/ppermute | solution.py:450
  41.9 7.2 %collective-permute-start.5 = (f32[3,8,8,128]{3,2,1,0:T(8,128)S(1)}, f32[3,8,8,128]{3,2,1,0:T(8,128)S(1)}, u32[]{:S(2)}, u32[]{:S(2)}) collective-permute-start(f32[3,8,8,128]{3,2,1,0:T(8,128)S(1)} %get-tuple-element.26), channel_id=1, source_target_pairs={{1,0},{2,1},{3,2},{4,3},{5,4},{6,5},{7,6},{8,7},{9,8},{10,9},{11,1... | collective-permute-start | bytes 294920 | tf_op jit(solution)/shard_map/ppermute | solution.py:450
  49.1 8.1 %collective-permute-start.7 = (f32[3,8,24,128]{3,2,1,0:T(8,128)S(1)}, f32[3,8,24,128]{3,2,1,0:T(8,128)}, u32[]{:S(2)}, u32[]{:S(2)}) collective-permute-start(f32[3,8,24,128]{3,2,1,0:T(8,128)S(1)} %constant_dynamic-update-slice_fusion.z_mid), channel_id=1, source_target_pairs={{32,0},{64,32},{96,64},{128,96},{160,128},{192,160},{224,192},{256... | collective-permute-start | bytes 884744 | tf_op jit(solution)/shard_map/ppermute | solution.py:450
  51.1 7.3 %collective-permute-start.6 = (f32[3,8,24,128]{3,2,1,0:T(8,128)S(1)}, f32[3,8,24,128]{3,2,1,0:T(8,128)}, u32[]{:S(2)}, u32[]{:S(2)}) collective-permute-start(f32[3,8,24,128]{3,2,1,0:T(8,128)S(1)} %constant_dynamic-update-slice_fusion.z_mid), channel_id=1, source_target_pairs={{0,32},{32,64},{64,96},{96,128},{128,160},{160,192},{192,224},{224... | collective-permute-start | bytes 884744 | tf_op jit(solution)/shard_map/ppermute | solution.py:450
  67.4 51.4 %copy-start.3 = (f32[26,32,128]{2,1,0:T(8,128)S(1)}, f32[26,32,128]{2,1,0:T(8,128)}, u32[]{:S(2)}) copy-start(f32[26,32,128]{2,1,0:T(8,128)} %copy-done.2) | copy-start | bytes 1277956

commit v2 on v1

v2 whole, which is shorter than its diff:
```python
import jax
import jax.numpy as jnp
from jax import lax
from jax.experimental import pallas as pl
from jax.experimental.pallas import tpu as pltpu
from jax.sharding import PartitionSpec as P

CLASSES = 8
OMEGA = 0.6
COUPLE = 0.05
SLAB = 16
COL = 32
F32 = jnp.float32

UNROLL = 8


def each(planes, body, unroll=None):
    unroll = unroll or UNROLL
    low, high = planes
    rounds = (high - low) // unroll
    if rounds > 1:
        def chunk(t, carry):
            for q in range(unroll):
                body(low + t * unroll + q)
            return carry

        lax.fori_loop(0, rounds, chunk, 0)
        low += rounds * unroll
    for p in range(low, high):
        body(p)


def lanes_of(rows):
    return lax.broadcasted_iota(jnp.int32, (rows, 128), 1)


def lane_next(v, step):
    return pltpu.roll(v, 128 - step, 1)


def lane_prev(v, step):
    return pltpu.roll(v, step, 1)


def row_next(v):
    return pltpu.roll(v, v.shape[0] - 1, 0)


def row_prev(v):
    return pltpu.roll(v, 1, 0)


def spread(v, lane, width):
    step = 1
    while step < width:
        v = v + jnp.where((lane & step) != 0, lane_prev(v, step), lane_next(v, step))
        step *= 2
    return v


def coefficients(k, k_lo, k_hi, scale, step, mask, total=None):
    lane = lanes_of(k.shape[0])
    half = 0.5 * scale
    k_next = lane_next(k, step)
    cx = jnp.where(lane < 128 - step, half * (k + k_next), 0.0)
    ky = row_next(k)
    cy = half * (k + ky)
    cz = half * (k + k_hi)
    if total is None:
        sides = jnp.where(lane < 128 - step, k_next, 0.0) + jnp.where(lane >= step, lane_prev(k, step), 0.0)
        total = half * (6.0 * k + sides + ky + row_prev(k) + k_lo + k_hi)
    diag = total + 2.0 * COUPLE * k
    top = OMEGA if mask is None else OMEGA * mask
    weight = jnp.where(k > 0.0, top / diag, 0.0)
    return cx, cy, cz, total + COUPLE * k, weight


def remainder(b, u, u_lo, u_hi, k, cx, cy, cz, cz_lo, e, step):
    cx_lo = lane_prev(cx, step)
    cy_lo = row_prev(cy)
    shared = COUPLE * k * (u[0] + u[1] + u[2])
    out = []
    for c in range(3):
        v = u[c]
        around = cx * lane_next(v, step) + cx_lo * lane_prev(v, step)
        around = around + cy * row_next(v) + cy_lo * row_prev(v)
        around = around + cz * u_hi[c] + cz_lo * u_lo[c]
        out.append((b[c] - shared) + (around - e * v))
    return out


def fill_coefficients(k_ref, co, planes, scale, step, total_ref=None):
    def body(p):
        total = None if total_ref is None else total_ref[p]
        values = coefficients(k_ref[p], k_ref[p - 1], k_ref[p + 1], scale, step, None, total)
        for ref, v in zip(co, values):
            ref[p] = v

    each(planes, body)


def fine_coefficients(k_ref, m_ref, co, planes):
    def body(p):
        k = k_ref[p, 4:28]
        k_lo, k_hi = k_ref[p - 1, 4:28], k_ref[p + 1, 4:28]
        ky, ky_lo = k_ref[p, 5:29], k_ref[p, 3:27]
        lane = lanes_of(24)
        k_next = jnp.where(lane < 127, lane_next(k, 1), 0.0)
        k_prev = jnp.where(lane >= 1, lane_prev(k, 1), 0.0)
        total = 0.5 * (6.0 * k + k_next + k_prev + ky + ky_lo + k_lo + k_hi)
        values = (
            jnp.where(lane < 127, 0.5 * (k + k_next), 0.0), 0.5 * (k + ky), 0.5 * (k + k_hi),
            total + COUPLE * k,
            jnp.where(k > 0.0, OMEGA * m_ref[p] / (total + 2.0 * COUPLE * k), 0.0),
        )
        for ref, v in zip(co, values):
            ref[p] = v

    each(planes, body)


def left_over(p, b_ref, u_ref, k_ref, co, step, rows=slice(None)):
    cx_ref, cy_ref, cz_ref, e_ref, _ = co
    b = [b_ref[c, p] for c in range(3)]
    u = [u_ref[c, p] for c in range(3)]
    lo = [u_ref[c, p - 1] for c in range(3)]
    hi = [u_ref[c, p + 1] for c in range(3)]
    k = k_ref[p, rows]
    return u, remainder(b, u, lo, hi, k, cx_ref[p], cy_ref[p], cz_ref[p], cz_ref[p - 1], e_ref[p], step)


def sweep(planes, b_ref, u_ref, new_ref, k_ref, co, step, rows=slice(None)):
    def body(p):
        u, rest = left_over(p, b_ref, u_ref, k_ref, co, step, rows)
        w = co[4][p]
        for c in range(3):
            new_ref[c, p] = u[c] + w * rest[c]

    each(planes, body)


def first_sweep(planes, b_ref, new_ref, w_ref):
    def body(p):
        w = w_ref[p]
        for c in range(3):
            new_ref[c, p] = w * b_ref[c, p]

    each(planes, body)


def block_mean(a, b, tmp, step):
    lane = lanes_of(a.shape[0])
    s = a + b
    s = s + jnp.where((lane & step) != 0, lane_prev(s, step), lane_next(s, step))
    n = a.shape[0]
    tmp[0:n] = s
    return 0.125 * (tmp[pl.ds(0, n // 2, stride=2)] + tmp[pl.ds(1, n // 2, stride=2)])


def double_rows(v, tmp):
    n = v.shape[0]
    tmp[pl.ds(0, n, stride=2)] = v
    tmp[pl.ds(1, n, stride=2)] = v


FINE = slice(4, 28)


def prep_kernel(moduli_in, load_in, density_in, fixed_in, load, k_out, m_out, low, high, moduli, density, fixed, sems):
    copies = [
        pltpu.make_async_copy(src, dst, sems.at[n])
        for n, (src, dst) in enumerate(
            ((moduli_in, moduli), (density_in, density), (fixed_in, fixed), (load_in, load))
        )
    ]
    for copy in copies:
        copy.start()
    for copy in copies[:3]:
        copy.wait()
    for z in range(16):
        d = density[z]
        k = jnp.zeros((16, 128), F32)
        for klass in range(CLASSES):
            k = jnp.where(d == klass, moduli[klass], k)
        m = 1.0 - fixed[z].astype(F32)
        k_out[z] = k
        m_out[z] = m
        low[z, 12:16] = m[0:4]
        high[z, 12:16] = m[12:16]
        low[z, 16:24] = k[0:8]
        high[z, 16:24] = k[8:16]
    copies[3].wait()
    for z in range(16):
        for c in range(3):
            low[z, 4 * c : 4 * c + 4] = load[c, z, 0:4]
            high[z, 4 * c : 4 * c + 4] = load[c, z, 12:16]


def planes_kernel(place, load, k, m, from_low, from_high, partner, cross):
    odd = place[0] & 1
    for out, start, k_start in (
        (partner, 12 * (1 - odd), 11 * (1 - odd)), (cross, 12 * odd, 11 * odd),
    ):
        for q in range(4):
            z = start + q
            for a in range(4):
                base = 24 * (4 * a + q)
                own = load[a, z] if a < 3 else m[z]
                out[base : base + 4] = from_low[z, 4 * a : 4 * a + 4]
                out[base + 4 : base + 20] = own
                out[base + 20 : base + 24] = from_high[z, 4 * a : 4 * a + 4]
        for q in range(5):
            z = k_start + q
            base = 384 + 32 * q
            out[base : base + 8] = from_low[z, 16:24]
            out[base + 8 : base + 24] = k[z]
            out[base + 24 : base + 32] = from_high[z, 16:24]


def fine_kernel(place, load, k_own, m_own, y_low, y_high, partner, cross,
                b, u, k, m, message,
                cx, cy, cz, e, w, first, k1, tmp):
    co = (cx, cy, cz, e, w)
    odd = place[0] & 1
    for z in range(16):
        p = z + 5
        for c in range(3):
            b[c, p, 0:4] = y_low[z, 4 * c : 4 * c + 4]
            b[c, p, 4:20] = load[c, z]
            b[c, p, 20:24] = y_high[z, 4 * c : 4 * c + 4]
        m[p, 0:4] = y_low[z, 12:16]
        m[p, 4:20] = m_own[z]
        m[p, 20:24] = y_high[z, 12:16]
        k[p, 0:8] = y_low[z, 16:24]
        k[p, 8:24] = k_own[z]
        k[p, 24:32] = y_high[z, 16:24]
    for src, high in ((partner.at[1 - odd], 1 - odd), (cross, odd)):
        start, k_start = 1 + 20 * high, 21 * high
        for q in range(4):
            for a in range(4):
                part = src[24 * (4 * a + q) : 24 * (4 * a + q) + 24]
                if a < 3:
                    b[a, start + q] = part
                else:
                    m[start + q] = part
        for q in range(5):
            k[k_start + q] = src[384 + 32 * q : 416 + 32 * q]
    fine_coefficients(k, m, co, (1, 25))
    first_sweep((1, 25), b, first, w)
    sweep((2, 24), b, first, u, k, co, 1, FINE)

    for z1 in range(-1, 9):
        p = 2 * z1 + 5
        k1[z1 + 1] = block_mean(k[p], k[p + 1], tmp.at[(z1 + 1) % 4], 1)
    lane = lanes_of(8)
    odd_lane = (lane & 1) != 0
    lane = lanes_of(16)
    for z1 in range(8):
        p = 2 * z1 + 5
        rests = [left_over(q, b, u, k, co, 1, FINE)[1] for q in (p, p + 1)]
        parts = [
            block_mean(m[p] * rests[0][c], m[p + 1] * rests[1][c], tmp.at[c], 1)[2:10] for c in range(3)
        ]
        centre = k1[z1 + 1]
        sides = jnp.where(lane < 126, lane_next(centre, 2), 0.0) + jnp.where(lane >= 2, lane_prev(centre, 2), 0.0)
        total = 0.125 * (6.0 * centre + sides + row_next(centre) + row_prev(centre) + k1[z1] + k1[z1 + 2])
        message[0, z1] = jnp.where(odd_lane, parts[1], parts[0])
        message[1, z1] = jnp.where(odd_lane, centre[4:12], parts[2])
        message[2, z1] = total[4:12]


def middle_kernel(place, own, partner, cross,
                  b1_out, u1_out, k1_out, t1_out, b2, k2, u2b, packed,
                  b1, u1, k1, t1, cx, cy, cz, e, w, first, cx2, cy2, cz2, e2, w2, u2a, tmp):
    co = (cx, cy, cz, e, w)
    lane = lanes_of(24)
    odd_lane = (lane & 1) != 0
    odd = place[0] & 1
    for src, start in ((own, 8), (partner.at[1 - odd], 16 * (1 - odd)), (cross, 16 * odd)):
        for q in range(8):
            p = start + q
            v = src[0, q]
            b1[0, p] = jnp.where(odd_lane, lane_prev(v, 1), v)
            b1[1, p] = jnp.where(odd_lane, v, lane_next(v, 1))
            v = src[1, q]
            b1[2, p] = jnp.where(odd_lane, lane_prev(v, 1), v)
            k1[p] = jnp.where(odd_lane, v, lane_next(v, 1))
            t1[p] = src[2, q]
    k1[24] = jnp.zeros((24, 128), F32)

    def fill(p):
        for ref, v in zip(co, coefficients(k1[p], None, k1[p + 1], 0.25, 2, None, t1[p])):
            ref[p] = v
        for c in range(3):
            first[c, p] = w[p] * b1[c, p]

    each((0, 24), fill)
    sweep((1, 23), b1, first, u1, k1, co, 2)
    for p in range(16):
        k1_out[p] = k1[p + 4, 4:20]
        t1_out[p] = t1[p + 4, 4:20]
        for c in range(3):
            b1_out[c, p] = b1[c, p + 4, 4:20]
            u1_out[c, p] = u1[c, p + 4, 4:20]
    for q2 in range(12):
        k2[q2, 4:16] = block_mean(k1[2 * q2], k1[2 * q2 + 1], tmp.at[q2 % 4], 2)
        k2[q2, 0:4] = jnp.zeros((4, 128), F32)
    for q2 in range(1, 11):
        rests = [left_over(p, b1, u1, k1, co, 2)[1] for p in (2 * q2, 2 * q2 + 1)]
        for c in range(3):
            b2[c, q2, 4:16] = block_mean(rests[0][c], rests[1][c], tmp.at[c], 2)
            b2[c, q2, 0:4] = jnp.zeros((4, 128), F32)
    co2 = (cx2, cy2, cz2, e2, w2)
    fill_coefficients(k2, co2, (1, 11), 0.0625, 4)
    first_sweep((1, 11), b2, u2a, w2)
    sweep((2, 10), b2, u2a, u2b, k2, co2, 4)
    j = place[0] // 2
    lane = lanes_of(8)
    group = lane & 7
    pack = jnp.zeros((8, 128), F32)
    for zz in range(2):
        rests = [left_over(p, b2, u2b, k2, co2, 4)[1] for p in (4 + 2 * zz, 5 + 2 * zz)]
        parts = [block_mean(rests[0][c], rests[1][c], tmp.at[c], 4) for c in range(3)]
        parts.append(block_mean(k2[4 + 2 * zz], k2[5 + 2 * zz], tmp.at[3], 4))
        for a in range(4):
            pack = jnp.where(group == ((j + 2 * a + zz) & 7), parts[a], pack)
    quad = lane & 3
    low, high = tmp.at[0], tmp.at[1]
    low[0:2] = pack[4:6]
    high[0:2] = pack[4:6]
    for c in range(3):
        v = u2b[c, 7, 8:16]
        for zz in (2, 1, 0):
            v = jnp.where(quad == zz, u2b[c, 4 + zz, 8:16], v)
        low[2 + 2 * c : 4 + 2 * c] = v[2:4]
        high[2 + 2 * c : 4 + 2 * c] = v[0:2]
    to_low, to_high = low[0:8], high[0:8]
    for peer in range(COL):
        packed[peer] = jnp.where(place[1] < peer, to_high, to_low)


def window_kernel(place, received, u2, out, tmp):
    c, d = place[1], place[0]
    for q in range(11):
        peer = c - 5 + q
        inside = jnp.logical_and(peer >= 0, peer < COL).astype(F32)
        tmp[2 * q : 2 * q + 2] = inside * received[jnp.clip(peer, 0, COL - 1), 0:2]
    for comp in range(3):
        for q, peer in ((0, c - 1), (1, c + 1)):
            inside = jnp.logical_and(peer >= 0, peer < COL).astype(F32)
            part = received[jnp.clip(peer, 0, COL - 1), 2 + 2 * comp : 4 + 2 * comp]
            base = 22 + 4 * comp + 2 * q
            tmp[base : base + 2] = inside * part
    quad = lanes_of(4) & 3
    tmp[46:48] = jnp.zeros((2, 128), F32)

    def inner(near):
        for comp in range(3):
            a = [u2[comp, 4 + near + f, 6:10] for f in range(2)]
            b = [u2[comp, 4 + near + f, 10:14] for f in range(2)]
            v = jnp.where(quad == 0, a[0], jnp.where(quad == 1, a[1], jnp.where(quad == 2, b[0], b[1])))
            tmp[34 + 4 * comp : 38 + 4 * comp] = v
        return tmp[...]

    to_high = inner(0)
    to_low = inner(2)
    for peer in range(SLAB):
        out[peer] = jnp.where(d < peer, to_high, to_low)


def upper_kernel(place, received, u2, b2, k2, b1, u1, k1, t1, b0, u0, k0, m0,
                 field, residual,
                 b3, k3, co3, u3a, u3b, co2, u2a, u2b, co1, u1a, u1b, co0, u0a, u0b, tmp):
    d = place[0]
    lane = lanes_of(24)
    group = lane & 7
    for a in range(2):
        for r in range(8):
            mix = jnp.zeros((24, 128), F32)
            for j in range(8):
                mix = jnp.where(group == ((j + r) & 7), received[2 * j + a, 0:24], mix)
            if r:
                mix = jnp.where(group < 8 - r, lane_next(mix, r), lane_prev(mix, 8 - r))
            arr, plane = r // 2, 2 * a + r % 2
            if arr < 3:
                b3[arr, plane] = mix
            else:
                k3[plane] = mix

    def above(v_of, i):
        return v_of(i + 1) if i < 3 else jnp.where(group < 7, lane_next(v_of(0), 1), 0.0)

    def below(v_of, i):
        return v_of(i - 1) if i > 0 else jnp.where(group > 0, lane_prev(v_of(3), 1), 0.0)

    cx3, cy3, cz3, e3, w3 = (co3.at[n] for n in range(5))
    for i in range(4):
        cx, cy, cz, e, w = coefficients(
            k3[i], below(lambda q: k3[q], i), above(lambda q: k3[q], i), 1.0 / 64.0, 8, None
        )
        cx3[i] = cx
        cy3[i] = cy
        cz3[i] = cz
        e3[i] = e
        w3[i] = w
        for c in range(3):
            u3a[c, i] = w * b3[c, i]

    def coarse(src, dst):
        for i in range(4):
            u = [src[c, i] for c in range(3)]
            lo = [below(lambda q: src[c, q], i) for c in range(3)]
            hi = [above(lambda q: src[c, q], i) for c in range(3)]
            b = [b3[c, i] for c in range(3)]
            cz_lo = below(lambda q: cz3[q], i)
            rest = remainder(b, u, lo, hi, k3[i], cx3[i], cy3[i], cz3[i], cz_lo, e3[i], 8)
            for c in range(3):
                dst[c, i] = u[c] + w3[i] * rest[c]

    def two(t, carry):
        coarse(u3a, u3b)
        coarse(u3b, u3a)
        return carry

    lax.fori_loop(0, 3, two, 0)
    coarse(u3a, u3b)

    c2 = tuple(co2.at[n] for n in range(5))
    fill_coefficients(k2, c2, (1, 11), 0.0625, 4)
    c2[2][0] = (0.5 * 0.0625) * (k2[0] + k2[1])
    lane8 = lanes_of(8)
    lane4 = lanes_of(4)
    for q2 in range(12):
        zz = q2 % 4
        peer = d - 1 + q2 // 4
        inside = jnp.logical_and(peer >= 0, peer < SLAB)
        peer = jnp.clip(peer, 0, SLAB - 1)
        far = q2 if q2 < 2 else q2 - 10 if q2 >= 10 else None
        for c in range(3):
            v = jnp.where(jnp.logical_and((lane4 & 3) == zz, inside), received[peer, 22 + 4 * c : 26 + 4 * c], 0.0)
            v = spread(v, lane4, 4)
            u2a[c, q2, 0:4] = jnp.zeros((4, 128), F32)
            u2a[c, q2, 4:6] = v[0:2]
            u2a[c, q2, 14:16] = v[2:4]
            if far is None:
                u2a[c, q2, 6:14] = u2[c, q2, 6:14]
            else:
                v = received[peer, 34 + 4 * c : 38 + 4 * c]
                for half in range(2):
                    pick = jnp.logical_and((lane4 & 3) == 2 * half + far, inside)
                    u2a[c, q2, 6 + 4 * half : 10 + 4 * half] = spread(jnp.where(pick, v, 0.0), lane4, 4)
    for t in range(6):
        z = 2 * d - 2 + t
        i = (z + 32) & 3
        j = z >> 2
        for c in range(3):
            v = jnp.where((lane8 & 7) == j, u3b[c, i, 8:16], 0.0)
            double_rows(spread(v, lane8, 8), tmp.at[c])
            for q2 in (2 * t, 2 * t + 1):
                u2a[c, q2, 4:16] = u2a[c, q2, 4:16] + tmp[c, 0:12]
    sweep((1, 11), b2, u2a, u2b, k2, c2, 4)
    sweep((2, 10), b2, u2b, u2a, k2, c2, 4)

    c1 = tuple(co1.at[n] for n in range(5))

    def fill(p):
        for ref, v in zip(c1, coefficients(k1[p], None, k1[p + 1], 0.25, 2, None, t1[p])):
            ref[p] = v

    each((0, 15), fill)
    for q2 in range(2, 10):
        for c in range(3):
            double_rows(u2a[c, q2, 6:14], tmp.at[c])
            more = tmp[c, 0:16]
            for p in (2 * q2 - 4, 2 * q2 - 3):
                u1a[c, p] = u1[c, p] + more
    sweep((1, 15), b1, u1a, u1b, k1, c1, 2)
    sweep((2, 14), b1, u1b, u1a, k1, c1, 2)

    c0 = tuple(co0.at[n] for n in range(5))
    fine_coefficients(k0, m0, c0, (2, 24))
    for p1 in range(2, 14):
        for c in range(3):
            double_rows(u1a[c, p1], tmp.at[c])
            more = tmp[c, 4:28]
            for p in (2 * p1 - 3, 2 * p1 - 2):
                if 2 <= p < 24:
                    u0a[c, p] = u0[c, p] + m0[p] * more
    sweep((3, 23), b0, u0a, u0b, k0, c0, 1, FINE)
    sweep((4, 22), b0, u0b, u0a, k0, c0, 1, FINE)

    def last(z):
        p = z + 5
        u, rest = left_over(p, b0, u0a, k0, c0, 1, FINE)
        for c in range(3):
            field[c, z] = u[c][4:20]
            residual[c, z] = (m0[p] * rest[c])[4:20]

    each((0, 16), last)


def struct(*shape):
    return jax.ShapeDtypeStruct(shape, F32)


def call(kernel, name, outs, scratch, *args, smem=0, hbm=0):
    vmem = pl.BlockSpec(memory_space=pltpu.VMEM)
    specs = [pl.BlockSpec(memory_space=pltpu.SMEM)] * smem + [pl.BlockSpec(memory_space=pltpu.HBM)] * hbm
    return pl.pallas_call(
        kernel,
        name=name,
        out_shape=outs,
        in_specs=specs + [vmem] * (len(args) - len(specs)),
        out_specs=jax.tree.map(lambda _: vmem, outs),
        scratch_shapes=[pltpu.VMEM(s, F32) if isinstance(s, tuple) else s for s in scratch],
        compiler_params=pltpu.CompilerParams(vmem_limit_bytes=40 * 1024 * 1024),
    )(*args)


def shift(block, axis, count, by):
    pairs = [(i, i + by) for i in range(count) if 0 <= i + by < count]
    return lax.ppermute(block, axis, pairs)


def slab_neighbours(to_partner, to_cross):
    pairs = []
    for i in range(1, SLAB - 1, 2):
        pairs += [(i, i + 1), (i + 1, i)]
    cross = lax.ppermute(to_cross, "slab", pairs)
    groups = [[i, i + 1] for i in range(0, SLAB, 2)]
    return lax.all_gather(to_partner, "slab", axis_index_groups=groups), cross


def on_device(load, density, moduli, fixed):
    place = jnp.stack([lax.axis_index("slab"), lax.axis_index("col")]).astype(jnp.int32)
    own = struct(16, 16, 128)
    whole_int = pltpu.VMEM((16, 16, 128), jnp.int32)
    load, k, m, low, high = call(
        prep_kernel, "prep",
        (struct(3, 16, 16, 128), own, own, struct(16, 24, 128), struct(16, 24, 128)),
        [pltpu.SMEM((8,), F32), whole_int, whole_int, pltpu.SemaphoreType.DMA((4,))], moduli, load, density, fixed, hbm=4,
    )
    y_low = shift(high, "col", COL, 1)
    y_high = shift(low, "col", COL, -1)
    to_partner, to_cross = call(
        planes_kernel, "planes", (struct(544, 128), struct(544, 128)), [],
        place, load, k, m, y_low, y_high, smem=1,
    )
    partner, cross = slab_neighbours(to_partner, to_cross)
    part0, full0, full0v = (26, 24, 128), (26, 32, 128), (3, 26, 24, 128)
    b0, u0, k0, m0, message = call(
        fine_kernel, "fine",
        (struct(*full0v), struct(*full0v), struct(*full0), struct(*part0), struct(3, 8, 8, 128)),
        [part0] * 5 + [full0v, (10, 16, 128), (4, 48, 128)],
        place, load, k, m, y_low, y_high, partner, cross, smem=1,
    )
    y_low = shift(message, "col", COL, 1)
    y_high = shift(message, "col", COL, -1)
    wide = jnp.concatenate([y_low, message, y_high], axis=2)
    partner, cross = slab_neighbours(wide, wide)
    full1, full1v, more1 = (24, 24, 128), (3, 24, 24, 128), (25, 24, 128)
    part1, part1v = (16, 16, 128), (3, 16, 16, 128)
    full2, full2v = (12, 16, 128), (3, 12, 16, 128)
    b1, u1, k1, t1, b2, k2, u2, packed = call(
        middle_kernel, "middle",
        (struct(*part1v), struct(*part1v), struct(*part1), struct(*part1), struct(*full2v), struct(*full2),
         struct(*full2v), struct(COL, 8, 128)),
        [full1v, full1v, more1, full1] + [full1] * 5 + [full1v] + [full2] * 5 + [full2v, (4, 48, 128)],
        place, wide, partner, cross, smem=1,
    )
    received = lax.all_to_all(packed, "col", 0, 0)
    window = call(window_kernel, "window", struct(SLAB, 48, 128), [(48, 128)], place, received, u2, smem=1)
    received = lax.all_to_all(window, "slab", 0, 0)
    full3, full3v = (4, 24, 128), (3, 4, 24, 128)
    return call(
        upper_kernel, "upper",
        (struct(3, 16, 16, 128), struct(3, 16, 16, 128)),
        [full3v, full3, (5,) + full3, full3v, full3v, (5,) + full2, full2v, full2v,
         (5,) + part1, part1v, part1v, (5,) + part0, full0v, full0v, (4, 48, 128)],
        place, received, u2, b2, k2, b1, u1, k1, t1, b0, u0, k0, m0, smem=1,
    )


def solution(mesh):
    placed = (P(None, "slab", "col", None), P("slab", "col", None), P(), P("slab", "col", None))
    return jax.shard_map(
        on_device,
        mesh=mesh,
        in_specs=placed,
        out_specs=(P(None, "slab", "col", None), P(None, "slab", "col", None)),
        check_vma=False,
    )
```

time: 139 us -> 115 us (0.83)
  Pallas kernels: 36.2 us -> 22.9 us
  waiting for transfers between devices: 21.1 us -> 15.7 us
  starting transfers between devices: 24.8 us -> 22.3 us
    ppermute x8 -> x4, starting transfers between devices: 24.8 us -> 11.4 us  [shift(): return lax.ppermute(block, axis, pairs)]
    pallas_call x6, Pallas kernels: 36.2 us -> 22.9 us  [call(): pl.pallas_call(kernel, name=name, out_shape=outs, in_specs=specs + [vmem]...]
    ppermute x0 -> x2, starting transfers between devices: none -> 10.9 us  [slab_neighbours(): cross = lax.ppermute(to_cross, 'slab', pairs)]
    ppermute x8 -> x4, waiting for transfers between devices: 21.1 us -> 11.6 us  [shift(): return lax.ppermute(block, axis, pairs)]
    all_to_all x1, blocking collectives: 30.1 us -> 25.7 us  [on_device(): received = lax.all_to_all(window, 'slab', 0, 0)]
    all_gather x0 -> x2, blocking collectives: none -> 4.43 us  [slab_neighbours(): return (lax.all_gather(to_partner, 'slab', axis_index_groups=groups), cross)]
    ppermute x0 -> x2, waiting for transfers between devices: none -> 4.17 us  [slab_neighbours(): cross = lax.ppermute(to_cross, 'slab', pairs)]
    unnamed x16 -> x10, local copies, waits for them, and re-layouts: 4.47 us -> 3.47 us
  transfers between devices with their start and end apart: 8 -> 6, of which waited for: 8 -> 6; matrix products, arithmetic and copies ran while one was open for 0% -> 0% of each run, Pallas kernels for 0% -> 0%
where the time goes in v2:
time: 115 us
  blocking collectives  49.5 us (43%)
  Pallas kernels  22.9 us (20%)
  starting transfers between devices  22.3 us (19%)
  waiting for transfers between devices  15.7 us (14%)
  local copies, waits for them, and re-layouts  3.47 us (3%)
    all_to_all x1, blocking collectives, on_device(): received = lax.all_to_all(window, 'slab', 0, 0)  25.7 us
    pallas_call x6, Pallas kernels, call(): pl.pallas_call(kernel, name=name, out_shape=outs, in_specs=specs + [vmem]...  22.9 us
    all_to_all x1, blocking collectives, on_device(): received = lax.all_to_all(packed, 'col', 0, 0)  19.4 us
    ppermute x4, waiting for transfers between devices, shift(): return lax.ppermute(block, axis, pairs)  11.6 us
    ppermute x4, starting transfers between devices, shift(): return lax.ppermute(block, axis, pairs)  11.4 us
    ppermute x2, starting transfers between devices, slab_neighbours(): cross = lax.ppermute(to_cross, 'slab', pairs)  10.9 us
    all_gather x2, blocking collectives, slab_neighbours(): return (lax.all_gather(to_partner, 'slab', axis_index_groups=groups), cross)  4.43 us
    ppermute x2, waiting for transfers between devices, slab_neighbours(): cross = lax.ppermute(to_cross, 'slab', pairs)  4.17 us
  transfers between devices with their start and end apart: 6, of which 6 were waited for; matrix products, arithmetic and copies ran while one was open for 0% of the time, Pallas kernels for 0%

profile of v2, /device:TPU:1, one launch (start us, length us, event | category | flops | bytes accessed | tf_op | source)
XLA Modules:
  0.0 114.7 jit_solution(10174091632892340565)
XLA Ops:
  0.6 0.0 copy-start
  0.6 1.0 copy-done
  1.6 0.0 copy-start.1
  1.6 0.9 copy-done.1
  2.5 0.0 copy-start.2
  2.5 0.9 copy-done.2
  3.4 0.0 copy-start.3
  3.4 0.7 copy-done.3
  4.1 0.7 prep.1
  4.8 4.8 %collective-permute-start = (f32[16,24,128]{2,1,0:T(8,128)S(1)}, f32[16,24,128]{2,1,0:T(8,128)S(1)}, u32[]{:S(2)}, u32[]{:S(2)}) collective-permute-start(f32[16,24,128]{2,1,0:T(8,128)S(1)} %get-tuple-element.25), channel_id=1, source_target_pairs={{0,1},{1,2},{2,3},{3,4},{4,5},{5,6},{6,7},{7,8},{8,9},{9,10},{10,1... | collective-permute-start | bytes 589832 | tf_op jit(solution)/shard_map/ppermute | solution.py:523
  9.6 1.3 %collective-permute-start.1 = (f32[16,24,128]{2,1,0:T(8,128)S(1)}, f32[16,24,128]{2,1,0:T(8,128)S(1)}, u32[]{:S(2)}, u32[]{:S(2)}) collective-permute-start(f32[16,24,128]{2,1,0:T(8,128)S(1)} %get-tuple-element.26), channel_id=1, source_target_pairs={{1,0},{2,1},{3,2},{4,3},{5,4},{6,5},{7,6},{8,7},{9,8},{10,9},{11,1... | collective-permute-start | bytes 589832 | tf_op jit(solution)/shard_map/ppermute | solution.py:523
  10.9 0.1 pad_add_fusion.place
  11.0 1.2 %collective-permute-done.from_low.y_low = f32[16,24,128]{2,1,0:T(8,128)S(1)} collective-permute-done((f32[16,24,128]{2,1,0:T(8,128)S(1)}, f32[16,24,128]{2,1,0:T(8,128)S(1)}, u32[]{:S(2)}, u32[]{:S(2)}) %collective-permute-start) | collective-permute-done | bytes 196640 | tf_op jit(solution)/shard_map/ppermute | solution.py:523
  12.2 4.5 %collective-permute-done.1.from_high.y_high = f32[16,24,128]{2,1,0:T(8,128)S(1)} collective-permute-done((f32[16,24,128]{2,1,0:T(8,128)S(1)}, f32[16,24,128]{2,1,0:T(8,128)S(1)}, u32[]{:S(2)}, u32[]{:S(2)}) %collective-permute-start.1) | collective-permute-done | bytes 196640 | tf_op jit(solution)/shard_map/ppermute | solution.py:523
  16.7 0.6 planes.1
  17.3 5.9 %collective-permute-start.2 = (f32[544,128]{1,0:T(8,128)S(1)}, f32[544,128]{1,0:T(8,128)S(1)}, u32[]{:S(2)}, u32[]{:S(2)}) collective-permute-start(f32[544,128]{1,0:T(8,128)S(1)} %get-tuple-element.28), channel_id=1, source_target_pairs={{32,64},{64,32},{96,128},{128,96},{160,192},{192,160},{224,256},{2... | collective-permute-start | bytes 835592 | tf_op jit(solution)/shard_map/ppermute | solution.py:530
  23.2 2.2 %all-gather = f32[1088,128]{1,0:T(8,128)S(1)} all-gather(f32[544,128]{1,0:T(8,128)S(1)} %get-tuple-element.27), channel_id=2, replica_groups={{0,32},{64,96},{128,160},{192,224},{256,288},{320,352},{384,416},{448,4..., dimensions={0}, use_global_device_ids=true | all-gather | bytes 835584 | tf_op jit(solution)/shard_map/all_gather | solution.py:532
  25.4 2.0 %collective-permute-done.2.cross = f32[544,128]{1,0:T(8,128)S(1)} collective-permute-done((f32[544,128]{1,0:T(8,128)S(1)}, f32[544,128]{1,0:T(8,128)S(1)}, u32[]{:S(2)}, u32[]{:S(2)}) %collective-permute-start.2) | collective-permute-done | bytes 278560 | tf_op jit(solution)/shard_map/ppermute | solution.py:530
  27.4 3.4 %fine.1 = (f32[3,26,24,128]{3,2,1,0:T(8,128)S(1)}, f32[3,26,24,128]{3,2,1,0:T(8,128)S(1)}, f32[26,32,128]{2,1,0:T(8,128)S(1)}, f32[26,24,128]{2,1,0:T(8,128)S(1)}, f32[3,8,8,128]{3,2,1,0:T(8,128)S(1)}) custom-call(s32[2]{0:T(128)S(1)} %pad_add_fusion.place, f32[3,16,16,128]{3,2,1,0:T(8,128)S(1)} %get-tuple-element.22.load, ...), custom_call_target="tpu_custom_call" | custom-call | tf_op jit(solution)/shard_map/fine/pallas_call | solution.py:510
  30.8 4.0 %collective-permute-start.3 = (f32[3,8,8,128]{3,2,1,0:T(8,128)S(1)}, f32[3,8,8,128]{3,2,1,0:T(8,128)S(1)}, u32[]{:S(2)}, u32[]{:S(2)}) collective-permute-start(f32[3,8,8,128]{3,2,1,0:T(8,128)S(1)} %get-tuple-element.29), channel_id=1, source_target_pairs={{0,1},{1,2},{2,3},{3,4},{4,5},{5,6},{6,7},{7,8},{8,9},{9,10},{10,1... | collective-permute-start | bytes 294920 | tf_op jit(solution)/shard_map/ppermute | solution.py:523
  34.8 1.3 %collective-permute-start.4 = (f32[3,8,8,128]{3,2,1,0:T(8,128)S(1)}, f32[3,8,8,128]{3,2,1,0:T(8,128)S(1)}, u32[]{:S(2)}, u32[]{:S(2)}) collective-permute-start(f32[3,8,8,128]{3,2,1,0:T(8,128)S(1)} %get-tuple-element.29), channel_id=1, source_target_pairs={{1,0},{2,1},{3,2},{4,3},{5,4},{6,5},{7,6},{8,7},{9,8},{10,9},{11,1... | collective-permute-start | bytes 294920 | tf_op jit(solution)/shard_map/ppermute | solution.py:523
  36.1 0.3 collective-permute-done.3
  36.5 5.6 %collective-permute-done.4 = f32[3,8,8,128]{3,2,1,0:T(8,128)S(1)} collective-permute-done((f32[3,8,8,128]{3,2,1,0:T(8,128)S(1)}, f32[3,8,8,128]{3,2,1,0:T(8,128)S(1)}, u32[]{:S(2)}, u32[]{:S(2)}) %collective-permute-start.4) | collective-permute-done | bytes 98336 | tf_op jit(solution)/shard_map/ppermute | solution.py:523
  42.1 5.0 %collective-permute-start.5 = (f32[3,8,24,128]{3,2,1,0:T(8,128)S(1)}, f32[3,8,24,128]{3,2,1,0:T(8,128)S(1)}, u32[]{:S(2)}, u32[]{:S(2)}) collective-permute-start(f32[3,8,24,128]{3,2,1,0:T(8,128)S(1)} %constant_dynamic-update-slice_fusion.own), channel_id=1, source_target_pairs={{32,64},{64,32},{96,128},{128,96},{160,192},{192,160},{224,256},{2... | collective-permute-start | bytes 884744 | tf_op jit(solution)/shard_map/ppermute | solution.py:530
  47.1 2.2 %all-gather.1 = f32[6,8,24,128]{3,2,1,0:T(8,128)S(1)} all-gather(f32[3,8,24,128]{3,2,1,0:T(8,128)S(1)} %constant_dynamic-update-slice_fusion.own), channel_id=3, replica_groups={{0,32},{64,96},{128,160},{192,224},{256,288},{320,352},{384,416},{448,4..., dimensions={0}, use_global_device_ids=true | all-gather | bytes 884736 | tf_op jit(solution)/shard_map/all_gather | solution.py:532
  49.3 2.2 %collective-permute-done.5.cross = f32[3,8,24,128]{3,2,1,0:T(8,128)S(1)} collective-permute-done((f32[3,8,24,128]{3,2,1,0:T(8,128)S(1)}, f32[3,8,24,128]{3,2,1,0:T(8,128)S(1)}, u32[]{:S(2)}, u32[]{:S(2)}) %collective-permute-start.5) | collective-permute-done | bytes 294944 | tf_op jit(solution)/shard_map/ppermute | solution.py:530
  51.5 4.0 %middle.1 = (f32[3,16,16,128]{3,2,1,0:T(8,128)S(1)}, f32[3,16,16,128]{3,2,1,0:T(8,128)S(1)}, f32[16,16,128]{2,1,0:T(8,128)S(1)}, f32[16,16,128]{2,1,0:T(8,128)S(...) custom-call(s32[2]{0:T(128)S(1)} %pad_add_fusion.place, ...), custom_call_target="tpu_custom_call" | custom-call | tf_op jit(solution)/shard_map/middle/pallas_call | solution.py:510
  55.4 19.4 %all_to_all.10.received = f32[32,8,128]{2,1,0:T(8,128)S(1)} all-to-all(f32[32,8,128]{2,1,0:T(8,128)S(1)} %get-tuple-element.30), channel_id=1, replica_groups=mesh['slab'=16,'col'=32] {'col'}, dimensions={0} | all-to-all | bytes 262144 | tf_op jit(solution)/shard_map/all_to_all | solution.py:572
  74.8 0.6 window.1
  75.4 25.7 %all_to_all.11.received = f32[16,48,128]{2,1,0:T(8,128)S(1)} all-to-all(f32[16,48,128]{2,1,0:T(8,128)S(1)} %window.1), channel_id=1, replica_groups=mesh['slab'=16,'col'=32] {'slab'}, dimensions={0} | all-to-all | bytes 786432 | tf_op jit(solution)/shard_map/all_to_all | solution.py:574
  101.1 13.6 %upper.1 = (f32[3,16,16,128]{3,2,1,0:T(8,128)}, f32[3,16,16,128]{3,2,1,0:T(8,128)}) custom-call(s32[2]{0:T(128)S(1)} %pad_add_fusion.place, f32[16,48,128]{2,1,0:T(8,128)S(1)} %all_to_all.11.received, f32[3,12,16,128]{3,2,1,0:T(8,128)S(1)} %get-tuple-element.31.u2, f32[3,12,16,128]{3,2,1,0:T(8,128)S(1)} %get-tuple-element.32.b2, ...), custom_call_target="tpu_custom_call" | custom-call | tf_op jit(solution)/shard_map/upper/pallas_call | solution.py:510
  (3 shorter events, 0.0 us)
Async XLA Ops:
  0.6 1.0 copy-start
  1.6 0.9 copy-start.1
  2.5 0.9 copy-start.2
  3.4 0.7 copy-start.3
  4.8 7.4 %collective-permute-start = (f32[16,24,128]{2,1,0:T(8,128)S(1)}, f32[16,24,128]{2,1,0:T(8,128)S(1)}, u32[]{:S(2)}, u32[]{:S(2)}) collective-permute-start(f32[16,24,128]{2,1,0:T(8,128)S(1)} %get-tuple-element.25), channel_id=1, source_target_pairs={{0,1},{1,2},{2,3},{3,4},{4,5},{5,6},{6,7},{7,8},{8,9},{9,10},{10,1... | collective-permute-start | bytes 589832 | tf_op jit(solution)/shard_map/ppermute | solution.py:523
  9.6 7.0 %collective-permute-start.1 = (f32[16,24,128]{2,1,0:T(8,128)S(1)}, f32[16,24,128]{2,1,0:T(8,128)S(1)}, u32[]{:S(2)}, u32[]{:S(2)}) collective-permute-start(f32[16,24,128]{2,1,0:T(8,128)S(1)} %get-tuple-element.26), channel_id=1, source_target_pairs={{1,0},{2,1},{3,2},{4,3},{5,4},{6,5},{7,6},{8,7},{9,8},{10,9},{11,1... | collective-permute-start | bytes 589832 | tf_op jit(solution)/shard_map/ppermute | solution.py:523
  17.3 10.1 %collective-permute-start.2 = (f32[544,128]{1,0:T(8,128)S(1)}, f32[544,128]{1,0:T(8,128)S(1)}, u32[]{:S(2)}, u32[]{:S(2)}) collective-permute-start(f32[544,128]{1,0:T(8,128)S(1)} %get-tuple-element.28), channel_id=1, source_target_pairs={{32,64},{64,32},{96,128},{128,96},{160,192},{192,160},{224,256},{2... | collective-permute-start | bytes 835592 | tf_op jit(solution)/shard_map/ppermute | solution.py:530
  30.8 5.6 %collective-permute-start.3 = (f32[3,8,8,128]{3,2,1,0:T(8,128)S(1)}, f32[3,8,8,128]{3,2,1,0:T(8,128)S(1)}, u32[]{:S(2)}, u32[]{:S(2)}) collective-permute-start(f32[3,8,8,128]{3,2,1,0:T(8,128)S(1)} %get-tuple-element.29), channel_id=1, source_target_pairs={{0,1},{1,2},{2,3},{3,4},{4,5},{5,6},{6,7},{7,8},{8,9},{9,10},{10,1... | collective-permute-start | bytes 294920 | tf_op jit(solution)/shard_map/ppermute | solution.py:523
  34.8 7.2 %collective-permute-start.4 = (f32[3,8,8,128]{3,2,1,0:T(8,128)S(1)}, f32[3,8,8,128]{3,2,1,0:T(8,128)S(1)}, u32[]{:S(2)}, u32[]{:S(2)}) collective-permute-start(f32[3,8,8,128]{3,2,1,0:T(8,128)S(1)} %get-tuple-element.29), channel_id=1, source_target_pairs={{1,0},{2,1},{3,2},{4,3},{5,4},{6,5},{7,6},{8,7},{9,8},{10,9},{11,1... | collective-permute-start | bytes 294920 | tf_op jit(solution)/shard_map/ppermute | solution.py:523
  42.1 9.4 %collective-permute-start.5 = (f32[3,8,24,128]{3,2,1,0:T(8,128)S(1)}, f32[3,8,24,128]{3,2,1,0:T(8,128)S(1)}, u32[]{:S(2)}, u32[]{:S(2)}) collective-permute-start(f32[3,8,24,128]{3,2,1,0:T(8,128)S(1)} %constant_dynamic-update-slice_fusion.own), channel_id=1, source_target_pairs={{32,64},{64,32},{96,128},{128,96},{160,192},{192,160},{224,256},{2... | collective-permute-start | bytes 884744 | tf_op jit(solution)/shard_map/ppermute | solution.py:530

commit v3 on v2

--- a/solution.py
+++ b/solution.py
@@ -12,23 +12,21 @@
 COL = 32
 F32 = jnp.float32
 
-UNROLL = 8
-
-
-def each(planes, body, unroll=None):
-    unroll = unroll or UNROLL
-    low, high = planes
-    rounds = (high - low) // unroll
-    if rounds > 1:
-        def chunk(t, carry):
-            for q in range(unroll):
-                body(low + t * unroll + q)
-            return carry
-
-        lax.fori_loop(0, rounds, chunk, 0)
-        low += rounds * unroll
-    for p in range(low, high):
-        body(p)
+
+def loop(low, high, body, unroll):
+    def step(t, carry):
+        for q in range(unroll):
+            body(low + t * unroll + q, q)
+        return carry
+
+    assert (high - low) % unroll == 0
+    lax.fori_loop(0, (high - low) // unroll, step, 0)
+
+
+def each(planes, body):
+    count = planes[1] - planes[0]
+    fits = [n for n in (8, 7, 6, 5, 4, 11, 3) if count % n == 0]
+    loop(*planes, lambda p, q: body(p), fits[0])
 
 
 def lanes_of(rows):
@@ -167,34 +165,24 @@
 FINE = slice(4, 28)
 
 
-def prep_kernel(moduli_in, load_in, density_in, fixed_in, load, k_out, m_out, low, high, moduli, density, fixed, sems):
-    copies = [
-        pltpu.make_async_copy(src, dst, sems.at[n])
-        for n, (src, dst) in enumerate(
-            ((moduli_in, moduli), (density_in, density), (fixed_in, fixed), (load_in, load))
-        )
-    ]
-    for copy in copies:
-        copy.start()
-    for copy in copies[:3]:
-        copy.wait()
-    for z in range(16):
-        d = density[z]
+def prep_kernel(moduli, raw, k_out, m_out, low, high):
+    def body(z):
+        d = raw[3, z]
         k = jnp.zeros((16, 128), F32)
         for klass in range(CLASSES):
-            k = jnp.where(d == klass, moduli[klass], k)
-        m = 1.0 - fixed[z].astype(F32)
+            k = jnp.where(d == float(klass), moduli[klass], k)
+        m = 1.0 - raw[4, z]
         k_out[z] = k
         m_out[z] = m
+        for c in range(3):
+            low[z, 4 * c : 4 * c + 4] = raw[c, z, 0:4]
+            high[z, 4 * c : 4 * c + 4] = raw[c, z, 12:16]
         low[z, 12:16] = m[0:4]
         high[z, 12:16] = m[12:16]
         low[z, 16:24] = k[0:8]
         high[z, 16:24] = k[8:16]
-    copies[3].wait()
-    for z in range(16):
-        for c in range(3):
-            low[z, 4 * c : 4 * c + 4] = load[c, z, 0:4]
-            high[z, 4 * c : 4 * c + 4] = load[c, z, 12:16]
+
+    each((0, 16), body)
 
 
 def planes_kernel(place, load, k, m, from_low, from_high, partner, cross):
@@ -220,8 +208,9 @@
 
 def fine_kernel(place, load, k_own, m_own, y_low, y_high, partner, cross,
                 b, u, k, m, message,
-                cx, cy, cz, e, w, first, k1, tmp):
-    co = (cx, cy, cz, e, w)
+                co_out, first, k1, sums, tmp):
+    co = tuple(co_out.at[n] for n in range(5))
+    w = co[4]
     odd = place[0] & 1
     for z in range(16):
         p = z + 5
@@ -250,29 +239,36 @@
     first_sweep((1, 25), b, first, w)
     sweep((2, 24), b, first, u, k, co, 1, FINE)
 
-    for z1 in range(-1, 9):
-        p = 2 * z1 + 5
-        k1[z1 + 1] = block_mean(k[p], k[p + 1], tmp.at[(z1 + 1) % 4], 1)
+    def coarse_k(n, q):
+        p = 2 * n + 3
+        k1[n] = block_mean(k[p], k[p + 1], tmp.at[q], 1)
+
+    loop(0, 10, coarse_k, 5)
     lane = lanes_of(8)
     odd_lane = (lane & 1) != 0
     lane = lanes_of(16)
-    for z1 in range(8):
+
+    def down(z1, s):
         p = 2 * z1 + 5
         rests = [left_over(q, b, u, k, co, 1, FINE)[1] for q in (p, p + 1)]
         parts = [
-            block_mean(m[p] * rests[0][c], m[p + 1] * rests[1][c], tmp.at[c], 1)[2:10] for c in range(3)
+            block_mean(m[p] * rests[0][c], m[p + 1] * rests[1][c], tmp.at[3 * s + c], 1)[2:10] for c in range(3)
         ]
         centre = k1[z1 + 1]
         sides = jnp.where(lane < 126, lane_next(centre, 2), 0.0) + jnp.where(lane >= 2, lane_prev(centre, 2), 0.0)
         total = 0.125 * (6.0 * centre + sides + row_next(centre) + row_prev(centre) + k1[z1] + k1[z1 + 2])
-        message[0, z1] = jnp.where(odd_lane, parts[1], parts[0])
-        message[1, z1] = jnp.where(odd_lane, centre[4:12], parts[2])
-        message[2, z1] = total[4:12]
+        message[z1] = jnp.where(odd_lane, parts[1], parts[0])
+        message[8 + z1] = jnp.where(odd_lane, centre[4:12], parts[2])
+        sums[z1] = total[4:12]
+
+    loop(0, 8, down, 4)
+    for z1 in range(4):
+        message[16 + z1] = jnp.where(odd_lane, sums[z1 + 4], sums[z1])
 
 
 def middle_kernel(place, own, partner, cross,
-                  b1_out, u1_out, k1_out, t1_out, b2, k2, u2b, packed,
-                  b1, u1, k1, t1, cx, cy, cz, e, w, first, cx2, cy2, cz2, e2, w2, u2a, tmp):
+                  b1_out, u1_out, k1_out, t1_out, b2, k2, u2b, packed, co2_out,
+                  b1, u1, k1, t1, cx, cy, cz, e, w, first, u2a, tmp):
     co = (cx, cy, cz, e, w)
     lane = lanes_of(24)
     odd_lane = (lane & 1) != 0
@@ -280,13 +276,16 @@
     for src, start in ((own, 8), (partner.at[1 - odd], 16 * (1 - odd)), (cross, 16 * odd)):
         for q in range(8):
             p = start + q
-            v = src[0, q]
+            v = src[q]
             b1[0, p] = jnp.where(odd_lane, lane_prev(v, 1), v)
             b1[1, p] = jnp.where(odd_lane, v, lane_next(v, 1))
-            v = src[1, q]
+            v = src[8 + q]
             b1[2, p] = jnp.where(odd_lane, lane_prev(v, 1), v)
             k1[p] = jnp.where(odd_lane, v, lane_next(v, 1))
-            t1[p] = src[2, q]
+        for q in range(4):
+            v = src[16 + q]
+            t1[start + q] = jnp.where(odd_lane, lane_prev(v, 1), v)
+            t1[start + 4 + q] = jnp.where(odd_lane, v, lane_next(v, 1))
     k1[24] = jnp.zeros((24, 128), F32)
 
     def fill(p):
@@ -297,23 +296,32 @@
 
     each((0, 24), fill)
     sweep((1, 23), b1, first, u1, k1, co, 2)
-    for p in range(16):
+    def keep(p):
         k1_out[p] = k1[p + 4, 4:20]
         t1_out[p] = t1[p + 4, 4:20]
         for c in range(3):
             b1_out[c, p] = b1[c, p + 4, 4:20]
             u1_out[c, p] = u1[c, p + 4, 4:20]
-    for q2 in range(12):
-        k2[q2, 4:16] = block_mean(k1[2 * q2], k1[2 * q2 + 1], tmp.at[q2 % 4], 2)
+
+    each((0, 16), keep)
+
+    def coarse_k(q2, s):
+        k2[q2, 4:16] = block_mean(k1[2 * q2], k1[2 * q2 + 1], tmp.at[s], 2)
         k2[q2, 0:4] = jnp.zeros((4, 128), F32)
-    for q2 in range(1, 11):
+
+    loop(0, 12, coarse_k, 6)
+
+    def down(q2, s):
         rests = [left_over(p, b1, u1, k1, co, 2)[1] for p in (2 * q2, 2 * q2 + 1)]
         for c in range(3):
-            b2[c, q2, 4:16] = block_mean(rests[0][c], rests[1][c], tmp.at[c], 2)
+            b2[c, q2, 4:16] = block_mean(rests[0][c], rests[1][c], tmp.at[3 * s + c], 2)
             b2[c, q2, 0:4] = jnp.zeros((4, 128), F32)
-    co2 = (cx2, cy2, cz2, e2, w2)
+
+    loop(1, 11, down, 5)
+    co2 = tuple(co2_out.at[n] for n in range(5))
     fill_coefficients(k2, co2, (1, 11), 0.0625, 4)
-    first_sweep((1, 11), b2, u2a, w2)
+    co2[2][0] = (0.5 * 0.0625) * (k2[0] + k2[1])
+    first_sweep((1, 11), b2, u2a, co2[4])
     sweep((2, 10), b2, u2a, u2b, k2, co2, 4)
     j = place[0] // 2
     lane = lanes_of(8)
@@ -321,12 +329,12 @@
     pack = jnp.zeros((8, 128), F32)
     for zz in range(2):
         rests = [left_over(p, b2, u2b, k2, co2, 4)[1] for p in (4 + 2 * zz, 5 + 2 * zz)]
-        parts = [block_mean(rests[0][c], rests[1][c], tmp.at[c], 4) for c in range(3)]
-        parts.append(block_mean(k2[4 + 2 * zz], k2[5 + 2 * zz], tmp.at[3], 4))
+        parts = [block_mean(rests[0][c], rests[1][c], tmp.at[4 * zz + c], 4) for c in range(3)]
+        parts.append(block_mean(k2[4 + 2 * zz], k2[5 + 2 * zz], tmp.at[4 * zz + 3], 4))
         for a in range(4):
             pack = jnp.where(group == ((j + 2 * a + zz) & 7), parts[a], pack)
     quad = lane & 3
-    low, high = tmp.at[0], tmp.at[1]
+    low, high = tmp.at[8], tmp.at[9]
     low[0:2] = pack[4:6]
     high[0:2] = pack[4:6]
     for c in range(3):
@@ -365,21 +373,25 @@
 
     to_high = inner(0)
     to_low = inner(2)
-    for peer in range(SLAB):
-        out[peer] = jnp.where(d < peer, to_high, to_low)
-
-
-def upper_kernel(place, received, u2, b2, k2, b1, u1, k1, t1, b0, u0, k0, m0,
+    for q in range(SLAB // 2):
+        out[q] = jnp.where(q + 1 - (d & 1) > d // 2, to_high, to_low)
+
+
+def upper_kernel(place, received, u2, b2, k2, co2, b1, u1, k1, t1, b0, u0, k0, m0, co0,
                  field, residual,
-                 b3, k3, co3, u3a, u3b, co2, u2a, u2b, co1, u1a, u1b, co0, u0a, u0b, tmp):
+                 b3, k3, co3, u3a, u3b, u2a, u2b, co1, u1a, u1b, u0a, u0b, tmp):
     d = place[0]
     lane = lanes_of(24)
     group = lane & 7
-    for a in range(2):
+
+    def unpack(a, carry):
+        mixes = [jnp.zeros((24, 128), F32)] * 8
+        for j in range(8):
+            v = received[a, j, 0:24]
+            for r in range(8):
+                mixes[r] = jnp.where(group == ((j + r) & 7), v, mixes[r])
         for r in range(8):
-            mix = jnp.zeros((24, 128), F32)
-            for j in range(8):
-                mix = jnp.where(group == ((j + r) & 7), received[2 * j + a, 0:24], mix)
+            mix = mixes[r]
             if r:
                 mix = jnp.where(group < 8 - r, lane_next(mix, r), lane_prev(mix, 8 - r))
             arr, plane = r // 2, 2 * a + r % 2
@@ -387,6 +399,9 @@
                 b3[arr, plane] = mix
             else:
                 k3[plane] = mix
+        return carry
+
+    lax.fori_loop(0, 2, unpack, 0)
 
     def above(v_of, i):
         return v_of(i + 1) if i < 3 else jnp.where(group < 7, lane_next(v_of(0), 1), 0.0)
@@ -427,38 +442,55 @@
     coarse(u3a, u3b)
 
     c2 = tuple(co2.at[n] for n in range(5))
-    fill_coefficients(k2, c2, (1, 11), 0.0625, 4)
-    c2[2][0] = (0.5 * 0.0625) * (k2[0] + k2[1])
     lane8 = lanes_of(8)
     lane4 = lanes_of(4)
-    for q2 in range(12):
-        zz = q2 % 4
-        peer = d - 1 + q2 // 4
+
+    def outer(g, carry):
+        peer = d - 1 + g
         inside = jnp.logical_and(peer >= 0, peer < SLAB)
         peer = jnp.clip(peer, 0, SLAB - 1)
-        far = q2 if q2 < 2 else q2 - 10 if q2 >= 10 else None
-        for c in range(3):
-            v = jnp.where(jnp.logical_and((lane4 & 3) == zz, inside), received[peer, 22 + 4 * c : 26 + 4 * c], 0.0)
-            v = spread(v, lane4, 4)
-            u2a[c, q2, 0:4] = jnp.zeros((4, 128), F32)
-            u2a[c, q2, 4:6] = v[0:2]
-            u2a[c, q2, 14:16] = v[2:4]
-            if far is None:
-                u2a[c, q2, 6:14] = u2[c, q2, 6:14]
-            else:
-                v = received[peer, 34 + 4 * c : 38 + 4 * c]
+        for zz in range(4):
+            pick = jnp.logical_and((lane4 & 3) == zz, inside)
+            for c in range(3):
+                v = spread(jnp.where(pick, received[peer & 1, peer // 2, 22 + 4 * c : 26 + 4 * c], 0.0), lane4, 4)
+                u2a[c, 4 * g + zz, 0:4] = jnp.zeros((4, 128), F32)
+                u2a[c, 4 * g + zz, 4:6] = v[0:2]
+                u2a[c, 4 * g + zz, 14:16] = v[2:4]
+        return carry
+
+    lax.fori_loop(0, 3, outer, 0)
+
+    def middle(q2, _):
+        for c in range(3):
+            u2a[c, q2, 6:14] = u2[c, q2, 6:14]
+
+    loop(2, 10, middle, 4)
+
+    def far(g, carry):
+        peer = d - 1 + 2 * g
+        inside = jnp.logical_and(peer >= 0, peer < SLAB)
+        peer = jnp.clip(peer, 0, SLAB - 1)
+        for c in range(3):
+            v = received[peer & 1, peer // 2, 34 + 4 * c : 38 + 4 * c]
+            for f in range(2):
                 for half in range(2):
-                    pick = jnp.logical_and((lane4 & 3) == 2 * half + far, inside)
-                    u2a[c, q2, 6 + 4 * half : 10 + 4 * half] = spread(jnp.where(pick, v, 0.0), lane4, 4)
-    for t in range(6):
+                    pick = jnp.logical_and((lane4 & 3) == 2 * half + f, inside)
+                    u2a[c, 10 * g + f, 6 + 4 * half : 10 + 4 * half] = spread(jnp.where(pick, v, 0.0), lane4, 4)
+        return carry
+
+    lax.fori_loop(0, 2, far, 0)
+
+    def add_coarse(t, s):
         z = 2 * d - 2 + t
         i = (z + 32) & 3
         j = z >> 2
         for c in range(3):
             v = jnp.where((lane8 & 7) == j, u3b[c, i, 8:16], 0.0)
-            double_rows(spread(v, lane8, 8), tmp.at[c])
+            double_rows(spread(v, lane8, 8), tmp.at[3 * s + c])
             for q2 in (2 * t, 2 * t + 1):
-                u2a[c, q2, 4:16] = u2a[c, q2, 4:16] + tmp[c, 0:12]
+                u2a[c, q2, 4:16] = u2a[c, q2, 4:16] + tmp[3 * s + c, 0:12]
+
+    loop(0, 6, add_coarse, 3)
     sweep((1, 11), b2, u2a, u2b, k2, c2, 4)
     sweep((2, 10), b2, u2b, u2a, k2, c2, 4)
 
@@ -469,24 +501,27 @@
             ref[p] = v
 
     each((0, 15), fill)
-    for q2 in range(2, 10):
-        for c in range(3):
-            double_rows(u2a[c, q2, 6:14], tmp.at[c])
-            more = tmp[c, 0:16]
+
+    def add_middle(q2, s):
+        for c in range(3):
+            double_rows(u2a[c, q2, 6:14], tmp.at[3 * s + c])
+            more = tmp[3 * s + c, 0:16]
             for p in (2 * q2 - 4, 2 * q2 - 3):
                 u1a[c, p] = u1[c, p] + more
+
+    loop(2, 10, add_middle, 4)
     sweep((1, 15), b1, u1a, u1b, k1, c1, 2)
     sweep((2, 14), b1, u1b, u1a, k1, c1, 2)
 
     c0 = tuple(co0.at[n] for n in range(5))
-    fine_coefficients(k0, m0, c0, (2, 24))
-    for p1 in range(2, 14):
-        for c in range(3):
-            double_rows(u1a[c, p1], tmp.at[c])
-            more = tmp[c, 4:28]
+    def add_fine(p1, s):
+        for c in range(3):
+            double_rows(u1a[c, p1], tmp.at[3 * s + c])
+            more = tmp[3 * s + c, 4:28]
             for p in (2 * p1 - 3, 2 * p1 - 2):
-                if 2 <= p < 24:
-                    u0a[c, p] = u0[c, p] + m0[p] * more
+                u0a[c, p] = u0[c, p] + m0[p] * more
+
+    loop(2, 14, add_fine, 4)
     sweep((3, 23), b0, u0a, u0b, k0, c0, 1, FINE)
     sweep((4, 22), b0, u0b, u0a, k0, c0, 1, FINE)
 
@@ -504,16 +539,16 @@
     return jax.ShapeDtypeStruct(shape, F32)
 
 
-def call(kernel, name, outs, scratch, *args, smem=0, hbm=0):
+def call(kernel, name, outs, scratch, *args, smem=0):
     vmem = pl.BlockSpec(memory_space=pltpu.VMEM)
-    specs = [pl.BlockSpec(memory_space=pltpu.SMEM)] * smem + [pl.BlockSpec(memory_space=pltpu.HBM)] * hbm
+    specs = [pl.BlockSpec(memory_space=pltpu.SMEM)] * smem
     return pl.pallas_call(
         kernel,
         name=name,
         out_shape=outs,
         in_specs=specs + [vmem] * (len(args) - len(specs)),
         out_specs=jax.tree.map(lambda _: vmem, outs),
-        scratch_shapes=[pltpu.VMEM(s, F32) if isinstance(s, tuple) else s for s in scratch],
+        scratch_shapes=[pltpu.VMEM(s, F32) for s in scratch],
         compiler_params=pltpu.CompilerParams(vmem_limit_bytes=40 * 1024 * 1024),
     )(*args)
 
@@ -535,50 +570,51 @@
 def on_device(load, density, moduli, fixed):
     place = jnp.stack([lax.axis_index("slab"), lax.axis_index("col")]).astype(jnp.int32)
     own = struct(16, 16, 128)
-    whole_int = pltpu.VMEM((16, 16, 128), jnp.int32)
-    load, k, m, low, high = call(
-        prep_kernel, "prep",
-        (struct(3, 16, 16, 128), own, own, struct(16, 24, 128), struct(16, 24, 128)),
-        [pltpu.SMEM((8,), F32), whole_int, whole_int, pltpu.SemaphoreType.DMA((4,))], moduli, load, density, fixed, hbm=4,
+    raw = jnp.concatenate([load, density[None].astype(F32), fixed[None].astype(F32)], axis=0)
+    k, m, low, high = call(
+        prep_kernel, "prep", (own, own, struct(16, 24, 128), struct(16, 24, 128)), [], moduli, raw, smem=1
     )
     y_low = shift(high, "col", COL, 1)
     y_high = shift(low, "col", COL, -1)
     to_partner, to_cross = call(
         planes_kernel, "planes", (struct(544, 128), struct(544, 128)), [],
-        place, load, k, m, y_low, y_high, smem=1,
+        place, raw, k, m, y_low, y_high, smem=1,
     )
     partner, cross = slab_neighbours(to_partner, to_cross)
     part0, full0, full0v = (26, 24, 128), (26, 32, 128), (3, 26, 24, 128)
-    b0, u0, k0, m0, message = call(
+    b0, u0, k0, m0, message, co0 = call(
         fine_kernel, "fine",
-        (struct(*full0v), struct(*full0v), struct(*full0), struct(*part0), struct(3, 8, 8, 128)),
-        [part0] * 5 + [full0v, (10, 16, 128), (4, 48, 128)],
-        place, load, k, m, y_low, y_high, partner, cross, smem=1,
+        (struct(*full0v), struct(*full0v), struct(*full0), struct(*part0), struct(20, 8, 128),
+         struct(5, *part0)),
+        [full0v, (10, 16, 128), (8, 8, 128), (16, 48, 128)],
+        place, raw, k, m, y_low, y_high, partner, cross, smem=1,
     )
     y_low = shift(message, "col", COL, 1)
     y_high = shift(message, "col", COL, -1)
-    wide = jnp.concatenate([y_low, message, y_high], axis=2)
+    wide = jnp.concatenate([y_low, message, y_high], axis=1)
     partner, cross = slab_neighbours(wide, wide)
     full1, full1v, more1 = (24, 24, 128), (3, 24, 24, 128), (25, 24, 128)
     part1, part1v = (16, 16, 128), (3, 16, 16, 128)
     full2, full2v = (12, 16, 128), (3, 12, 16, 128)
-    b1, u1, k1, t1, b2, k2, u2, packed = call(
+    b1, u1, k1, t1, b2, k2, u2, packed, co2 = call(
         middle_kernel, "middle",
         (struct(*part1v), struct(*part1v), struct(*part1), struct(*part1), struct(*full2v), struct(*full2),
-         struct(*full2v), struct(COL, 8, 128)),
-        [full1v, full1v, more1, full1] + [full1] * 5 + [full1v] + [full2] * 5 + [full2v, (4, 48, 128)],
+         struct(*full2v), struct(COL, 8, 128), struct(5, *full2)),
+        [full1v, full1v, more1, full1] + [full1] * 5 + [full1v] + [full2v, (16, 48, 128)],
         place, wide, partner, cross, smem=1,
     )
     received = lax.all_to_all(packed, "col", 0, 0)
-    window = call(window_kernel, "window", struct(SLAB, 48, 128), [(48, 128)], place, received, u2, smem=1)
-    received = lax.all_to_all(window, "slab", 0, 0)
+    window = call(window_kernel, "window", struct(SLAB // 2, 48, 128), [(48, 128)], place, received, u2, smem=1)
+    groups = [list(range(par, SLAB, 2)) for par in range(2)]
+    received = lax.all_to_all(window, "slab", 0, 0, axis_index_groups=groups)
+    received = lax.all_gather(received, "slab", axis_index_groups=[[i, i + 1] for i in range(0, SLAB, 2)])
     full3, full3v = (4, 24, 128), (3, 4, 24, 128)
     return call(
         upper_kernel, "upper",
         (struct(3, 16, 16, 128), struct(3, 16, 16, 128)),
-        [full3v, full3, (5,) + full3, full3v, full3v, (5,) + full2, full2v, full2v,
-         (5,) + part1, part1v, part1v, (5,) + part0, full0v, full0v, (4, 48, 128)],
-        place, received, u2, b2, k2, b1, u1, k1, t1, b0, u0, k0, m0, smem=1,
+        [full3v, full3, (5,) + full3, full3v, full3v, full2v, full2v,
+         (5,) + part1, part1v, part1v, full0v, full0v, (16, 48, 128)],
+        place, received, u2, b2, k2, co2, b1, u1, k1, t1, b0, u0, k0, m0, co0, smem=1,
     )
 
 

time: 115 us -> 105 us (0.913)
  Pallas kernels: 22.9 us -> 18.4 us
  local copies, waits for them, and re-layouts: 3.47 us -> 0.02 us
  blocking collectives: 49.5 us -> 46.5 us
  other arithmetic: 0.08 us -> 2.11 us
    all_to_all x1, blocking collectives: 25.7 us -> 15.8 us  [on_device(): received = lax.all_to_all(window, 'slab', 0, 0, axis_index_groups=groups)]
    all_gather x0 -> x1, blocking collectives: none -> 6.34 us  [on_device(): lax.all_gather(received, 'slab', axis_index_groups=[[i, i + 1] for i in r...]
    pallas_call x6, Pallas kernels: 22.9 us -> 18.4 us  [call(): pl.pallas_call(kernel, name=name, out_shape=outs, in_specs=specs + [vmem]...]
    unnamed x10 -> x4, local copies, waits for them, and re-layouts: 3.47 us -> 0.02 us
where the time goes in v3:
time: 105 us
  blocking collectives  46.5 us (44%)
  starting transfers between devices  22.1 us (21%)
  Pallas kernels  18.4 us (18%)
  waiting for transfers between devices  15.1 us (14%)
  other arithmetic  2.11 us (2%)
    all_to_all x1, blocking collectives, on_device(): received = lax.all_to_all(packed, 'col', 0, 0)  20 us
    pallas_call x6, Pallas kernels, call(): pl.pallas_call(kernel, name=name, out_shape=outs, in_specs=specs + [vmem]...  18.4 us
    all_to_all x1, blocking collectives, on_device(): received = lax.all_to_all(window, 'slab', 0, 0, axis_index_groups=groups)  15.8 us
    ppermute x4, starting transfers between devices, shift(): return lax.ppermute(block, axis, pairs)  11.4 us
    ppermute x4, waiting for transfers between devices, shift(): return lax.ppermute(block, axis, pairs)  11.4 us
    ppermute x2, starting transfers between devices, slab_neighbours(): cross = lax.ppermute(to_cross, 'slab', pairs)  10.7 us
    all_gather x1, blocking collectives, on_device(): lax.all_gather(received, 'slab', axis_index_groups=[[i, i + 1] for i in r...  6.34 us
    all_gather x2, blocking collectives, slab_neighbours(): return (lax.all_gather(to_partner, 'slab', axis_index_groups=groups), cross)  4.36 us
  transfers between devices with their start and end apart: 6, of which 6 were waited for; matrix products, arithmetic and copies ran while one was open for 0% of the time, Pallas kernels for 0%

profile of v3, /device:TPU:1, one launch (start us, length us, event | category | flops | bytes accessed | tf_op | source)
XLA Modules:
  0.0 105.0 jit_solution(4089655620665423063)
XLA Ops:
  0.6 0.0 copy-start
  0.6 1.0 convert_bitcast_fusion
  1.6 1.0 pad_maximum_fusion.raw.load
  2.7 0.0 copy-done
  2.7 0.6 prep.1
  3.3 4.8 %collective-permute-start = (f32[16,24,128]{2,1,0:T(8,128)S(1)}, f32[16,24,128]{2,1,0:T(8,128)S(1)}, u32[]{:S(2)}, u32[]{:S(2)}) collective-permute-start(f32[16,24,128]{2,1,0:T(8,128)S(1)} %get-tuple-element.25), channel_id=1, source_target_pairs={{0,1},{1,2},{2,3},{3,4},{4,5},{5,6},{6,7},{7,8},{8,9},{9,10},{10,1... | collective-permute-start | bytes 589832 | tf_op jit(solution)/shard_map/ppermute | solution.py:558
  8.2 1.3 %collective-permute-start.1 = (f32[16,24,128]{2,1,0:T(8,128)S(1)}, f32[16,24,128]{2,1,0:T(8,128)S(1)}, u32[]{:S(2)}, u32[]{:S(2)}) collective-permute-start(f32[16,24,128]{2,1,0:T(8,128)S(1)} %get-tuple-element.26), channel_id=1, source_target_pairs={{1,0},{2,1},{3,2},{4,3},{5,4},{6,5},{7,6},{8,7},{9,8},{10,9},{11,1... | collective-permute-start | bytes 589832 | tf_op jit(solution)/shard_map/ppermute | solution.py:558
  9.5 0.1 pad_add_fusion.place
  9.6 1.2 %collective-permute-done.from_low.y_low = f32[16,24,128]{2,1,0:T(8,128)S(1)} collective-permute-done((f32[16,24,128]{2,1,0:T(8,128)S(1)}, f32[16,24,128]{2,1,0:T(8,128)S(1)}, u32[]{:S(2)}, u32[]{:S(2)}) %collective-permute-start) | collective-permute-done | bytes 196640 | tf_op jit(solution)/shard_map/ppermute | solution.py:558
  10.8 4.5 %collective-permute-done.1.from_high.y_high = f32[16,24,128]{2,1,0:T(8,128)S(1)} collective-permute-done((f32[16,24,128]{2,1,0:T(8,128)S(1)}, f32[16,24,128]{2,1,0:T(8,128)S(1)}, u32[]{:S(2)}, u32[]{:S(2)}) %collective-permute-start.1) | collective-permute-done | bytes 196640 | tf_op jit(solution)/shard_map/ppermute | solution.py:558
  15.2 0.6 planes.1
  15.8 5.9 %collective-permute-start.2 = (f32[544,128]{1,0:T(8,128)S(1)}, f32[544,128]{1,0:T(8,128)S(1)}, u32[]{:S(2)}, u32[]{:S(2)}) collective-permute-start(f32[544,128]{1,0:T(8,128)S(1)} %get-tuple-element.28), channel_id=1, source_target_pairs={{32,64},{64,32},{96,128},{128,96},{160,192},{192,160},{224,256},{2... | collective-permute-start | bytes 835592 | tf_op jit(solution)/shard_map/ppermute | solution.py:565
  21.7 2.2 %all-gather = f32[1088,128]{1,0:T(8,128)S(1)} all-gather(f32[544,128]{1,0:T(8,128)S(1)} %get-tuple-element.27), channel_id=2, replica_groups={{0,32},{64,96},{128,160},{192,224},{256,288},{320,352},{384,416},{448,4..., dimensions={0}, use_global_device_ids=true | all-gather | bytes 835584 | tf_op jit(solution)/shard_map/all_gather | solution.py:567
  23.9 2.0 %collective-permute-done.2.cross = f32[544,128]{1,0:T(8,128)S(1)} collective-permute-done((f32[544,128]{1,0:T(8,128)S(1)}, f32[544,128]{1,0:T(8,128)S(1)}, u32[]{:S(2)}, u32[]{:S(2)}) %collective-permute-start.2) | collective-permute-done | bytes 278560 | tf_op jit(solution)/shard_map/ppermute | solution.py:565
  25.9 3.6 %fine.1 = (f32[3,26,24,128]{3,2,1,0:T(8,128)S(1)}, f32[3,26,24,128]{3,2,1,0:T(8,128)S(1)}, f32[26,32,128]{2,1,0:T(8,128)S(1)}, f32[26,24,128]{2,1,0:T(8,128)S(1)...) custom-call(s32[2]{0:T(128)S(1)} %pad_add_fusion.place, f32[5,16,16,128]{3,2,1,0:T(8,128)S(1)} %pad_maximum_fusion.raw.load, ...), custom_call_target="tpu_custom_call" | custom-call | tf_op jit(solution)/shard_map/fine/pallas_call | solution.py:545
  29.5 4.0 %collective-permute-start.3 = (f32[20,8,128]{2,1,0:T(8,128)S(1)}, f32[20,8,128]{2,1,0:T(8,128)S(1)}, u32[]{:S(2)}, u32[]{:S(2)}) collective-permute-start(f32[20,8,128]{2,1,0:T(8,128)S(1)} %get-tuple-element.29), channel_id=1, source_target_pairs={{0,1},{1,2},{2,3},{3,4},{4,5},{5,6},{6,7},{7,8},{8,9},{9,10},{10,1... | collective-permute-start | bytes 245768 | tf_op jit(solution)/shard_map/ppermute | solution.py:558
  33.5 1.3 %collective-permute-start.4 = (f32[20,8,128]{2,1,0:T(8,128)S(1)}, f32[20,8,128]{2,1,0:T(8,128)S(1)}, u32[]{:S(2)}, u32[]{:S(2)}) collective-permute-start(f32[20,8,128]{2,1,0:T(8,128)S(1)} %get-tuple-element.29), channel_id=1, source_target_pairs={{1,0},{2,1},{3,2},{4,3},{5,4},{6,5},{7,6},{8,7},{9,8},{10,9},{11,1... | collective-permute-start | bytes 245768 | tf_op jit(solution)/shard_map/ppermute | solution.py:558
  34.8 0.2 collective-permute-done.3
  35.0 5.6 %collective-permute-done.4 = f32[20,8,128]{2,1,0:T(8,128)S(1)} collective-permute-done((f32[20,8,128]{2,1,0:T(8,128)S(1)}, f32[20,8,128]{2,1,0:T(8,128)S(1)}, u32[]{:S(2)}, u32[]{:S(2)}) %collective-permute-start.4) | collective-permute-done | bytes 81952 | tf_op jit(solution)/shard_map/ppermute | solution.py:558
  40.6 4.8 %collective-permute-start.5 = (f32[20,24,128]{2,1,0:T(8,128)S(1)}, f32[20,24,128]{2,1,0:T(8,128)S(1)}, u32[]{:S(2)}, u32[]{:S(2)}) collective-permute-start(f32[20,24,128]{2,1,0:T(8,128)S(1)} %constant_dynamic-update-slice_fusion.own), channel_id=1, source_target_pairs={{32,64},{64,32},{96,128},{128,96},{160,192},{192,160},{224,256},{2... | collective-permute-start | bytes 737288 | tf_op jit(solution)/shard_map/ppermute | solution.py:565
  45.4 2.2 %all-gather.1 = f32[40,24,128]{2,1,0:T(8,128)S(1)} all-gather(f32[20,24,128]{2,1,0:T(8,128)S(1)} %constant_dynamic-update-slice_fusion.own), channel_id=3, replica_groups={{0,32},{64,96},{128,160},{192,224},{256,288},{320,352},{384,416},{448,4..., dimensions={0}, use_global_device_ids=true | all-gather | bytes 737280 | tf_op jit(solution)/shard_map/all_gather | solution.py:567
  47.5 1.7 %collective-permute-done.5.cross = f32[20,24,128]{2,1,0:T(8,128)S(1)} collective-permute-done((f32[20,24,128]{2,1,0:T(8,128)S(1)}, f32[20,24,128]{2,1,0:T(8,128)S(1)}, u32[]{:S(2)}, u32[]{:S(2)}) %collective-permute-start.5) | collective-permute-done | bytes 245792 | tf_op jit(solution)/shard_map/ppermute | solution.py:565
  49.3 4.4 %middle.1 = (f32[3,16,16,128]{3,2,1,0:T(8,128)S(1)}, f32[3,16,16,128]{3,2,1,0:T(8,128)S(1)}, f32[16,16,128]{2,1,0:T(8,128)S(1)}, f32[16,16,128]{2,1,0:T(8,128)S(...) custom-call(s32[2]{0:T(128)S(1)} %pad_add_fusion.place, ...), custom_call_target="tpu_custom_call" | custom-call | tf_op jit(solution)/shard_map/middle/pallas_call | solution.py:545
  53.7 20.0 %all_to_all.10.received = f32[32,8,128]{2,1,0:T(8,128)S(1)} all-to-all(f32[32,8,128]{2,1,0:T(8,128)S(1)} %get-tuple-element.30), channel_id=1, replica_groups=mesh['slab'=16,'col'=32] {'col'}, dimensions={0} | all-to-all | bytes 262144 | tf_op jit(solution)/shard_map/all_to_all | solution.py:606
  73.7 0.6 window.1
  74.3 15.8 %all_to_all.11 = f32[8,48,128]{2,1,0:T(8,128)S(1)} all-to-all(f32[8,48,128]{2,1,0:T(8,128)S(1)} %window.1), channel_id=1, replica_groups={{0,64,128,192,256,320,384,448},{32,96,160,224,288,352,416,480},{1,65,12..., dimensions={0} | all-to-all | bytes 393216 | tf_op jit(solution)/shard_map/all_to_all | solution.py:609
  90.1 6.3 %all-gather.2 = f32[16,48,128]{2,1,0:T(8,128)S(1)} all-gather(f32[8,48,128]{2,1,0:T(8,128)S(1)} %all_to_all.11), channel_id=4, replica_groups={{0,32},{64,96},{128,160},{192,224},{256,288},{320,352},{384,416},{448,4..., dimensions={0}, use_global_device_ids=true | all-gather | bytes 589824 | tf_op jit(solution)/shard_map/all_gather | solution.py:610
  96.5 8.6 %upper.1 = (f32[3,16,16,128]{3,2,1,0:T(8,128)}, f32[3,16,16,128]{3,2,1,0:T(8,128)}) custom-call(s32[2]{0:T(128)S(1)} %pad_add_fusion.place, f32[2,8,48,128]{3,2,1,0:T(8,128)S(1)} %bitcast.11, f32[3,12,16,128]{3,2,1,0:T(8,128)S(1)} %get-tuple-element.31.u2, f32[3,12,16,128]{3,2,1,0:T(8,128)S(1)} %get-tuple-element.32.b2, ...), custom_call_target="tpu_custom_call" | custom-call | tf_op jit(solution)/shard_map/upper/pallas_call | solution.py:545
  (3 shorter events, 0.0 us)
Async XLA Ops:
  0.6 2.1 %copy-start = (f32[8]{0:T(128)S(1)}, f32[8]{0:T(128)}, u32[]{:S(2)}) copy-start(f32[8]{0:T(128)} %moduli.1) | copy-start | bytes 100
  3.3 7.4 %collective-permute-start = (f32[16,24,128]{2,1,0:T(8,128)S(1)}, f32[16,24,128]{2,1,0:T(8,128)S(1)}, u32[]{:S(2)}, u32[]{:S(2)}) collective-permute-start(f32[16,24,128]{2,1,0:T(8,128)S(1)} %get-tuple-element.25), channel_id=1, source_target_pairs={{0,1},{1,2},{2,3},{3,4},{4,5},{5,6},{6,7},{7,8},{8,9},{9,10},{10,1... | collective-permute-start | bytes 589832 | tf_op jit(solution)/shard_map/ppermute | solution.py:558
  8.2 7.0 %collective-permute-start.1 = (f32[16,24,128]{2,1,0:T(8,128)S(1)}, f32[16,24,128]{2,1,0:T(8,128)S(1)}, u32[]{:S(2)}, u32[]{:S(2)}) collective-permute-start(f32[16,24,128]{2,1,0:T(8,128)S(1)} %get-tuple-element.26), channel_id=1, source_target_pairs={{1,0},{2,1},{3,2},{4,3},{5,4},{6,5},{7,6},{8,7},{9,8},{10,9},{11,1... | collective-permute-start | bytes 589832 | tf_op jit(solution)/shard_map/ppermute | solution.py:558
  15.8 10.1 %collective-permute-start.2 = (f32[544,128]{1,0:T(8,128)S(1)}, f32[544,128]{1,0:T(8,128)S(1)}, u32[]{:S(2)}, u32[]{:S(2)}) collective-permute-start(f32[544,128]{1,0:T(8,128)S(1)} %get-tuple-element.28), channel_id=1, source_target_pairs={{32,64},{64,32},{96,128},{128,96},{160,192},{192,160},{224,256},{2... | collective-permute-start | bytes 835592 | tf_op jit(solution)/shard_map/ppermute | solution.py:565
  29.5 5.5 %collective-permute-start.3 = (f32[20,8,128]{2,1,0:T(8,128)S(1)}, f32[20,8,128]{2,1,0:T(8,128)S(1)}, u32[]{:S(2)}, u32[]{:S(2)}) collective-permute-start(f32[20,8,128]{2,1,0:T(8,128)S(1)} %get-tuple-element.29), channel_id=1, source_target_pairs={{0,1},{1,2},{2,3},{3,4},{4,5},{5,6},{6,7},{7,8},{8,9},{9,10},{10,1... | collective-permute-start | bytes 245768 | tf_op jit(solution)/shard_map/ppermute | solution.py:558
  33.5 7.0 %collective-permute-start.4 = (f32[20,8,128]{2,1,0:T(8,128)S(1)}, f32[20,8,128]{2,1,0:T(8,128)S(1)}, u32[]{:S(2)}, u32[]{:S(2)}) collective-permute-start(f32[20,8,128]{2,1,0:T(8,128)S(1)} %get-tuple-element.29), channel_id=1, source_target_pairs={{1,0},{2,1},{3,2},{4,3},{5,4},{6,5},{7,6},{8,7},{9,8},{10,9},{11,1... | collective-permute-start | bytes 245768 | tf_op jit(solution)/shard_map/ppermute | solution.py:558
  40.6 8.7 %collective-permute-start.5 = (f32[20,24,128]{2,1,0:T(8,128)S(1)}, f32[20,24,128]{2,1,0:T(8,128)S(1)}, u32[]{:S(2)}, u32[]{:S(2)}) collective-permute-start(f32[20,24,128]{2,1,0:T(8,128)S(1)} %constant_dynamic-update-slice_fusion.own), channel_id=1, source_target_pairs={{32,64},{64,32},{96,128},{128,96},{160,192},{192,160},{224,256},{2... | collective-permute-start | bytes 737288 | tf_op jit(solution)/shard_map/ppermute | solution.py:565

commit v4 on v3

--- a/solution.py
+++ b/solution.py
@@ -23,10 +23,14 @@
     lax.fori_loop(0, (high - low) // unroll, step, 0)
 
 
+def span(low, count, body, unroll=None):
+    fits = [n for n in (8, 7, 6, 5, 4, 11, 3, 2) if count % n == 0]
+    loop(0, count, lambda n, q: body(low + n, q), unroll or fits[0])
+
+
 def each(planes, body):
-    count = planes[1] - planes[0]
-    fits = [n for n in (8, 7, 6, 5, 4, 11, 3) if count % n == 0]
-    loop(*planes, lambda p, q: body(p), fits[0])
+    count = planes[2] if len(planes) == 3 else planes[1] - planes[0]
+    span(planes[0], count, lambda p, q: body(p))
 
 
 def lanes_of(rows):
@@ -206,44 +210,24 @@
             out[base + 24 : base + 32] = from_high[z, 16:24]
 
 
-def fine_kernel(place, load, k_own, m_own, y_low, y_high, partner, cross,
-                b, u, k, m, message,
-                co_out, first, k1, sums, tmp):
+def fine_part(odd, near, b, u, k, m, message, co_out, first, k1, sums, tmp):
     co = tuple(co_out.at[n] for n in range(5))
-    w = co[4]
-    odd = place[0] & 1
-    for z in range(16):
-        p = z + 5
-        for c in range(3):
-            b[c, p, 0:4] = y_low[z, 4 * c : 4 * c + 4]
-            b[c, p, 4:20] = load[c, z]
-            b[c, p, 20:24] = y_high[z, 4 * c : 4 * c + 4]
-        m[p, 0:4] = y_low[z, 12:16]
-        m[p, 4:20] = m_own[z]
-        m[p, 20:24] = y_high[z, 12:16]
-        k[p, 0:8] = y_low[z, 16:24]
-        k[p, 8:24] = k_own[z]
-        k[p, 24:32] = y_high[z, 16:24]
-    for src, high in ((partner.at[1 - odd], 1 - odd), (cross, odd)):
-        start, k_start = 1 + 20 * high, 21 * high
-        for q in range(4):
-            for a in range(4):
-                part = src[24 * (4 * a + q) : 24 * (4 * a + q) + 24]
-                if a < 3:
-                    b[a, start + q] = part
-                else:
-                    m[start + q] = part
-        for q in range(5):
-            k[k_start + q] = src[384 + 32 * q : 416 + 32 * q]
-    fine_coefficients(k, m, co, (1, 25))
-    first_sweep((1, 25), b, first, w)
-    sweep((2, 24), b, first, u, k, co, 1, FINE)
+    even = 1 - odd
+    if near:
+        (c_low, c_count), (s_low, s_count) = (1 + 6 * even, 18), (2 + 6 * even, 16)
+        (k_low, k_count), (d_low, d_count) = (2 * even, 8), (2 * even, 6)
+    else:
+        (c_low, c_count), (s_low, s_count) = (1 + 18 * odd, 6), (2 + 16 * odd, 6)
+        (k_low, k_count), (d_low, d_count) = (8 * odd, 2), (6 * odd, 2)
+    fine_coefficients(k, m, co, (c_low, None, c_count))
+    first_sweep((c_low, None, c_count), b, first, co[4])
+    sweep((s_low, None, s_count), b, first, u, k, co, 1, FINE)
 
     def coarse_k(n, q):
         p = 2 * n + 3
         k1[n] = block_mean(k[p], k[p + 1], tmp.at[q], 1)
 
-    loop(0, 10, coarse_k, 5)
+    span(k_low, k_count, coarse_k)
     lane = lanes_of(8)
     odd_lane = (lane & 1) != 0
     lane = lanes_of(16)
@@ -261,41 +245,122 @@
         message[8 + z1] = jnp.where(odd_lane, centre[4:12], parts[2])
         sums[z1] = total[4:12]
 
-    loop(0, 8, down, 4)
+    span(d_low, d_count, down, 3 if near else 2)
+
+
+def place_planes(src, high, b, m, k):
+    start, k_start = 1 + 20 * high, 21 * high
+    for q in range(4):
+        for a in range(4):
+            part = src[24 * (4 * a + q) : 24 * (4 * a + q) + 24]
+            if a < 3:
+                b[a, start + q] = part
+            else:
+                m[start + q] = part
+    for q in range(5):
+        k[k_start + q] = src[384 + 32 * q : 416 + 32 * q]
+
+
+def fine_near_kernel(place, load, k_own, m_own, y_low, y_high, partner, *refs):
+    b, u, k, m, message, co_out, first, k1, sums, tmp = refs
+    odd = place[0] & 1
+
+    def own(z):
+        p = z + 5
+        for c in range(3):
+            b[c, p, 0:4] = y_low[z, 4 * c : 4 * c + 4]
+            b[c, p, 4:20] = load[c, z]
+            b[c, p, 20:24] = y_high[z, 4 * c : 4 * c + 4]
+        m[p, 0:4] = y_low[z, 12:16]
+        m[p, 4:20] = m_own[z]
+        m[p, 20:24] = y_high[z, 12:16]
+        k[p, 0:8] = y_low[z, 16:24]
+        k[p, 8:24] = k_own[z]
+        k[p, 24:32] = y_high[z, 16:24]
+
+    each((0, 16), own)
+    place_planes(partner.at[1 - odd], 1 - odd, b, m, k)
+    fine_part(odd, True, *refs)
+
+
+def fine_far_kernel(place, cross, *refs):
+    refs = refs[9:]
+    b, u, k, m, message, co_out, first, k1, sums, tmp = refs
+    odd = place[0] & 1
+    place_planes(cross, odd, b, m, k)
+    fine_part(odd, False, *refs)
+    odd_lane = (lanes_of(8) & 1) != 0
     for z1 in range(4):
         message[16 + z1] = jnp.where(odd_lane, sums[z1 + 4], sums[z1])
 
 
-def middle_kernel(place, own, partner, cross,
-                  b1_out, u1_out, k1_out, t1_out, b2, k2, u2b, packed, co2_out,
-                  b1, u1, k1, t1, cx, cy, cz, e, w, first, u2a, tmp):
-    co = (cx, cy, cz, e, w)
-    lane = lanes_of(24)
-    odd_lane = (lane & 1) != 0
-    odd = place[0] & 1
-    for src, start in ((own, 8), (partner.at[1 - odd], 16 * (1 - odd)), (cross, 16 * odd)):
-        for q in range(8):
-            p = start + q
-            v = src[q]
-            b1[0, p] = jnp.where(odd_lane, lane_prev(v, 1), v)
-            b1[1, p] = jnp.where(odd_lane, v, lane_next(v, 1))
-            v = src[8 + q]
-            b1[2, p] = jnp.where(odd_lane, lane_prev(v, 1), v)
-            k1[p] = jnp.where(odd_lane, v, lane_next(v, 1))
-        for q in range(4):
-            v = src[16 + q]
-            t1[start + q] = jnp.where(odd_lane, lane_prev(v, 1), v)
-            t1[start + 4 + q] = jnp.where(odd_lane, v, lane_next(v, 1))
-    k1[24] = jnp.zeros((24, 128), F32)
+def middle_part(odd, near, b1, u1, k1, t1, co_out, first, b2, k2, tmp):
+    co = tuple(co_out.at[n] for n in range(5))
+    even = 1 - odd
+    if near:
+        (c_low, c_count), (s_low, s_count) = (8 * even, 16), (1 + 8 * even, 14)
+        (k_low, k_count), (d_low, d_count) = (4 * even, 8), (1 + 4 * even, 6)
+    else:
+        (c_low, c_count), (s_low, s_count) = (15 * odd, 9), (1 + 14 * odd, 8)
+        (k_low, k_count), (d_low, d_count) = (8 * odd, 4), (1 + 6 * odd, 4)
 
     def fill(p):
         for ref, v in zip(co, coefficients(k1[p], None, k1[p + 1], 0.25, 2, None, t1[p])):
             ref[p] = v
         for c in range(3):
-            first[c, p] = w[p] * b1[c, p]
-
-    each((0, 24), fill)
-    sweep((1, 23), b1, first, u1, k1, co, 2)
+            first[c, p] = co[4][p] * b1[c, p]
+
+    each((c_low, None, c_count), fill)
+    sweep((s_low, None, s_count), b1, first, u1, k1, co, 2)
+
+    def coarse_k(q2, s):
+        k2[q2, 4:16] = block_mean(k1[2 * q2], k1[2 * q2 + 1], tmp.at[s], 2)
+        k2[q2, 0:4] = jnp.zeros((4, 128), F32)
+
+    span(k_low, k_count, coarse_k, 4)
+
+    def down(q2, s):
+        rests = [left_over(p, b1, u1, k1, co, 2)[1] for p in (2 * q2, 2 * q2 + 1)]
+        for c in range(3):
+            b2[c, q2, 4:16] = block_mean(rests[0][c], rests[1][c], tmp.at[3 * s + c], 2)
+            b2[c, q2, 0:4] = jnp.zeros((4, 128), F32)
+
+    span(d_low, d_count, down, 3 if near else 4)
+
+
+def take(src, start, b1, k1, t1):
+    odd_lane = (lanes_of(24) & 1) != 0
+    for q in range(8):
+        p = start + q
+        v = src[q]
+        b1[0, p] = jnp.where(odd_lane, lane_prev(v, 1), v)
+        b1[1, p] = jnp.where(odd_lane, v, lane_next(v, 1))
+        v = src[8 + q]
+        b1[2, p] = jnp.where(odd_lane, lane_prev(v, 1), v)
+        k1[p] = jnp.where(odd_lane, v, lane_next(v, 1))
+    for q in range(4):
+        v = src[16 + q]
+        t1[start + q] = jnp.where(odd_lane, lane_prev(v, 1), v)
+        t1[start + 4 + q] = jnp.where(odd_lane, v, lane_next(v, 1))
+
+
+def middle_near_kernel(place, own, partner, *refs):
+    b1, u1, k1, t1 = refs[:4]
+    odd = place[0] & 1
+    take(own, 8, b1, k1, t1)
+    take(partner.at[1 - odd], 16 * (1 - odd), b1, k1, t1)
+    k1[24] = jnp.zeros((24, 128), F32)
+    middle_part(odd, True, *refs)
+
+
+def middle_far_kernel(place, cross, *refs):
+    refs = refs[8:]
+    b1, u1, k1, t1, co_out, first, b2, k2 = refs[:8]
+    b1_out, u1_out, k1_out, t1_out, u2b, packed, co2_out, u2a, tmp = refs[8:]
+    odd = place[0] & 1
+    take(cross, 16 * odd, b1, k1, t1)
+    middle_part(odd, False, b1, u1, k1, t1, co_out, first, b2, k2, tmp)
+
     def keep(p):
         k1_out[p] = k1[p + 4, 4:20]
         t1_out[p] = t1[p + 4, 4:20]
@@ -304,20 +369,6 @@
             u1_out[c, p] = u1[c, p + 4, 4:20]
 
     each((0, 16), keep)
-
-    def coarse_k(q2, s):
-        k2[q2, 4:16] = block_mean(k1[2 * q2], k1[2 * q2 + 1], tmp.at[s], 2)
-        k2[q2, 0:4] = jnp.zeros((4, 128), F32)
-
-    loop(0, 12, coarse_k, 6)
-
-    def down(q2, s):
-        rests = [left_over(p, b1, u1, k1, co, 2)[1] for p in (2 * q2, 2 * q2 + 1)]
-        for c in range(3):
-            b2[c, q2, 4:16] = block_mean(rests[0][c], rests[1][c], tmp.at[3 * s + c], 2)
-            b2[c, q2, 0:4] = jnp.zeros((4, 128), F32)
-
-    loop(1, 11, down, 5)
     co2 = tuple(co2_out.at[n] for n in range(5))
     fill_coefficients(k2, co2, (1, 11), 0.0625, 4)
     co2[2][0] = (0.5 * 0.0625) * (k2[0] + k2[1])
@@ -539,7 +590,7 @@
     return jax.ShapeDtypeStruct(shape, F32)
 
 
-def call(kernel, name, outs, scratch, *args, smem=0):
+def call(kernel, name, outs, scratch, *args, smem=0, alias=None, flops=0):
     vmem = pl.BlockSpec(memory_space=pltpu.VMEM)
     specs = [pl.BlockSpec(memory_space=pltpu.SMEM)] * smem
     return pl.pallas_call(
@@ -549,6 +600,8 @@
         in_specs=specs + [vmem] * (len(args) - len(specs)),
         out_specs=jax.tree.map(lambda _: vmem, outs),
         scratch_shapes=[pltpu.VMEM(s, F32) for s in scratch],
+        input_output_aliases=alias or {},
+        cost_estimate=pl.CostEstimate(flops=flops, bytes_accessed=flops, transcendentals=0) if flops else None,
         compiler_params=pltpu.CompilerParams(vmem_limit_bytes=40 * 1024 * 1024),
     )(*args)
 
@@ -582,12 +635,16 @@
     )
     partner, cross = slab_neighbours(to_partner, to_cross)
     part0, full0, full0v = (26, 24, 128), (26, 32, 128), (3, 26, 24, 128)
-    b0, u0, k0, m0, message, co0 = call(
-        fine_kernel, "fine",
-        (struct(*full0v), struct(*full0v), struct(*full0), struct(*part0), struct(20, 8, 128),
-         struct(5, *part0)),
-        [full0v, (10, 16, 128), (8, 8, 128), (16, 48, 128)],
-        place, raw, k, m, y_low, y_high, partner, cross, smem=1,
+    kept = (struct(*full0v), struct(*full0v), struct(*full0), struct(*part0), struct(20, 8, 128),
+            struct(5, *part0), struct(*full0v), struct(10, 16, 128), struct(8, 8, 128))
+    rows = [(16, 48, 128)]
+    near = call(
+        fine_near_kernel, "fine_near", kept, rows, place, raw, k, m, y_low, y_high, partner,
+        smem=1, flops=8_000_000,
+    )
+    b0, u0, k0, m0, message, co0, *_ = call(
+        fine_far_kernel, "fine_far", kept, rows, place, cross, *near,
+        smem=1, alias={2 + n: n for n in range(len(kept))},
     )
     y_low = shift(message, "col", COL, 1)
     y_high = shift(message, "col", COL, -1)
@@ -596,13 +653,19 @@
     full1, full1v, more1 = (24, 24, 128), (3, 24, 24, 128), (25, 24, 128)
     part1, part1v = (16, 16, 128), (3, 16, 16, 128)
     full2, full2v = (12, 16, 128), (3, 12, 16, 128)
-    b1, u1, k1, t1, b2, k2, u2, packed, co2 = call(
-        middle_kernel, "middle",
-        (struct(*part1v), struct(*part1v), struct(*part1), struct(*part1), struct(*full2v), struct(*full2),
-         struct(*full2v), struct(COL, 8, 128), struct(5, *full2)),
-        [full1v, full1v, more1, full1] + [full1] * 5 + [full1v] + [full2v, (16, 48, 128)],
-        place, wide, partner, cross, smem=1,
-    )
+    kept = (struct(*full1v), struct(*full1v), struct(*more1), struct(*full1), struct(5, *full1), struct(*full1v),
+            struct(*full2v), struct(*full2))
+    near = call(
+        middle_near_kernel, "middle_near", kept, rows, place, wide, partner, smem=1, flops=8_000_000
+    )
+    outs = call(
+        middle_far_kernel, "middle_far",
+        kept + (struct(*part1v), struct(*part1v), struct(*part1), struct(*part1), struct(*full2v),
+                struct(COL, 8, 128), struct(5, *full2)),
+        [full2v] + rows, place, cross, *near,
+        smem=1, alias={2 + n: n for n in range(len(kept))},
+    )
+    b2, k2, b1, u1, k1, t1, u2, packed, co2 = outs[6:]
     received = lax.all_to_all(packed, "col", 0, 0)
     window = call(window_kernel, "window", struct(SLAB // 2, 48, 128), [(48, 128)], place, received, u2, smem=1)
     groups = [list(range(par, SLAB, 2)) for par in range(2)]

time: 105 us -> 101 us (0.962)
  waiting for transfers between devices: 15.1 us -> 12 us
  blocking collectives: 46.5 us -> 44.9 us
  Pallas kernels: 18.4 us -> 19.7 us
    ppermute x2, waiting for transfers between devices: 3.72 us -> 0.01 us  [slab_neighbours(): cross = lax.ppermute(to_cross, 'slab', pairs)]
    pallas_call x6 -> x8, Pallas kernels: 18.4 us -> 19.7 us  [call(): pl.pallas_call(kernel, name=name, out_shape=outs, in_specs=specs + [vmem]...]
    all_to_all x1, blocking collectives: 15.8 us -> 14.7 us  [on_device(): received = lax.all_to_all(window, 'slab', 0, 0, axis_index_groups=groups)]
  transfers between devices with their start and end apart: 6 -> 6, of which waited for: 6 -> 4; matrix products, arithmetic and copies ran while one was open for 0% -> 0% of each run, Pallas kernels for 0% -> 6%
where the time goes in v4:
time: 101 us
  blocking collectives  44.9 us (44%)
  starting transfers between devices  21.3 us (21%)
  Pallas kernels  19.7 us (20%)
  waiting for transfers between devices  12 us (12%)
  other arithmetic  2.11 us (2%)
    pallas_call x8, Pallas kernels, call(): pl.pallas_call(kernel, name=name, out_shape=outs, in_specs=specs + [vmem]...  19.7 us
    all_to_all x1, blocking collectives, on_device(): received = lax.all_to_all(packed, 'col', 0, 0)  19.4 us
    all_to_all x1, blocking collectives, on_device(): received = lax.all_to_all(window, 'slab', 0, 0, axis_index_groups=groups)  14.7 us
    ppermute x4, waiting for transfers between devices, shift(): return lax.ppermute(block, axis, pairs)  12 us
    ppermute x4, starting transfers between devices, shift(): return lax.ppermute(block, axis, pairs)  11.4 us
    ppermute x2, starting transfers between devices, slab_neighbours(): cross = lax.ppermute(to_cross, 'slab', pairs)  9.92 us
    all_gather x1, blocking collectives, on_device(): lax.all_gather(received, 'slab', axis_index_groups=[[i, i + 1] for i in r...  6.37 us
    all_gather x2, blocking collectives, slab_neighbours(): return (lax.all_gather(to_partner, 'slab', axis_index_groups=groups), cross)  4.36 us
  transfers between devices with their start and end apart: 6, of which 4 were waited for; matrix products, arithmetic and copies ran while one was open for 0% of the time, Pallas kernels for 6%

profile of v4, /device:TPU:1, one launch (start us, length us, event | category | flops | bytes accessed | tf_op | source)
XLA Modules:
  0.0 100.8 jit_solution(13378517621498559498)
XLA Ops:
  0.6 0.0 copy-start
  0.6 1.0 convert_bitcast_fusion
  1.6 1.0 %pad_maximum_fusion.raw.load = f32[5,16,16,128]{3,2,1,0:T(8,128)S(1)} fusion(f32[1,16,16,128]{3,2,1,0:T(8,128)S(1)} %get-tuple-element.78, f32[1,16,16,128]{3,2,1,0:T(8,128)S(1)} %get-tuple-element.79, f32[3,16,16,128]{3,2,1,0:T(8,128)} %param.4), kind=kLoop, calls=%fused_computation | loop fusion | flops 327680 | bytes 1310720 | tf_op jit(solution)/shard_map/concatenate | solution.py:626
  2.7 0.0 copy-done
  2.7 0.6 prep.1
  3.3 4.8 %collective-permute-start = (f32[16,24,128]{2,1,0:T(8,128)S(1)}, f32[16,24,128]{2,1,0:T(8,128)S(1)}, u32[]{:S(2)}, u32[]{:S(2)}) collective-permute-start(f32[16,24,128]{2,1,0:T(8,128)S(1)} %get-tuple-element.42), channel_id=1, source_target_pairs={{0,1},{1,2},{2,3},{3,4},{4,5},{5,6},{6,7},{7,8},{8,9},{9,10},{10,1... | collective-permute-start | bytes 589832 | tf_op jit(solution)/shard_map/ppermute | solution.py:611
  8.2 1.3 %collective-permute-start.1 = (f32[16,24,128]{2,1,0:T(8,128)S(1)}, f32[16,24,128]{2,1,0:T(8,128)S(1)}, u32[]{:S(2)}, u32[]{:S(2)}) collective-permute-start(f32[16,24,128]{2,1,0:T(8,128)S(1)} %get-tuple-element.43), channel_id=1, source_target_pairs={{1,0},{2,1},{3,2},{4,3},{5,4},{6,5},{7,6},{8,7},{9,8},{10,9},{11,1... | collective-permute-start | bytes 589832 | tf_op jit(solution)/shard_map/ppermute | solution.py:611
  9.5 0.1 pad_add_fusion.place
  9.6 1.2 %collective-permute-done.from_low.y_low = f32[16,24,128]{2,1,0:T(8,128)S(1)} collective-permute-done((f32[16,24,128]{2,1,0:T(8,128)S(1)}, f32[16,24,128]{2,1,0:T(8,128)S(1)}, u32[]{:S(2)}, u32[]{:S(2)}) %collective-permute-start) | collective-permute-done | bytes 196640 | tf_op jit(solution)/shard_map/ppermute | solution.py:611
  10.8 4.5 %collective-permute-done.1.from_high.y_high = f32[16,24,128]{2,1,0:T(8,128)S(1)} collective-permute-done((f32[16,24,128]{2,1,0:T(8,128)S(1)}, f32[16,24,128]{2,1,0:T(8,128)S(1)}, u32[]{:S(2)}, u32[]{:S(2)}) %collective-permute-start.1) | collective-permute-done | bytes 196640 | tf_op jit(solution)/shard_map/ppermute | solution.py:611
  15.2 0.6 planes.1
  15.8 5.9 %collective-permute-start.2 = (f32[544,128]{1,0:T(8,128)S(1)}, f32[544,128]{1,0:T(8,128)S(1)}, u32[]{:S(2)}, u32[]{:S(2)}) collective-permute-start(f32[544,128]{1,0:T(8,128)S(1)} %get-tuple-element.44), channel_id=1, source_target_pairs={{32,64},{64,32},{96,128},{128,96},{160,192},{192,160},{224,256},{2... | collective-permute-start | bytes 835592 | tf_op jit(solution)/shard_map/ppermute | solution.py:618
  21.7 2.2 %all-gather = f32[1088,128]{1,0:T(8,128)S(1)} all-gather(f32[544,128]{1,0:T(8,128)S(1)} %get-tuple-element.45), channel_id=2, replica_groups={{0,32},{64,96},{128,160},{192,224},{256,288},{320,352},{384,416},{448,4..., dimensions={0}, use_global_device_ids=true | all-gather | bytes 835584 | tf_op jit(solution)/shard_map/all_gather | solution.py:620
  23.9 2.9 %fine_near.1 = (f32[3,26,24,128]{3,2,1,0:T(8,128)S(1)}, f32[3,26,24,128]{3,2,1,0:T(8,128)S(1)}, f32[26,32,128]{2,1,0:T(8,128)S(1)}, f32[26,24,128]{2,1,0:T(8,128...) custom-call(s32[2]{0:T(128)S(1)} %pad_add_fusion.place, ...), custom_call_target="tpu_custom_call" | custom-call | flops 8000000 | bytes 8000000 | tf_op jit(solution)/shard_map/fine_near/pallas_call | solution.py:596
  26.9 0.0 collective-permute-done.2.cross
  26.9 1.2 %fine_far.1 = (f32[3,26,24,128]{3,2,1,0:T(8,128)S(1)}, f32[3,26,24,128]{3,2,1,0:T(8,128)S(1)}, f32[26,32,128]{2,1,0:T(8,128)S(1)}, f32[26,24,128]{2,1,0:T(8,128)...) custom-call(s32[2]{0:T(128)S(1)} %pad_add_fusion.place, ...), custom_call_target="tpu_custom_call", output_to_operand_aliasing={{0}: (2, {}), {1}: (3, {}), {2}: (4, {}), {3}: (5, {}), {4}... | custom-call | tf_op jit(solution)/shard_map/fine_far/pallas_call | solution.py:596
  28.1 4.0 %collective-permute-start.3 = (f32[20,8,128]{2,1,0:T(8,128)S(1)}, f32[20,8,128]{2,1,0:T(8,128)S(1)}, u32[]{:S(2)}, u32[]{:S(2)}) collective-permute-start(f32[20,8,128]{2,1,0:T(8,128)S(1)} %get-tuple-element.55), channel_id=1, source_target_pairs={{0,1},{1,2},{2,3},{3,4},{4,5},{5,6},{6,7},{7,8},{8,9},{9,10},{10,1... | collective-permute-start | bytes 245768 | tf_op jit(solution)/shard_map/ppermute | solution.py:611
  32.1 1.3 %collective-permute-start.4 = (f32[20,8,128]{2,1,0:T(8,128)S(1)}, f32[20,8,128]{2,1,0:T(8,128)S(1)}, u32[]{:S(2)}, u32[]{:S(2)}) collective-permute-start(f32[20,8,128]{2,1,0:T(8,128)S(1)} %get-tuple-element.55), channel_id=1, source_target_pairs={{1,0},{2,1},{3,2},{4,3},{5,4},{6,5},{7,6},{8,7},{9,8},{10,9},{11,1... | collective-permute-start | bytes 245768 | tf_op jit(solution)/shard_map/ppermute | solution.py:611
  33.4 0.4 collective-permute-done.3
  33.8 5.9 %collective-permute-done.4 = f32[20,8,128]{2,1,0:T(8,128)S(1)} collective-permute-done((f32[20,8,128]{2,1,0:T(8,128)S(1)}, f32[20,8,128]{2,1,0:T(8,128)S(1)}, u32[]{:S(2)}, u32[]{:S(2)}) %collective-permute-start.4) | collective-permute-done | bytes 81952 | tf_op jit(solution)/shard_map/ppermute | solution.py:611
  39.8 4.0 %collective-permute-start.5 = (f32[20,24,128]{2,1,0:T(8,128)S(1)}, f32[20,24,128]{2,1,0:T(8,128)S(1)}, u32[]{:S(2)}, u32[]{:S(2)}) collective-permute-start(f32[20,24,128]{2,1,0:T(8,128)S(1)} %constant_dynamic-update-slice_fusion.own), channel_id=1, source_target_pairs={{32,64},{64,32},{96,128},{128,96},{160,192},{192,160},{224,256},{2... | collective-permute-start | bytes 737288 | tf_op jit(solution)/shard_map/ppermute | solution.py:618
  43.8 2.2 %all-gather.1 = f32[40,24,128]{2,1,0:T(8,128)S(1)} all-gather(f32[20,24,128]{2,1,0:T(8,128)S(1)} %constant_dynamic-update-slice_fusion.own), channel_id=3, replica_groups={{0,32},{64,96},{128,160},{192,224},{256,288},{320,352},{384,416},{448,4..., dimensions={0}, use_global_device_ids=true | all-gather | bytes 737280 | tf_op jit(solution)/shard_map/all_gather | solution.py:620
  46.0 2.7 %middle_near.1 = (f32[3,24,24,128]{3,2,1,0:T(8,128)S(1)}, f32[3,24,24,128]{3,2,1,0:T(8,128)S(1)}, f32[25,24,128]{2,1,0:T(8,128)S(1)}, f32[24,24,128]{2,1,0:T(8,1...) custom-call(s32[2]{0:T(128)S(1)} %pad_add_fusion.place, ...), custom_call_target="tpu_custom_call" | custom-call | flops 8000000 | bytes 8000000 | tf_op jit(solution)/shard_map/middle_near/pallas_call | solution.py:596
  48.7 0.0 collective-permute-done.5.cross
  48.7 2.5 %middle_far.1 = (f32[3,24,24,128]{3,2,1,0:T(8,128)S(1)}, f32[3,24,24,128]{3,2,1,0:T(8,128)S(1)}, f32[25,24,128]{2,1,0:T(8,128)S(1)}, f32[24,24,128]{2,1,0:T(8,12...) custom-call(s32[2]{0:T(128)S(1)} %pad_add_fusion.place, ...), custom_call_target="tpu_custom_call", output_to_operand_aliasing={{0}: (2, {}), {1}: (3, {}), {2}: (4, {}), {3}: (5, {}), {4}... | custom-call | tf_op jit(solution)/shard_map/middle_far/pallas_call | solution.py:596
  51.2 19.4 %all_to_all.10.received = f32[32,8,128]{2,1,0:T(8,128)S(1)} all-to-all(f32[32,8,128]{2,1,0:T(8,128)S(1)} %get-tuple-element.64), channel_id=1, replica_groups=mesh['slab'=16,'col'=32] {'col'}, dimensions={0} | all-to-all | bytes 262144 | tf_op jit(solution)/shard_map/all_to_all | solution.py:669
  70.6 0.6 window.1
  71.2 14.7 %all_to_all.11 = f32[8,48,128]{2,1,0:T(8,128)S(1)} all-to-all(f32[8,48,128]{2,1,0:T(8,128)S(1)} %window.1), channel_id=1, replica_groups={{0,64,128,192,256,320,384,448},{32,96,160,224,288,352,416,480},{1,65,12..., dimensions={0} | all-to-all | bytes 393216 | tf_op jit(solution)/shard_map/all_to_all | solution.py:672
  86.0 6.4 %all-gather.2 = f32[16,48,128]{2,1,0:T(8,128)S(1)} all-gather(f32[8,48,128]{2,1,0:T(8,128)S(1)} %all_to_all.11), channel_id=4, replica_groups={{0,32},{64,96},{128,160},{192,224},{256,288},{320,352},{384,416},{448,4..., dimensions={0}, use_global_device_ids=true | all-gather | bytes 589824 | tf_op jit(solution)/shard_map/all_gather | solution.py:673
  92.3 8.5 %upper.1 = (f32[3,16,16,128]{3,2,1,0:T(8,128)}, f32[3,16,16,128]{3,2,1,0:T(8,128)}) custom-call(s32[2]{0:T(128)S(1)} %pad_add_fusion.place, f32[2,8,48,128]{3,2,1,0:T(8,128)S(1)} %bitcast.11, f32[3,12,16,128]{3,2,1,0:T(8,128)S(1)} %get-tuple-element.65.u2, f32[3,12,16,128]{3,2,1,0:T(8,128)S(1)} %get-tuple-element.66.b2, ...), custom_call_target="tpu_custom_call" | custom-call | tf_op jit(solution)/shard_map/upper/pallas_call | solution.py:596
  (3 shorter events, 0.0 us)
Async XLA Ops:
  0.6 2.1 %copy-start = (f32[8]{0:T(128)S(1)}, f32[8]{0:T(128)}, u32[]{:S(2)}) copy-start(f32[8]{0:T(128)} %moduli.1) | copy-start | bytes 100
  3.3 7.4 %collective-permute-start = (f32[16,24,128]{2,1,0:T(8,128)S(1)}, f32[16,24,128]{2,1,0:T(8,128)S(1)}, u32[]{:S(2)}, u32[]{:S(2)}) collective-permute-start(f32[16,24,128]{2,1,0:T(8,128)S(1)} %get-tuple-element.42), channel_id=1, source_target_pairs={{0,1},{1,2},{2,3},{3,4},{4,5},{5,6},{6,7},{7,8},{8,9},{9,10},{10,1... | collective-permute-start | bytes 589832 | tf_op jit(solution)/shard_map/ppermute | solution.py:611
  8.2 7.0 %collective-permute-start.1 = (f32[16,24,128]{2,1,0:T(8,128)S(1)}, f32[16,24,128]{2,1,0:T(8,128)S(1)}, u32[]{:S(2)}, u32[]{:S(2)}) collective-permute-start(f32[16,24,128]{2,1,0:T(8,128)S(1)} %get-tuple-element.43), channel_id=1, source_target_pairs={{1,0},{2,1},{3,2},{4,3},{5,4},{6,5},{7,6},{8,7},{9,8},{10,9},{11,1... | collective-permute-start | bytes 589832 | tf_op jit(solution)/shard_map/ppermute | solution.py:611
  15.8 11.0 %collective-permute-start.2 = (f32[544,128]{1,0:T(8,128)S(1)}, f32[544,128]{1,0:T(8,128)S(1)}, u32[]{:S(2)}, u32[]{:S(2)}) collective-permute-start(f32[544,128]{1,0:T(8,128)S(1)} %get-tuple-element.44), channel_id=1, source_target_pairs={{32,64},{64,32},{96,128},{128,96},{160,192},{192,160},{224,256},{2... | collective-permute-start | bytes 835592 | tf_op jit(solution)/shard_map/ppermute | solution.py:618
  28.1 5.7 %collective-permute-start.3 = (f32[20,8,128]{2,1,0:T(8,128)S(1)}, f32[20,8,128]{2,1,0:T(8,128)S(1)}, u32[]{:S(2)}, u32[]{:S(2)}) collective-permute-start(f32[20,8,128]{2,1,0:T(8,128)S(1)} %get-tuple-element.55), channel_id=1, source_target_pairs={{0,1},{1,2},{2,3},{3,4},{4,5},{5,6},{6,7},{7,8},{8,9},{9,10},{10,1... | collective-permute-start | bytes 245768 | tf_op jit(solution)/shard_map/ppermute | solution.py:611
  32.1 7.7 %collective-permute-start.4 = (f32[20,8,128]{2,1,0:T(8,128)S(1)}, f32[20,8,128]{2,1,0:T(8,128)S(1)}, u32[]{:S(2)}, u32[]{:S(2)}) collective-permute-start(f32[20,8,128]{2,1,0:T(8,128)S(1)} %get-tuple-element.55), channel_id=1, source_target_pairs={{1,0},{2,1},{3,2},{4,3},{5,4},{6,5},{7,6},{8,7},{9,8},{10,9},{11,1... | collective-permute-start | bytes 245768 | tf_op jit(solution)/shard_map/ppermute | solution.py:611
  39.8 8.9 %collective-permute-start.5 = (f32[20,24,128]{2,1,0:T(8,128)S(1)}, f32[20,24,128]{2,1,0:T(8,128)S(1)}, u32[]{:S(2)}, u32[]{:S(2)}) collective-permute-start(f32[20,24,128]{2,1,0:T(8,128)S(1)} %constant_dynamic-update-slice_fusion.own), channel_id=1, source_target_pairs={{32,64},{64,32},{96,128},{128,96},{160,192},{192,160},{224,256},{2... | collective-permute-start | bytes 737288 | tf_op jit(solution)/shard_map/ppermute | solution.py:618

commit v5 on v4

--- a/solution.py
+++ b/solution.py
@@ -409,17 +409,17 @@
         for q, peer in ((0, c - 1), (1, c + 1)):
             inside = jnp.logical_and(peer >= 0, peer < COL).astype(F32)
             part = received[jnp.clip(peer, 0, COL - 1), 2 + 2 * comp : 4 + 2 * comp]
-            base = 22 + 4 * comp + 2 * q
+            base = 24 + 4 * comp + 2 * q
             tmp[base : base + 2] = inside * part
     quad = lanes_of(4) & 3
-    tmp[46:48] = jnp.zeros((2, 128), F32)
+    tmp[22:24] = jnp.zeros((2, 128), F32)
 
     def inner(near):
         for comp in range(3):
             a = [u2[comp, 4 + near + f, 6:10] for f in range(2)]
             b = [u2[comp, 4 + near + f, 10:14] for f in range(2)]
             v = jnp.where(quad == 0, a[0], jnp.where(quad == 1, a[1], jnp.where(quad == 2, b[0], b[1])))
-            tmp[34 + 4 * comp : 38 + 4 * comp] = v
+            tmp[36 + 4 * comp : 40 + 4 * comp] = v
         return tmp[...]
 
     to_high = inner(0)
@@ -494,19 +494,20 @@
 
     c2 = tuple(co2.at[n] for n in range(5))
     lane8 = lanes_of(8)
-    lane4 = lanes_of(4)
+    lane12 = lanes_of(12)
 
     def outer(g, carry):
         peer = d - 1 + g
         inside = jnp.logical_and(peer >= 0, peer < SLAB)
         peer = jnp.clip(peer, 0, SLAB - 1)
+        rows = received[peer & 1, peer // 2, 24:36]
         for zz in range(4):
-            pick = jnp.logical_and((lane4 & 3) == zz, inside)
+            pick = jnp.logical_and((lane12 & 3) == zz, inside)
+            v = spread(jnp.where(pick, rows, 0.0), lane12, 4)
             for c in range(3):
-                v = spread(jnp.where(pick, received[peer & 1, peer // 2, 22 + 4 * c : 26 + 4 * c], 0.0), lane4, 4)
                 u2a[c, 4 * g + zz, 0:4] = jnp.zeros((4, 128), F32)
-                u2a[c, 4 * g + zz, 4:6] = v[0:2]
-                u2a[c, 4 * g + zz, 14:16] = v[2:4]
+                u2a[c, 4 * g + zz, 4:6] = v[4 * c : 4 * c + 2]
+                u2a[c, 4 * g + zz, 14:16] = v[4 * c + 2 : 4 * c + 4]
         return carry
 
     lax.fori_loop(0, 3, outer, 0)
@@ -521,12 +522,13 @@
         peer = d - 1 + 2 * g
         inside = jnp.logical_and(peer >= 0, peer < SLAB)
         peer = jnp.clip(peer, 0, SLAB - 1)
-        for c in range(3):
-            v = received[peer & 1, peer // 2, 34 + 4 * c : 38 + 4 * c]
-            for f in range(2):
-                for half in range(2):
-                    pick = jnp.logical_and((lane4 & 3) == 2 * half + f, inside)
-                    u2a[c, 10 * g + f, 6 + 4 * half : 10 + 4 * half] = spread(jnp.where(pick, v, 0.0), lane4, 4)
+        rows = received[peer & 1, peer // 2, 36:48]
+        for f in range(2):
+            for half in range(2):
+                pick = jnp.logical_and((lane12 & 3) == 2 * half + f, inside)
+                v = spread(jnp.where(pick, rows, 0.0), lane12, 4)
+                for c in range(3):
+                    u2a[c, 10 * g + f, 6 + 4 * half : 10 + 4 * half] = v[4 * c : 4 * c + 4]
         return carry
 
     lax.fori_loop(0, 2, far, 0)

time: 101 us -> 101 us (level)
  no operation moved by 1% of the time
where the time goes in v5:
time: 101 us
  blocking collectives  44.9 us (44%)
  starting transfers between devices  21.3 us (21%)
  Pallas kernels  19.6 us (19%)
  waiting for transfers between devices  12 us (12%)
  other arithmetic  2.11 us (2%)
    pallas_call x8, Pallas kernels, call(): pl.pallas_call(kernel, name=name, out_shape=outs, in_specs=specs + [vmem]...  19.6 us
    all_to_all x1, blocking collectives, on_device(): received = lax.all_to_all(packed, 'col', 0, 0)  19.4 us
    all_to_all x1, blocking collectives, on_device(): received = lax.all_to_all(window, 'slab', 0, 0, axis_index_groups=groups)  14.7 us
    ppermute x4, waiting for transfers between devices, shift(): return lax.ppermute(block, axis, pairs)  12 us
    ppermute x4, starting transfers between devices, shift(): return lax.ppermute(block, axis, pairs)  11.4 us
    ppermute x2, starting transfers between devices, slab_neighbours(): cross = lax.ppermute(to_cross, 'slab', pairs)  9.92 us
    all_gather x1, blocking collectives, on_device(): lax.all_gather(received, 'slab', axis_index_groups=[[i, i + 1] for i in r...  6.37 us
    all_gather x2, blocking collectives, slab_neighbours(): return (lax.all_gather(to_partner, 'slab', axis_index_groups=groups), cross)  4.36 us
  transfers between devices with their start and end apart: 6, of which 4 were waited for; matrix products, arithmetic and copies ran while one was open for 0% of the time, Pallas kernels for 6%

profile of v5, /device:TPU:1, one launch (start us, length us, event | category | flops | bytes accessed | tf_op | source)
XLA Modules:
  0.0 100.8 jit_solution(9443104377205142075)
XLA Ops:
  0.6 0.0 copy-start
  0.6 1.0 convert_bitcast_fusion
  1.6 1.0 %pad_maximum_fusion.raw.load = f32[5,16,16,128]{3,2,1,0:T(8,128)S(1)} fusion(f32[1,16,16,128]{3,2,1,0:T(8,128)S(1)} %get-tuple-element.78, f32[1,16,16,128]{3,2,1,0:T(8,128)S(1)} %get-tuple-element.79, f32[3,16,16,128]{3,2,1,0:T(8,128)} %param.4), kind=kLoop, calls=%fused_computation | loop fusion | flops 327680 | bytes 1310720 | tf_op jit(solution)/shard_map/concatenate | solution.py:628
  2.7 0.0 copy-done
  2.7 0.6 prep.1
  3.3 4.8 %collective-permute-start = (f32[16,24,128]{2,1,0:T(8,128)S(1)}, f32[16,24,128]{2,1,0:T(8,128)S(1)}, u32[]{:S(2)}, u32[]{:S(2)}) collective-permute-start(f32[16,24,128]{2,1,0:T(8,128)S(1)} %get-tuple-element.42), channel_id=1, source_target_pairs={{0,1},{1,2},{2,3},{3,4},{4,5},{5,6},{6,7},{7,8},{8,9},{9,10},{10,1... | collective-permute-start | bytes 589832 | tf_op jit(solution)/shard_map/ppermute | solution.py:613
  8.2 1.3 %collective-permute-start.1 = (f32[16,24,128]{2,1,0:T(8,128)S(1)}, f32[16,24,128]{2,1,0:T(8,128)S(1)}, u32[]{:S(2)}, u32[]{:S(2)}) collective-permute-start(f32[16,24,128]{2,1,0:T(8,128)S(1)} %get-tuple-element.43), channel_id=1, source_target_pairs={{1,0},{2,1},{3,2},{4,3},{5,4},{6,5},{7,6},{8,7},{9,8},{10,9},{11,1... | collective-permute-start | bytes 589832 | tf_op jit(solution)/shard_map/ppermute | solution.py:613
  9.5 0.1 pad_add_fusion.place
  9.6 1.2 %collective-permute-done.from_low.y_low = f32[16,24,128]{2,1,0:T(8,128)S(1)} collective-permute-done((f32[16,24,128]{2,1,0:T(8,128)S(1)}, f32[16,24,128]{2,1,0:T(8,128)S(1)}, u32[]{:S(2)}, u32[]{:S(2)}) %collective-permute-start) | collective-permute-done | bytes 196640 | tf_op jit(solution)/shard_map/ppermute | solution.py:613
  10.8 4.5 %collective-permute-done.1.from_high.y_high = f32[16,24,128]{2,1,0:T(8,128)S(1)} collective-permute-done((f32[16,24,128]{2,1,0:T(8,128)S(1)}, f32[16,24,128]{2,1,0:T(8,128)S(1)}, u32[]{:S(2)}, u32[]{:S(2)}) %collective-permute-start.1) | collective-permute-done | bytes 196640 | tf_op jit(solution)/shard_map/ppermute | solution.py:613
  15.2 0.6 planes.1
  15.8 5.9 %collective-permute-start.2 = (f32[544,128]{1,0:T(8,128)S(1)}, f32[544,128]{1,0:T(8,128)S(1)}, u32[]{:S(2)}, u32[]{:S(2)}) collective-permute-start(f32[544,128]{1,0:T(8,128)S(1)} %get-tuple-element.44), channel_id=1, source_target_pairs={{32,64},{64,32},{96,128},{128,96},{160,192},{192,160},{224,256},{2... | collective-permute-start | bytes 835592 | tf_op jit(solution)/shard_map/ppermute | solution.py:620
  21.7 2.2 %all-gather = f32[1088,128]{1,0:T(8,128)S(1)} all-gather(f32[544,128]{1,0:T(8,128)S(1)} %get-tuple-element.45), channel_id=2, replica_groups={{0,32},{64,96},{128,160},{192,224},{256,288},{320,352},{384,416},{448,4..., dimensions={0}, use_global_device_ids=true | all-gather | bytes 835584 | tf_op jit(solution)/shard_map/all_gather | solution.py:622
  23.9 2.9 %fine_near.1 = (f32[3,26,24,128]{3,2,1,0:T(8,128)S(1)}, f32[3,26,24,128]{3,2,1,0:T(8,128)S(1)}, f32[26,32,128]{2,1,0:T(8,128)S(1)}, f32[26,24,128]{2,1,0:T(8,128...) custom-call(s32[2]{0:T(128)S(1)} %pad_add_fusion.place, ...), custom_call_target="tpu_custom_call" | custom-call | flops 8000000 | bytes 8000000 | tf_op jit(solution)/shard_map/fine_near/pallas_call | solution.py:598
  26.9 0.0 collective-permute-done.2.cross
  26.9 1.2 %fine_far.1 = (f32[3,26,24,128]{3,2,1,0:T(8,128)S(1)}, f32[3,26,24,128]{3,2,1,0:T(8,128)S(1)}, f32[26,32,128]{2,1,0:T(8,128)S(1)}, f32[26,24,128]{2,1,0:T(8,128)...) custom-call(s32[2]{0:T(128)S(1)} %pad_add_fusion.place, ...), custom_call_target="tpu_custom_call", output_to_operand_aliasing={{0}: (2, {}), {1}: (3, {}), {2}: (4, {}), {3}: (5, {}), {4}... | custom-call | tf_op jit(solution)/shard_map/fine_far/pallas_call | solution.py:598
  28.1 4.0 %collective-permute-start.3 = (f32[20,8,128]{2,1,0:T(8,128)S(1)}, f32[20,8,128]{2,1,0:T(8,128)S(1)}, u32[]{:S(2)}, u32[]{:S(2)}) collective-permute-start(f32[20,8,128]{2,1,0:T(8,128)S(1)} %get-tuple-element.55), channel_id=1, source_target_pairs={{0,1},{1,2},{2,3},{3,4},{4,5},{5,6},{6,7},{7,8},{8,9},{9,10},{10,1... | collective-permute-start | bytes 245768 | tf_op jit(solution)/shard_map/ppermute | solution.py:613
  32.1 1.3 %collective-permute-start.4 = (f32[20,8,128]{2,1,0:T(8,128)S(1)}, f32[20,8,128]{2,1,0:T(8,128)S(1)}, u32[]{:S(2)}, u32[]{:S(2)}) collective-permute-start(f32[20,8,128]{2,1,0:T(8,128)S(1)} %get-tuple-element.55), channel_id=1, source_target_pairs={{1,0},{2,1},{3,2},{4,3},{5,4},{6,5},{7,6},{8,7},{9,8},{10,9},{11,1... | collective-permute-start | bytes 245768 | tf_op jit(solution)/shard_map/ppermute | solution.py:613
  33.4 0.4 collective-permute-done.3
  33.8 5.9 %collective-permute-done.4 = f32[20,8,128]{2,1,0:T(8,128)S(1)} collective-permute-done((f32[20,8,128]{2,1,0:T(8,128)S(1)}, f32[20,8,128]{2,1,0:T(8,128)S(1)}, u32[]{:S(2)}, u32[]{:S(2)}) %collective-permute-start.4) | collective-permute-done | bytes 81952 | tf_op jit(solution)/shard_map/ppermute | solution.py:613
  39.8 4.0 %collective-permute-start.5 = (f32[20,24,128]{2,1,0:T(8,128)S(1)}, f32[20,24,128]{2,1,0:T(8,128)S(1)}, u32[]{:S(2)}, u32[]{:S(2)}) collective-permute-start(f32[20,24,128]{2,1,0:T(8,128)S(1)} %constant_dynamic-update-slice_fusion.own), channel_id=1, source_target_pairs={{32,64},{64,32},{96,128},{128,96},{160,192},{192,160},{224,256},{2... | collective-permute-start | bytes 737288 | tf_op jit(solution)/shard_map/ppermute | solution.py:620
  43.8 2.2 %all-gather.1 = f32[40,24,128]{2,1,0:T(8,128)S(1)} all-gather(f32[20,24,128]{2,1,0:T(8,128)S(1)} %constant_dynamic-update-slice_fusion.own), channel_id=3, replica_groups={{0,32},{64,96},{128,160},{192,224},{256,288},{320,352},{384,416},{448,4..., dimensions={0}, use_global_device_ids=true | all-gather | bytes 737280 | tf_op jit(solution)/shard_map/all_gather | solution.py:622
  46.0 2.7 %middle_near.1 = (f32[3,24,24,128]{3,2,1,0:T(8,128)S(1)}, f32[3,24,24,128]{3,2,1,0:T(8,128)S(1)}, f32[25,24,128]{2,1,0:T(8,128)S(1)}, f32[24,24,128]{2,1,0:T(8,1...) custom-call(s32[2]{0:T(128)S(1)} %pad_add_fusion.place, ...), custom_call_target="tpu_custom_call" | custom-call | flops 8000000 | bytes 8000000 | tf_op jit(solution)/shard_map/middle_near/pallas_call | solution.py:598
  48.7 0.0 collective-permute-done.5.cross
  48.7 2.5 %middle_far.1 = (f32[3,24,24,128]{3,2,1,0:T(8,128)S(1)}, f32[3,24,24,128]{3,2,1,0:T(8,128)S(1)}, f32[25,24,128]{2,1,0:T(8,128)S(1)}, f32[24,24,128]{2,1,0:T(8,12...) custom-call(s32[2]{0:T(128)S(1)} %pad_add_fusion.place, ...), custom_call_target="tpu_custom_call", output_to_operand_aliasing={{0}: (2, {}), {1}: (3, {}), {2}: (4, {}), {3}: (5, {}), {4}... | custom-call | tf_op jit(solution)/shard_map/middle_far/pallas_call | solution.py:598
  51.2 19.4 %all_to_all.10.received = f32[32,8,128]{2,1,0:T(8,128)S(1)} all-to-all(f32[32,8,128]{2,1,0:T(8,128)S(1)} %get-tuple-element.64), channel_id=1, replica_groups=mesh['slab'=16,'col'=32] {'col'}, dimensions={0} | all-to-all | bytes 262144 | tf_op jit(solution)/shard_map/all_to_all | solution.py:671
  70.6 0.6 window.1
  71.2 14.7 %all_to_all.11 = f32[8,48,128]{2,1,0:T(8,128)S(1)} all-to-all(f32[8,48,128]{2,1,0:T(8,128)S(1)} %window.1), channel_id=1, replica_groups={{0,64,128,192,256,320,384,448},{32,96,160,224,288,352,416,480},{1,65,12..., dimensions={0} | all-to-all | bytes 393216 | tf_op jit(solution)/shard_map/all_to_all | solution.py:674
  86.0 6.4 %all-gather.2 = f32[16,48,128]{2,1,0:T(8,128)S(1)} all-gather(f32[8,48,128]{2,1,0:T(8,128)S(1)} %all_to_all.11), channel_id=4, replica_groups={{0,32},{64,96},{128,160},{192,224},{256,288},{320,352},{384,416},{448,4..., dimensions={0}, use_global_device_ids=true | all-gather | bytes 589824 | tf_op jit(solution)/shard_map/all_gather | solution.py:675
  92.3 8.4 %upper.1 = (f32[3,16,16,128]{3,2,1,0:T(8,128)}, f32[3,16,16,128]{3,2,1,0:T(8,128)}) custom-call(s32[2]{0:T(128)S(1)} %pad_add_fusion.place, f32[2,8,48,128]{3,2,1,0:T(8,128)S(1)} %bitcast.11, f32[3,12,16,128]{3,2,1,0:T(8,128)S(1)} %get-tuple-element.65.u2, f32[3,12,16,128]{3,2,1,0:T(8,128)S(1)} %get-tuple-element.66.b2, ...), custom_call_target="tpu_custom_call" | custom-call | tf_op jit(solution)/shard_map/upper/pallas_call | solution.py:598
  (3 shorter events, 0.0 us)
Async XLA Ops:
  0.6 2.1 %copy-start = (f32[8]{0:T(128)S(1)}, f32[8]{0:T(128)}, u32[]{:S(2)}) copy-start(f32[8]{0:T(128)} %moduli.1) | copy-start | bytes 100
  3.3 7.4 %collective-permute-start = (f32[16,24,128]{2,1,0:T(8,128)S(1)}, f32[16,24,128]{2,1,0:T(8,128)S(1)}, u32[]{:S(2)}, u32[]{:S(2)}) collective-permute-start(f32[16,24,128]{2,1,0:T(8,128)S(1)} %get-tuple-element.42), channel_id=1, source_target_pairs={{0,1},{1,2},{2,3},{3,4},{4,5},{5,6},{6,7},{7,8},{8,9},{9,10},{10,1... | collective-permute-start | bytes 589832 | tf_op jit(solution)/shard_map/ppermute | solution.py:613
  8.2 7.0 %collective-permute-start.1 = (f32[16,24,128]{2,1,0:T(8,128)S(1)}, f32[16,24,128]{2,1,0:T(8,128)S(1)}, u32[]{:S(2)}, u32[]{:S(2)}) collective-permute-start(f32[16,24,128]{2,1,0:T(8,128)S(1)} %get-tuple-element.43), channel_id=1, source_target_pairs={{1,0},{2,1},{3,2},{4,3},{5,4},{6,5},{7,6},{8,7},{9,8},{10,9},{11,1... | collective-permute-start | bytes 589832 | tf_op jit(solution)/shard_map/ppermute | solution.py:613
  15.8 11.0 %collective-permute-start.2 = (f32[544,128]{1,0:T(8,128)S(1)}, f32[544,128]{1,0:T(8,128)S(1)}, u32[]{:S(2)}, u32[]{:S(2)}) collective-permute-start(f32[544,128]{1,0:T(8,128)S(1)} %get-tuple-element.44), channel_id=1, source_target_pairs={{32,64},{64,32},{96,128},{128,96},{160,192},{192,160},{224,256},{2... | collective-permute-start | bytes 835592 | tf_op jit(solution)/shard_map/ppermute | solution.py:620
  28.1 5.7 %collective-permute-start.3 = (f32[20,8,128]{2,1,0:T(8,128)S(1)}, f32[20,8,128]{2,1,0:T(8,128)S(1)}, u32[]{:S(2)}, u32[]{:S(2)}) collective-permute-start(f32[20,8,128]{2,1,0:T(8,128)S(1)} %get-tuple-element.55), channel_id=1, source_target_pairs={{0,1},{1,2},{2,3},{3,4},{4,5},{5,6},{6,7},{7,8},{8,9},{9,10},{10,1... | collective-permute-start | bytes 245768 | tf_op jit(solution)/shard_map/ppermute | solution.py:613
  32.1 7.7 %collective-permute-start.4 = (f32[20,8,128]{2,1,0:T(8,128)S(1)}, f32[20,8,128]{2,1,0:T(8,128)S(1)}, u32[]{:S(2)}, u32[]{:S(2)}) collective-permute-start(f32[20,8,128]{2,1,0:T(8,128)S(1)} %get-tuple-element.55), channel_id=1, source_target_pairs={{1,0},{2,1},{3,2},{4,3},{5,4},{6,5},{7,6},{8,7},{9,8},{10,9},{11,1... | collective-permute-start | bytes 245768 | tf_op jit(solution)/shard_map/ppermute | solution.py:613
  39.8 8.9 %collective-permute-start.5 = (f32[20,24,128]{2,1,0:T(8,128)S(1)}, f32[20,24,128]{2,1,0:T(8,128)S(1)}, u32[]{:S(2)}, u32[]{:S(2)}) collective-permute-start(f32[20,24,128]{2,1,0:T(8,128)S(1)} %constant_dynamic-update-slice_fusion.own), channel_id=1, source_target_pairs={{32,64},{64,32},{96,128},{128,96},{160,192},{192,160},{224,256},{2... | collective-permute-start | bytes 737288 | tf_op jit(solution)/shard_map/ppermute | solution.py:620

commit v6 on v5

--- a/solution.py
+++ b/solution.py
@@ -122,20 +122,25 @@
     each(planes, body)
 
 
-def left_over(p, b_ref, u_ref, k_ref, co, step, rows=slice(None)):
+def left_over(p, b_ref, u_ref, k_ref, co, step, rows=slice(None), part=None):
     cx_ref, cy_ref, cz_ref, e_ref, _ = co
-    b = [b_ref[c, p] for c in range(3)]
+    more, side = part or (0, slice(None))
+    n = p + more
+    b = [b_ref[c, n, side] for c in range(3)]
     u = [u_ref[c, p] for c in range(3)]
     lo = [u_ref[c, p - 1] for c in range(3)]
     hi = [u_ref[c, p + 1] for c in range(3)]
-    k = k_ref[p, rows]
-    return u, remainder(b, u, lo, hi, k, cx_ref[p], cy_ref[p], cz_ref[p], cz_ref[p - 1], e_ref[p], step)
-
-
-def sweep(planes, b_ref, u_ref, new_ref, k_ref, co, step, rows=slice(None)):
+    k = k_ref[n, rows if part is None else side]
+    cx, cy, cz, cz_lo, e = cx_ref[n, side], cy_ref[n, side], cz_ref[n, side], cz_ref[n - 1, side], e_ref[n, side]
+    return u, remainder(b, u, lo, hi, k, cx, cy, cz, cz_lo, e, step)
+
+
+def sweep(planes, b_ref, u_ref, new_ref, k_ref, co, step, rows=slice(None), part=None):
+    more, side = part or (0, slice(None))
+
     def body(p):
-        u, rest = left_over(p, b_ref, u_ref, k_ref, co, step, rows)
-        w = co[4][p]
+        u, rest = left_over(p, b_ref, u_ref, k_ref, co, step, rows, part)
+        w = co[4][p + more, side]
         for c in range(3):
             new_ref[c, p] = u[c] + w * rest[c]
 
@@ -356,19 +361,11 @@
 def middle_far_kernel(place, cross, *refs):
     refs = refs[8:]
     b1, u1, k1, t1, co_out, first, b2, k2 = refs[:8]
-    b1_out, u1_out, k1_out, t1_out, u2b, packed, co2_out, u2a, tmp = refs[8:]
+    u2b, packed, co2_out, u2a, tmp = refs[8:]
     odd = place[0] & 1
     take(cross, 16 * odd, b1, k1, t1)
     middle_part(odd, False, b1, u1, k1, t1, co_out, first, b2, k2, tmp)
 
-    def keep(p):
-        k1_out[p] = k1[p + 4, 4:20]
-        t1_out[p] = t1[p + 4, 4:20]
-        for c in range(3):
-            b1_out[c, p] = b1[c, p + 4, 4:20]
-            u1_out[c, p] = u1[c, p + 4, 4:20]
-
-    each((0, 16), keep)
     co2 = tuple(co2_out.at[n] for n in range(5))
     fill_coefficients(k2, co2, (1, 11), 0.0625, 4)
     co2[2][0] = (0.5 * 0.0625) * (k2[0] + k2[1])
@@ -428,9 +425,9 @@
         out[q] = jnp.where(q + 1 - (d & 1) > d // 2, to_high, to_low)
 
 
-def upper_kernel(place, received, u2, b2, k2, co2, b1, u1, k1, t1, b0, u0, k0, m0, co0,
+def upper_kernel(place, received, u2, b2, k2, co2, b1, u1, k1, co1, b0, u0, k0, m0, co0,
                  field, residual,
-                 b3, k3, co3, u3a, u3b, u2a, u2b, co1, u1a, u1b, u0a, u0b, tmp):
+                 b3, k3, co3, u3a, u3b, u2a, u2b, u1a, u1b, u0a, u0b, tmp):
     d = place[0]
     lane = lanes_of(24)
     group = lane & 7
@@ -549,22 +546,16 @@
 
     c1 = tuple(co1.at[n] for n in range(5))
 
-    def fill(p):
-        for ref, v in zip(c1, coefficients(k1[p], None, k1[p + 1], 0.25, 2, None, t1[p])):
-            ref[p] = v
-
-    each((0, 15), fill)
-
     def add_middle(q2, s):
         for c in range(3):
             double_rows(u2a[c, q2, 6:14], tmp.at[3 * s + c])
             more = tmp[3 * s + c, 0:16]
             for p in (2 * q2 - 4, 2 * q2 - 3):
-                u1a[c, p] = u1[c, p] + more
+                u1a[c, p] = u1[c, p + 4, 4:20] + more
 
     loop(2, 10, add_middle, 4)
-    sweep((1, 15), b1, u1a, u1b, k1, c1, 2)
-    sweep((2, 14), b1, u1b, u1a, k1, c1, 2)
+    sweep((1, 15), b1, u1a, u1b, k1, c1, 2, part=(4, slice(4, 20)))
+    sweep((2, 14), b1, u1b, u1a, k1, c1, 2, part=(4, slice(4, 20)))
 
     c0 = tuple(co0.at[n] for n in range(5))
     def add_fine(p1, s):
@@ -653,7 +644,7 @@
     wide = jnp.concatenate([y_low, message, y_high], axis=1)
     partner, cross = slab_neighbours(wide, wide)
     full1, full1v, more1 = (24, 24, 128), (3, 24, 24, 128), (25, 24, 128)
-    part1, part1v = (16, 16, 128), (3, 16, 16, 128)
+    part1v = (3, 16, 16, 128)
     full2, full2v = (12, 16, 128), (3, 12, 16, 128)
     kept = (struct(*full1v), struct(*full1v), struct(*more1), struct(*full1), struct(5, *full1), struct(*full1v),
             struct(*full2v), struct(*full2))
@@ -662,12 +653,11 @@
     )
     outs = call(
         middle_far_kernel, "middle_far",
-        kept + (struct(*part1v), struct(*part1v), struct(*part1), struct(*part1), struct(*full2v),
-                struct(COL, 8, 128), struct(5, *full2)),
+        kept + (struct(*full2v), struct(COL, 8, 128), struct(5, *full2)),
         [full2v] + rows, place, cross, *near,
         smem=1, alias={2 + n: n for n in range(len(kept))},
     )
-    b2, k2, b1, u1, k1, t1, u2, packed, co2 = outs[6:]
+    b1, u1, k1, _, co1, _, b2, k2, u2, packed, co2 = outs
     received = lax.all_to_all(packed, "col", 0, 0)
     window = call(window_kernel, "window", struct(SLAB // 2, 48, 128), [(48, 128)], place, received, u2, smem=1)
     groups = [list(range(par, SLAB, 2)) for par in range(2)]
@@ -678,8 +668,8 @@
         upper_kernel, "upper",
         (struct(3, 16, 16, 128), struct(3, 16, 16, 128)),
         [full3v, full3, (5,) + full3, full3v, full3v, full2v, full2v,
-         (5,) + part1, part1v, part1v, full0v, full0v, (16, 48, 128)],
-        place, received, u2, b2, k2, co2, b1, u1, k1, t1, b0, u0, k0, m0, co0, smem=1,
+         part1v, part1v, full0v, full0v, (16, 48, 128)],
+        place, received, u2, b2, k2, co2, b1, u1, k1, co1, b0, u0, k0, m0, co0, smem=1,
     )
 
 

time: 101 us -> 101 us (level)
  no operation moved by 1% of the time
where the time goes in v6:
time: 101 us; the launch traced here: 100 us
  blocking collectives  44.9 us (44%)
  starting transfers between devices  21.3 us (21%)
  Pallas kernels  19.3 us (19%)
  waiting for transfers between devices  12.1 us (12%)
  other arithmetic  2.11 us (2%)
    all_to_all x1, blocking collectives, on_device(): received = lax.all_to_all(packed, 'col', 0, 0)  19.4 us
    pallas_call x8, Pallas kernels, call(): pl.pallas_call(kernel, name=name, out_shape=outs, in_specs=specs + [vmem]...  19.3 us
    all_to_all x1, blocking collectives, on_device(): received = lax.all_to_all(window, 'slab', 0, 0, axis_index_groups=groups)  14.8 us
    ppermute x4, waiting for transfers between devices, shift(): return lax.ppermute(block, axis, pairs)  12.1 us
    ppermute x4, starting transfers between devices, shift(): return lax.ppermute(block, axis, pairs)  11.5 us
    ppermute x2, starting transfers between devices, slab_neighbours(): cross = lax.ppermute(to_cross, 'slab', pairs)  9.84 us
    all_gather x1, blocking collectives, on_device(): lax.all_gather(received, 'slab', axis_index_groups=[[i, i + 1] for i in r...  6.34 us
    all_gather x2, blocking collectives, slab_neighbours(): return (lax.all_gather(to_partner, 'slab', axis_index_groups=groups), cross)  4.36 us
  transfers between devices with their start and end apart: 6, of which 4 were waited for; matrix products, arithmetic and copies ran while one was open for 0% of the time, Pallas kernels for 6%

profile of v6, /device:TPU:1, one launch (start us, length us, event | category | flops | bytes accessed | tf_op | source)
XLA Modules:
  0.0 100.4 jit_solution(503272619819263437)
XLA Ops:
  0.6 0.0 copy-start
  0.6 1.0 convert_bitcast_fusion
  1.6 1.0 %pad_maximum_fusion.raw.load = f32[5,16,16,128]{3,2,1,0:T(8,128)S(1)} fusion(f32[1,16,16,128]{3,2,1,0:T(8,128)S(1)} %get-tuple-element.78, f32[1,16,16,128]{3,2,1,0:T(8,128)S(1)} %get-tuple-element.79, f32[3,16,16,128]{3,2,1,0:T(8,128)} %param.4), kind=kLoop, calls=%fused_computation | loop fusion | flops 327680 | bytes 1310720 | tf_op jit(solution)/shard_map/concatenate | solution.py:619
  2.7 0.0 copy-done
  2.7 0.6 prep.1
  3.3 4.8 %collective-permute-start = (f32[16,24,128]{2,1,0:T(8,128)S(1)}, f32[16,24,128]{2,1,0:T(8,128)S(1)}, u32[]{:S(2)}, u32[]{:S(2)}) collective-permute-start(f32[16,24,128]{2,1,0:T(8,128)S(1)} %get-tuple-element.42), channel_id=1, source_target_pairs={{0,1},{1,2},{2,3},{3,4},{4,5},{5,6},{6,7},{7,8},{8,9},{9,10},{10,1... | collective-permute-start | bytes 589832 | tf_op jit(solution)/shard_map/ppermute | solution.py:604
  8.2 1.3 %collective-permute-start.1 = (f32[16,24,128]{2,1,0:T(8,128)S(1)}, f32[16,24,128]{2,1,0:T(8,128)S(1)}, u32[]{:S(2)}, u32[]{:S(2)}) collective-permute-start(f32[16,24,128]{2,1,0:T(8,128)S(1)} %get-tuple-element.43), channel_id=1, source_target_pairs={{1,0},{2,1},{3,2},{4,3},{5,4},{6,5},{7,6},{8,7},{9,8},{10,9},{11,1... | collective-permute-start | bytes 589832 | tf_op jit(solution)/shard_map/ppermute | solution.py:604
  9.5 0.1 pad_add_fusion.place
  9.6 1.2 %collective-permute-done.from_low.y_low = f32[16,24,128]{2,1,0:T(8,128)S(1)} collective-permute-done((f32[16,24,128]{2,1,0:T(8,128)S(1)}, f32[16,24,128]{2,1,0:T(8,128)S(1)}, u32[]{:S(2)}, u32[]{:S(2)}) %collective-permute-start) | collective-permute-done | bytes 196640 | tf_op jit(solution)/shard_map/ppermute | solution.py:604
  10.8 4.5 %collective-permute-done.1.from_high.y_high = f32[16,24,128]{2,1,0:T(8,128)S(1)} collective-permute-done((f32[16,24,128]{2,1,0:T(8,128)S(1)}, f32[16,24,128]{2,1,0:T(8,128)S(1)}, u32[]{:S(2)}, u32[]{:S(2)}) %collective-permute-start.1) | collective-permute-done | bytes 196640 | tf_op jit(solution)/shard_map/ppermute | solution.py:604
  15.2 0.6 planes.1
  15.8 5.9 %collective-permute-start.2 = (f32[544,128]{1,0:T(8,128)S(1)}, f32[544,128]{1,0:T(8,128)S(1)}, u32[]{:S(2)}, u32[]{:S(2)}) collective-permute-start(f32[544,128]{1,0:T(8,128)S(1)} %get-tuple-element.44), channel_id=1, source_target_pairs={{32,64},{64,32},{96,128},{128,96},{160,192},{192,160},{224,256},{2... | collective-permute-start | bytes 835592 | tf_op jit(solution)/shard_map/ppermute | solution.py:611
  21.7 2.2 %all-gather = f32[1088,128]{1,0:T(8,128)S(1)} all-gather(f32[544,128]{1,0:T(8,128)S(1)} %get-tuple-element.45), channel_id=2, replica_groups={{0,32},{64,96},{128,160},{192,224},{256,288},{320,352},{384,416},{448,4..., dimensions={0}, use_global_device_ids=true | all-gather | bytes 835584 | tf_op jit(solution)/shard_map/all_gather | solution.py:613
  23.9 2.9 %fine_near.1 = (f32[3,26,24,128]{3,2,1,0:T(8,128)S(1)}, f32[3,26,24,128]{3,2,1,0:T(8,128)S(1)}, f32[26,32,128]{2,1,0:T(8,128)S(1)}, f32[26,24,128]{2,1,0:T(8,128...) custom-call(s32[2]{0:T(128)S(1)} %pad_add_fusion.place, ...), custom_call_target="tpu_custom_call" | custom-call | flops 8000000 | bytes 8000000 | tf_op jit(solution)/shard_map/fine_near/pallas_call | solution.py:589
  26.8 0.0 collective-permute-done.2.cross
  26.8 1.2 %fine_far.1 = (f32[3,26,24,128]{3,2,1,0:T(8,128)S(1)}, f32[3,26,24,128]{3,2,1,0:T(8,128)S(1)}, f32[26,32,128]{2,1,0:T(8,128)S(1)}, f32[26,24,128]{2,1,0:T(8,128)...) custom-call(s32[2]{0:T(128)S(1)} %pad_add_fusion.place, ...), custom_call_target="tpu_custom_call", output_to_operand_aliasing={{0}: (2, {}), {1}: (3, {}), {2}: (4, {}), {3}: (5, {}), {4}... | custom-call | tf_op jit(solution)/shard_map/fine_far/pallas_call | solution.py:589
  28.1 4.0 %collective-permute-start.3 = (f32[20,8,128]{2,1,0:T(8,128)S(1)}, f32[20,8,128]{2,1,0:T(8,128)S(1)}, u32[]{:S(2)}, u32[]{:S(2)}) collective-permute-start(f32[20,8,128]{2,1,0:T(8,128)S(1)} %get-tuple-element.55), channel_id=1, source_target_pairs={{0,1},{1,2},{2,3},{3,4},{4,5},{5,6},{6,7},{7,8},{8,9},{9,10},{10,1... | collective-permute-start | bytes 245768 | tf_op jit(solution)/shard_map/ppermute | solution.py:604
  32.1 1.3 %collective-permute-start.4 = (f32[20,8,128]{2,1,0:T(8,128)S(1)}, f32[20,8,128]{2,1,0:T(8,128)S(1)}, u32[]{:S(2)}, u32[]{:S(2)}) collective-permute-start(f32[20,8,128]{2,1,0:T(8,128)S(1)} %get-tuple-element.55), channel_id=1, source_target_pairs={{1,0},{2,1},{3,2},{4,3},{5,4},{6,5},{7,6},{8,7},{9,8},{10,9},{11,1... | collective-permute-start | bytes 245768 | tf_op jit(solution)/shard_map/ppermute | solution.py:604
  33.4 0.5 collective-permute-done.3
  33.9 5.9 %collective-permute-done.4 = f32[20,8,128]{2,1,0:T(8,128)S(1)} collective-permute-done((f32[20,8,128]{2,1,0:T(8,128)S(1)}, f32[20,8,128]{2,1,0:T(8,128)S(1)}, u32[]{:S(2)}, u32[]{:S(2)}) %collective-permute-start.4) | collective-permute-done | bytes 81952 | tf_op jit(solution)/shard_map/ppermute | solution.py:604
  39.9 4.0 %collective-permute-start.5 = (f32[20,24,128]{2,1,0:T(8,128)S(1)}, f32[20,24,128]{2,1,0:T(8,128)S(1)}, u32[]{:S(2)}, u32[]{:S(2)}) collective-permute-start(f32[20,24,128]{2,1,0:T(8,128)S(1)} %constant_dynamic-update-slice_fusion.own), channel_id=1, source_target_pairs={{32,64},{64,32},{96,128},{128,96},{160,192},{192,160},{224,256},{2... | collective-permute-start | bytes 737288 | tf_op jit(solution)/shard_map/ppermute | solution.py:611
  43.8 2.2 %all-gather.1 = f32[40,24,128]{2,1,0:T(8,128)S(1)} all-gather(f32[20,24,128]{2,1,0:T(8,128)S(1)} %constant_dynamic-update-slice_fusion.own), channel_id=3, replica_groups={{0,32},{64,96},{128,160},{192,224},{256,288},{320,352},{384,416},{448,4..., dimensions={0}, use_global_device_ids=true | all-gather | bytes 737280 | tf_op jit(solution)/shard_map/all_gather | solution.py:613
  46.0 2.7 %middle_near.1 = (f32[3,24,24,128]{3,2,1,0:T(8,128)S(1)}, f32[3,24,24,128]{3,2,1,0:T(8,128)S(1)}, f32[25,24,128]{2,1,0:T(8,128)S(1)}, f32[24,24,128]{2,1,0:T(8,1...) custom-call(s32[2]{0:T(128)S(1)} %pad_add_fusion.place, ...), custom_call_target="tpu_custom_call" | custom-call | flops 8000000 | bytes 8000000 | tf_op jit(solution)/shard_map/middle_near/pallas_call | solution.py:589
  48.6 0.0 collective-permute-done.5.cross
  48.7 2.5 %middle_far.1 = (f32[3,24,24,128]{3,2,1,0:T(8,128)S(1)}, f32[3,24,24,128]{3,2,1,0:T(8,128)S(1)}, f32[25,24,128]{2,1,0:T(8,128)S(1)}, f32[24,24,128]{2,1,0:T(8,12...) custom-call(s32[2]{0:T(128)S(1)} %pad_add_fusion.place, ...), custom_call_target="tpu_custom_call", output_to_operand_aliasing={{0}: (2, {}), {1}: (3, {}), {2}: (4, {}), {3}: (5, {}), {4}... | custom-call | tf_op jit(solution)/shard_map/middle_far/pallas_call | solution.py:589
  51.1 19.4 %all_to_all.10.received = f32[32,8,128]{2,1,0:T(8,128)S(1)} all-to-all(f32[32,8,128]{2,1,0:T(8,128)S(1)} %get-tuple-element.64), channel_id=1, replica_groups=mesh['slab'=16,'col'=32] {'col'}, dimensions={0} | all-to-all | bytes 262144 | tf_op jit(solution)/shard_map/all_to_all | solution.py:661
  70.5 0.6 window.1
  71.1 14.8 %all_to_all.11 = f32[8,48,128]{2,1,0:T(8,128)S(1)} all-to-all(f32[8,48,128]{2,1,0:T(8,128)S(1)} %window.1), channel_id=1, replica_groups={{0,64,128,192,256,320,384,448},{32,96,160,224,288,352,416,480},{1,65,12..., dimensions={0} | all-to-all | bytes 393216 | tf_op jit(solution)/shard_map/all_to_all | solution.py:664
  85.9 6.3 %all-gather.2 = f32[16,48,128]{2,1,0:T(8,128)S(1)} all-gather(f32[8,48,128]{2,1,0:T(8,128)S(1)} %all_to_all.11), channel_id=4, replica_groups={{0,32},{64,96},{128,160},{192,224},{256,288},{320,352},{384,416},{448,4..., dimensions={0}, use_global_device_ids=true | all-gather | bytes 589824 | tf_op jit(solution)/shard_map/all_gather | solution.py:665
  92.2 8.2 %upper.1 = (f32[3,16,16,128]{3,2,1,0:T(8,128)}, f32[3,16,16,128]{3,2,1,0:T(8,128)}) custom-call(s32[2]{0:T(128)S(1)} %pad_add_fusion.place, f32[2,8,48,128]{3,2,1,0:T(8,128)S(1)} %bitcast.11, f32[3,12,16,128]{3,2,1,0:T(8,128)S(1)} %get-tuple-element.65.u2, f32[3,12,16,128]{3,2,1,0:T(8,128)S(1)} %get-tuple-element.66.b2, ...), custom_call_target="tpu_custom_call" | custom-call | tf_op jit(solution)/shard_map/upper/pallas_call | solution.py:589
  (3 shorter events, 0.0 us)
Async XLA Ops:
  0.6 2.1 %copy-start = (f32[8]{0:T(128)S(1)}, f32[8]{0:T(128)}, u32[]{:S(2)}) copy-start(f32[8]{0:T(128)} %moduli.1) | copy-start | bytes 100
  3.3 7.4 %collective-permute-start = (f32[16,24,128]{2,1,0:T(8,128)S(1)}, f32[16,24,128]{2,1,0:T(8,128)S(1)}, u32[]{:S(2)}, u32[]{:S(2)}) collective-permute-start(f32[16,24,128]{2,1,0:T(8,128)S(1)} %get-tuple-element.42), channel_id=1, source_target_pairs={{0,1},{1,2},{2,3},{3,4},{4,5},{5,6},{6,7},{7,8},{8,9},{9,10},{10,1... | collective-permute-start | bytes 589832 | tf_op jit(solution)/shard_map/ppermute | solution.py:604
  8.2 7.0 %collective-permute-start.1 = (f32[16,24,128]{2,1,0:T(8,128)S(1)}, f32[16,24,128]{2,1,0:T(8,128)S(1)}, u32[]{:S(2)}, u32[]{:S(2)}) collective-permute-start(f32[16,24,128]{2,1,0:T(8,128)S(1)} %get-tuple-element.43), channel_id=1, source_target_pairs={{1,0},{2,1},{3,2},{4,3},{5,4},{6,5},{7,6},{8,7},{9,8},{10,9},{11,1... | collective-permute-start | bytes 589832 | tf_op jit(solution)/shard_map/ppermute | solution.py:604
  15.8 11.0 %collective-permute-start.2 = (f32[544,128]{1,0:T(8,128)S(1)}, f32[544,128]{1,0:T(8,128)S(1)}, u32[]{:S(2)}, u32[]{:S(2)}) collective-permute-start(f32[544,128]{1,0:T(8,128)S(1)} %get-tuple-element.44), channel_id=1, source_target_pairs={{32,64},{64,32},{96,128},{128,96},{160,192},{192,160},{224,256},{2... | collective-permute-start | bytes 835592 | tf_op jit(solution)/shard_map/ppermute | solution.py:611
  28.1 5.8 %collective-permute-start.3 = (f32[20,8,128]{2,1,0:T(8,128)S(1)}, f32[20,8,128]{2,1,0:T(8,128)S(1)}, u32[]{:S(2)}, u32[]{:S(2)}) collective-permute-start(f32[20,8,128]{2,1,0:T(8,128)S(1)} %get-tuple-element.55), channel_id=1, source_target_pairs={{0,1},{1,2},{2,3},{3,4},{4,5},{5,6},{6,7},{7,8},{8,9},{9,10},{10,1... | collective-permute-start | bytes 245768 | tf_op jit(solution)/shard_map/ppermute | solution.py:604
  32.1 7.7 %collective-permute-start.4 = (f32[20,8,128]{2,1,0:T(8,128)S(1)}, f32[20,8,128]{2,1,0:T(8,128)S(1)}, u32[]{:S(2)}, u32[]{:S(2)}) collective-permute-start(f32[20,8,128]{2,1,0:T(8,128)S(1)} %get-tuple-element.55), channel_id=1, source_target_pairs={{1,0},{2,1},{3,2},{4,3},{5,4},{6,5},{7,6},{8,7},{9,8},{10,9},{11,1... | collective-permute-start | bytes 245768 | tf_op jit(solution)/shard_map/ppermute | solution.py:604
  39.9 8.8 %collective-permute-start.5 = (f32[20,24,128]{2,1,0:T(8,128)S(1)}, f32[20,24,128]{2,1,0:T(8,128)S(1)}, u32[]{:S(2)}, u32[]{:S(2)}) collective-permute-start(f32[20,24,128]{2,1,0:T(8,128)S(1)} %constant_dynamic-update-slice_fusion.own), channel_id=1, source_target_pairs={{32,64},{64,32},{96,128},{128,96},{160,192},{192,160},{224,256},{2... | collective-permute-start | bytes 737288 | tf_op jit(solution)/shard_map/ppermute | solution.py:611
